TPU v7x, 32 devices: a whole 2x2x4 slice. The times are simulated.
32 devices in a mesh: row: 8 (over y, x, core), col: 4 (over z).
Axes of the slice: x: 2, y: 2, z: 4, core: 2. Of those that a mesh axis runs over, the one named last changes fastest.
Arguments:
- images: bfloat16 [4, 4, 16, 3072], P(None, 'col', 'row'), may hold values from -6 to 6
- cotangent: bfloat16 [16, 16, 4, 4, 16], P('row', None, None, 'col'), may hold values from -192 to 192
Outputs:
- kernel: float32 [16, 16, 4, 4, 16], P('row', None, None, 'col')
- image_grads: float32 [4, 4, 16, 3072], P(None, 'col', 'row')
All inputs are finite; a program needn't handle non-finite values.
Results may differ from a plain program's by a relative error of at most 0.0003.
Values may be sent and summed in bfloat16 or wider, within the bound.
No kernel may reach another device: no remote copies, remote signals or barrier semaphores. Data moves between devices by JAX's collectives and lax.ppermute only.
A program may use at most 64 MiB of HBM per device.

v0:
```python
import math

import jax
import jax.numpy as jnp
import numpy as np
from jax import lax
from jax.sharding import PartitionSpec as P

CHAN = 3
LAYERS = 3


WEIGHT_VAR = 2.0
BIAS_VAR = 0.1


def shifted(field, offset):
    total = field.shape[-1]
    widths = [(0, 0)] * (field.ndim - 1) + [(max(-offset, 0), max(offset, 0))]
    padded = jnp.pad(field, widths)
    begin = max(offset, 0)
    return padded[..., begin : begin + total]


def spatial_blur(field, grid_side):
    column = jnp.arange(grid_side * grid_side) % grid_side
    left_ok = (column > 0).astype(jnp.float32)
    right_ok = (column < grid_side - 1).astype(jnp.float32)
    across = field + shifted(field, -1) * left_ok + shifted(field, 1) * right_ok
    summed = across + shifted(across, -grid_side) + shifted(across, grid_side)
    return WEIGHT_VAR * summed / 9.0 + BIAS_VAR


def relu_expect(cross_cov, left_var, right_var):
    fixed_cross = lax.stop_gradient(cross_cov)
    fixed_left = lax.stop_gradient(left_var)
    fixed_right = lax.stop_gradient(right_var)
    root_prod = jnp.sqrt(fixed_left * fixed_right)
    cosine = jnp.clip(fixed_cross / root_prod, -1.0, 1.0)
    angle_val = jnp.arccos(cosine)
    sine_val = jnp.sqrt(jnp.maximum(1.0 - cosine * cosine, 0.0))
    value = root_prod * (sine_val + (jnp.pi - angle_val) * cosine) / (2.0 * jnp.pi)
    slope_cross = (jnp.pi - angle_val) / (2.0 * jnp.pi)
    slope_left = jnp.sqrt(fixed_right / fixed_left) * sine_val / (4.0 * jnp.pi)
    slope_right = jnp.sqrt(fixed_left / fixed_right) * sine_val / (4.0 * jnp.pi)
    linear = slope_cross * cross_cov + slope_left * left_var + slope_right * right_var
    return lax.stop_gradient(value - linear) + linear


def tile_kernel(left_imgs, right_imgs):
    tile_rows = left_imgs.shape[0]
    positions = left_imgs.shape[1] // CHAN
    grid_side = math.isqrt(positions)
    left_px = left_imgs.reshape(tile_rows, CHAN, positions)
    right_px = right_imgs.reshape(right_imgs.shape[0], CHAN, positions)
    cross_cov = (
        jnp.einsum("acp,bcp->abp", left_px, right_px, precision=lax.Precision.HIGHEST) / CHAN
    )
    left_var = jnp.sum(left_px * left_px, axis=1) / CHAN
    right_var = jnp.sum(right_px * right_px, axis=1) / CHAN
    for layer_idx in range(LAYERS):
        cross_cov = spatial_blur(cross_cov, grid_side)
        left_var = spatial_blur(left_var, grid_side)
        right_var = spatial_blur(right_var, grid_side)
        cross_cov = relu_expect(cross_cov, left_var[:, None, :], right_var[None, :, :])
        left_var = 0.5 * left_var
        right_var = 0.5 * right_var
    return WEIGHT_VAR * jnp.mean(cross_cov, axis=-1) + BIAS_VAR


def tile_terms(left_blk, right_blk, cot_blk):
    left_full = left_blk.astype(jnp.float32)
    right_full = right_blk.astype(jnp.float32)
    value, pullback = jax.vjp(tile_kernel, left_full, right_full)
    grad_left, grad_right = pullback(cot_blk.astype(jnp.float32))
    return (value, grad_left, grad_right)


def slot_table(row_pos, col_pos, col_count, per_row):
    slot_ids = jnp.arange(2 * per_row, dtype=jnp.int32)
    upper = (2 * row_pos + slot_ids // per_row <= slot_ids % per_row * col_count + col_pos).astype(
        jnp.int32
    )
    places = jnp.cumsum(upper) - 1
    wanted = jnp.arange(2 * per_row, dtype=jnp.int32)
    hits = (upper[None, :] == 1) & (places[None, :] == wanted[:, None])
    listed = jnp.sum(jnp.where(hits, slot_ids[None, :], 0), axis=1)
    return (listed, jnp.sum(upper))


def load_table(row_count, col_count, per_row):
    row_ids = np.arange(row_count)[:, None, None, None]
    col_ids = np.arange(col_count)[None, :, None, None]
    halves = np.arange(2)[None, None, :, None]
    block_ids = np.arange(per_row)[None, None, None, :]
    return (2 * row_ids + halves <= block_ids * col_count + col_ids).sum(axis=(2, 3))


def body(images, cotangent):
    row_count = lax.axis_size("row")
    col_count = lax.axis_size("col")
    row_idx = lax.axis_index("row")
    col_idx = lax.axis_index("col")
    per_row = images.shape[0]
    feat_len = images.shape[3]
    tile_rows = images.shape[2] * row_count
    column_imgs = lax.all_gather(images, "row", axis=2, tiled=True).reshape(
        per_row, tile_rows, feat_len
    )
    own_block = 2 * row_idx // col_count
    chosen = lax.dynamic_index_in_dim(column_imgs, own_block, 0, keepdims=False)
    fetched = lax.all_gather(chosen[None], "col", axis=0, tiled=True)
    row_imgs = lax.dynamic_slice_in_dim(fetched, 2 * row_idx % col_count, 2, 0)
    cot_local = cotangent.reshape(2, tile_rows, per_row, tile_rows)
    listed, own_count = slot_table(row_idx, col_idx, col_count, per_row)
    counts = load_table(row_count, col_count, per_row)
    most_load = int(counts.max())

    def own_step(position, state):
        row_grad, col_grad, kernel_out = state
        slot = listed[position]
        live = (position < own_count).astype(jnp.float32)
        half_idx = slot // per_row
        block = slot % per_row
        left_blk = lax.dynamic_index_in_dim(row_imgs, half_idx, 0, keepdims=False)
        right_blk = lax.dynamic_index_in_dim(column_imgs, block, 0, keepdims=False)
        cot_blk = lax.dynamic_slice(
            cot_local, (half_idx, 0, block, 0), (1, tile_rows, 1, tile_rows)
        ).reshape(tile_rows, tile_rows)
        value, grad_left, grad_right = tile_terms(left_blk, right_blk, cot_blk)
        row_grad = row_grad.at[half_idx].add(grad_left * live)
        col_grad = col_grad.at[block].add(grad_right * live)
        kernel_out = kernel_out.at[half_idx, :, block, :].add(value * live)
        return (row_grad, col_grad, kernel_out)

    start = (
        jnp.zeros((2, tile_rows, feat_len), jnp.float32),
        jnp.zeros((per_row, tile_rows, feat_len), jnp.float32),
        jnp.zeros((2, tile_rows, per_row, tile_rows), jnp.float32),
    )
    row_grad, col_grad, kernel_out = lax.fori_loop(0, most_load, own_step, start)
    slotted = jnp.zeros((col_count, tile_rows, feat_len), jnp.float32)
    for half_idx in range(2):
        slotted = slotted.at[(2 * row_idx + half_idx) % col_count].set(row_grad[half_idx])
    received = lax.psum_scatter(slotted, "col", scatter_dimension=0, tiled=True)
    col_grad = col_grad.at[own_block].add(received[0])
    image_part = lax.psum_scatter(col_grad, "row", scatter_dimension=1, tiled=True)
    image_grads = image_part.reshape(per_row, 1, tile_rows // row_count, feat_len)
    kernel = kernel_out.reshape(2, tile_rows, per_row, 1, tile_rows)
    return (kernel, image_grads)


def solution(mesh):
    return jax.shard_map(
        body,
        mesh=mesh,
        in_specs=(P(None, "col", "row", None), P("row", None, None, "col", None)),
        out_specs=(P("row", None, None, "col", None), P(None, "col", "row", None)),
        check_vma=False,
    )
```

profile of v0, /device:TPU:0, one launch (start us, length us, event | category | flops | bytes accessed | tf_op | source)
XLA Modules:
  0.0 828.9 jit_solution(3217434722072947463)
XLA Ops:
  8.7 11.0 %all_gather.6 = bf16[4,1,16,3072]{3,0,1,2:T(4,128)(2,1)S(1)} all-gather(bf16[4,1,2,3072]{3,0,1,2:T(4,128)(2,1)S(1)} %copy.83), channel_id=1, replica_groups=mesh['row'=8,'col'=4] {'row'}, dimensions={2}, use_global_device_ids=true | all-gather | bytes 442368 | tf_op jit(solution)/shard_map/all_gather | solution.py:107
  20.0 14.9 %all-gather = bf16[4,1,16,3072]{3,2,1,0:T(8,128)(2,1)S(1)} all-gather(bf16[1,1,16,3072]{3,2,1,0:T(8,128)(2,1)S(1)} %copy.84), channel_id=2, replica_groups=mesh['row'=8,'col'=4] {'col'}, dimensions={0}, use_global_device_ids=true | all-gather | bytes 491520 | tf_op jit(solution)/shard_map/all_gather | solution.py:112
  39.7 689.7 %while.28 = (s32[]{:T(128)}, f32[2,16,3072]{2,1,0:T(8,128)}, f32[4,16,3072]{2,1,0:T(8,128)}, f32[2,16,4,16]{3,2,1,0:T(4,128)}, s32[8]{0:T(128)}, /*index=5*/bf16...) while((s32[]{:T(128)}, f32[2,16,3072]{2,1,0:T(8,128)}, ...), condition=%wide.region_16.17_spmd, body=%wide.region_3.16_spmd.sunk | while | flops 71649104 | bytes 83293752 | solution.py:141
  89.1 6.3 copy.123
  95.4 10.0 %fusion.246 = f32[1024,16,3]{1,2,0:T(4,128)} fusion(f32[1024,16,16]{2,1,0:T(8,128)} %copy.123, bf16[16,3,1024]{0,1,2:T(4,128)(2,1)S(1)} %copy.121), kind=kOutput, calls=%fused_computation.350.clone.1 | convolution fusion | flops 9437184 | bytes 1343488 | tf_op jit(solution)/shard_map/while/body/eval_jaxpr/transpose(jvp(acp,bcp->abp))/dot_general | solution.py:57
  109.5 6.5 fusion.239
  175.2 6.3 copy.123
  181.5 10.0 %fusion.246 = f32[1024,16,3]{1,2,0:T(4,128)} fusion(f32[1024,16,16]{2,1,0:T(8,128)} %copy.123, bf16[16,3,1024]{0,1,2:T(4,128)(2,1)S(1)} %copy.121), kind=kOutput, calls=%fused_computation.350.clone.1 | convolution fusion | flops 9437184 | bytes 1343488 | tf_op jit(solution)/shard_map/while/body/eval_jaxpr/transpose(jvp(acp,bcp->abp))/dot_general | solution.py:57
  195.5 6.5 fusion.239
  261.0 6.3 copy.123
  267.3 10.0 %fusion.246 = f32[1024,16,3]{1,2,0:T(4,128)} fusion(f32[1024,16,16]{2,1,0:T(8,128)} %copy.123, bf16[16,3,1024]{0,1,2:T(4,128)(2,1)S(1)} %copy.121), kind=kOutput, calls=%fused_computation.350.clone.1 | convolution fusion | flops 9437184 | bytes 1343488 | tf_op jit(solution)/shard_map/while/body/eval_jaxpr/transpose(jvp(acp,bcp->abp))/dot_general | solution.py:57
  281.4 6.5 fusion.239
  353.4 10.0 %fusion.246 = f32[1024,16,3]{1,2,0:T(4,128)} fusion(f32[1024,16,16]{2,1,0:T(8,128)} %copy.123, bf16[16,3,1024]{0,1,2:T(4,128)(2,1)S(1)} %copy.121), kind=kOutput, calls=%fused_computation.350.clone.1 | convolution fusion | flops 9437184 | bytes 1343488 | tf_op jit(solution)/shard_map/while/body/eval_jaxpr/transpose(jvp(acp,bcp->abp))/dot_general | solution.py:57
  367.5 6.5 fusion.239
  439.3 10.0 %fusion.246 = f32[1024,16,3]{1,2,0:T(4,128)} fusion(f32[1024,16,16]{2,1,0:T(8,128)} %copy.123, bf16[16,3,1024]{0,1,2:T(4,128)(2,1)S(1)} %copy.121), kind=kOutput, calls=%fused_computation.350.clone.1 | convolution fusion | flops 9437184 | bytes 1343488 | tf_op jit(solution)/shard_map/while/body/eval_jaxpr/transpose(jvp(acp,bcp->abp))/dot_general | solution.py:57
  453.3 6.5 fusion.239
  525.3 10.0 %fusion.246 = f32[1024,16,3]{1,2,0:T(4,128)} fusion(f32[1024,16,16]{2,1,0:T(8,128)} %copy.123, bf16[16,3,1024]{0,1,2:T(4,128)(2,1)S(1)} %copy.121), kind=kOutput, calls=%fused_computation.350.clone.1 | convolution fusion | flops 9437184 | bytes 1343488 | tf_op jit(solution)/shard_map/while/body/eval_jaxpr/transpose(jvp(acp,bcp->abp))/dot_general | solution.py:57
  539.4 6.5 fusion.239
  611.2 10.0 %fusion.246 = f32[1024,16,3]{1,2,0:T(4,128)} fusion(f32[1024,16,16]{2,1,0:T(8,128)} %copy.123, bf16[16,3,1024]{0,1,2:T(4,128)(2,1)S(1)} %copy.121), kind=kOutput, calls=%fused_computation.350.clone.1 | convolution fusion | flops 9437184 | bytes 1343488 | tf_op jit(solution)/shard_map/while/body/eval_jaxpr/transpose(jvp(acp,bcp->abp))/dot_general | solution.py:57
  625.2 6.5 fusion.239
  697.2 10.0 %fusion.246 = f32[1024,16,3]{1,2,0:T(4,128)} fusion(f32[1024,16,16]{2,1,0:T(8,128)} %copy.123, bf16[16,3,1024]{0,1,2:T(4,128)(2,1)S(1)} %copy.121), kind=kOutput, calls=%fused_computation.350.clone.1 | convolution fusion | flops 9437184 | bytes 1343488 | tf_op jit(solution)/shard_map/while/body/eval_jaxpr/transpose(jvp(acp,bcp->abp))/dot_general | solution.py:57
  711.3 6.5 fusion.239
  734.8 23.7 %reduce-scatter.2.cloned.1.call-done = f32[1,16,3072]{2,1,0:T(8,128)} async-done(((f32[4,16,3072]{2,1,0:T(8,128)}), f32[1,16,3072]{2,1,0:T(8,128)}) %reduce-scatter.2.cloned.1.call-update) | async-done | bytes 196624 | tf_op jit(solution)/shard_map/reduce_scatter | solution.py:145
  766.5 53.7 %all-reduce.75.cloned.1.call-done = f32[4,16,3072]{2,0,1:T(4,128)} async-done(((f32[4,16,3072]{2,0,1:T(4,128)}), f32[4,16,3072]{2,0,1:T(4,128)}) %all-reduce.75.cloned.1.call-update) | async-done | bytes 786448
  (927 shorter events, 525.5 us)
Async XLA Ops:
  7.2 751.3 %reduce-scatter.2.cloned.1.call-start = ((), (), s32[]{:S(2)}) async-start(), calls=%async_computation.1 | async-start | bytes 983040 | tf_op jit(solution)/shard_map/reduce_scatter | solution.py:145
  8.7 27.3 %copy-start.13 = (bf16[2,16,4,1,16]{4,2,3,1,0:T(4,128)(2,1)S(1)}, bf16[2,16,4,1,16]{4,2,3,1,0:T(4,128)(2,1)}, u32[]{:S(2)}) copy-start(bf16[2,16,4,1,16]{4,2,3,1,0:T(4,128)(2,1)} %param.17) | copy-start | bytes 12292
  39.7 28.7 %copy-start.11 = (bf16[2,16,4,16]{3,1,2,0:T(8,128)(2,1)}, bf16[2,16,4,16]{3,1,2,0:T(8,128)(2,1)S(1)}, u32[]{:S(2)}) copy-start(bf16[2,16,4,16]{3,1,2,0:T(8,128)(2,1)S(1)} %get-tuple-element.786) | copy-start | bytes 12292 | tf_op jit(solution)/shard_map/while
  116.7 6.0 copy-start.15
  116.7 8.8 %copy-start.12 = (bf16[2,16,4,16]{3,1,2,0:T(8,128)(2,1)S(1)}, bf16[2,16,4,16]{3,1,2,0:T(8,128)(2,1)}, u32[]{:S(2)}) copy-start(bf16[2,16,4,16]{3,1,2,0:T(8,128)(2,1)} %copy-done.11) | copy-start | bytes 12292 | tf_op jit(solution)/shard_map/while
  125.9 28.7 %copy-start.11 = (bf16[2,16,4,16]{3,1,2,0:T(8,128)(2,1)}, bf16[2,16,4,16]{3,1,2,0:T(8,128)(2,1)S(1)}, u32[]{:S(2)}) copy-start(bf16[2,16,4,16]{3,1,2,0:T(8,128)(2,1)S(1)} %get-tuple-element.786) | copy-start | bytes 12292 | tf_op jit(solution)/shard_map/while
  202.8 8.8 %copy-start.12 = (bf16[2,16,4,16]{3,1,2,0:T(8,128)(2,1)S(1)}, bf16[2,16,4,16]{3,1,2,0:T(8,128)(2,1)}, u32[]{:S(2)}) copy-start(bf16[2,16,4,16]{3,1,2,0:T(8,128)(2,1)} %copy-done.11) | copy-start | bytes 12292 | tf_op jit(solution)/shard_map/while
  211.8 28.7 %copy-start.11 = (bf16[2,16,4,16]{3,1,2,0:T(8,128)(2,1)}, bf16[2,16,4,16]{3,1,2,0:T(8,128)(2,1)S(1)}, u32[]{:S(2)}) copy-start(bf16[2,16,4,16]{3,1,2,0:T(8,128)(2,1)S(1)} %get-tuple-element.786) | copy-start | bytes 12292 | tf_op jit(solution)/shard_map/while
  288.6 8.8 %copy-start.12 = (bf16[2,16,4,16]{3,1,2,0:T(8,128)(2,1)S(1)}, bf16[2,16,4,16]{3,1,2,0:T(8,128)(2,1)}, u32[]{:S(2)}) copy-start(bf16[2,16,4,16]{3,1,2,0:T(8,128)(2,1)} %copy-done.11) | copy-start | bytes 12292 | tf_op jit(solution)/shard_map/while
  297.9 28.7 %copy-start.11 = (bf16[2,16,4,16]{3,1,2,0:T(8,128)(2,1)}, bf16[2,16,4,16]{3,1,2,0:T(8,128)(2,1)S(1)}, u32[]{:S(2)}) copy-start(bf16[2,16,4,16]{3,1,2,0:T(8,128)(2,1)S(1)} %get-tuple-element.786) | copy-start | bytes 12292 | tf_op jit(solution)/shard_map/while
  374.7 6.0 copy-start.15
  374.7 8.8 %copy-start.12 = (bf16[2,16,4,16]{3,1,2,0:T(8,128)(2,1)S(1)}, bf16[2,16,4,16]{3,1,2,0:T(8,128)(2,1)}, u32[]{:S(2)}) copy-start(bf16[2,16,4,16]{3,1,2,0:T(8,128)(2,1)} %copy-done.11) | copy-start | bytes 12292 | tf_op jit(solution)/shard_map/while
  383.7 28.7 %copy-start.11 = (bf16[2,16,4,16]{3,1,2,0:T(8,128)(2,1)}, bf16[2,16,4,16]{3,1,2,0:T(8,128)(2,1)S(1)}, u32[]{:S(2)}) copy-start(bf16[2,16,4,16]{3,1,2,0:T(8,128)(2,1)S(1)} %get-tuple-element.786) | copy-start | bytes 12292 | tf_op jit(solution)/shard_map/while
  460.5 8.8 %copy-start.12 = (bf16[2,16,4,16]{3,1,2,0:T(8,128)(2,1)S(1)}, bf16[2,16,4,16]{3,1,2,0:T(8,128)(2,1)}, u32[]{:S(2)}) copy-start(bf16[2,16,4,16]{3,1,2,0:T(8,128)(2,1)} %copy-done.11) | copy-start | bytes 12292 | tf_op jit(solution)/shard_map/while
  469.8 28.7 %copy-start.11 = (bf16[2,16,4,16]{3,1,2,0:T(8,128)(2,1)}, bf16[2,16,4,16]{3,1,2,0:T(8,128)(2,1)S(1)}, u32[]{:S(2)}) copy-start(bf16[2,16,4,16]{3,1,2,0:T(8,128)(2,1)S(1)} %get-tuple-element.786) | copy-start | bytes 12292 | tf_op jit(solution)/shard_map/while
  546.6 8.8 %copy-start.12 = (bf16[2,16,4,16]{3,1,2,0:T(8,128)(2,1)S(1)}, bf16[2,16,4,16]{3,1,2,0:T(8,128)(2,1)}, u32[]{:S(2)}) copy-start(bf16[2,16,4,16]{3,1,2,0:T(8,128)(2,1)} %copy-done.11) | copy-start | bytes 12292 | tf_op jit(solution)/shard_map/while
  555.6 28.7 %copy-start.11 = (bf16[2,16,4,16]{3,1,2,0:T(8,128)(2,1)}, bf16[2,16,4,16]{3,1,2,0:T(8,128)(2,1)S(1)}, u32[]{:S(2)}) copy-start(bf16[2,16,4,16]{3,1,2,0:T(8,128)(2,1)S(1)} %get-tuple-element.786) | copy-start | bytes 12292 | tf_op jit(solution)/shard_map/while
  632.4 6.0 copy-start.15
  632.5 8.8 %copy-start.12 = (bf16[2,16,4,16]{3,1,2,0:T(8,128)(2,1)S(1)}, bf16[2,16,4,16]{3,1,2,0:T(8,128)(2,1)}, u32[]{:S(2)}) copy-start(bf16[2,16,4,16]{3,1,2,0:T(8,128)(2,1)} %copy-done.11) | copy-start | bytes 12292 | tf_op jit(solution)/shard_map/while
  641.7 28.7 %copy-start.11 = (bf16[2,16,4,16]{3,1,2,0:T(8,128)(2,1)}, bf16[2,16,4,16]{3,1,2,0:T(8,128)(2,1)S(1)}, u32[]{:S(2)}) copy-start(bf16[2,16,4,16]{3,1,2,0:T(8,128)(2,1)S(1)} %get-tuple-element.786) | copy-start | bytes 12292 | tf_op jit(solution)/shard_map/while
  718.5 6.0 copy-start.15
  718.5 8.8 %copy-start.12 = (bf16[2,16,4,16]{3,1,2,0:T(8,128)(2,1)S(1)}, bf16[2,16,4,16]{3,1,2,0:T(8,128)(2,1)}, u32[]{:S(2)}) copy-start(bf16[2,16,4,16]{3,1,2,0:T(8,128)(2,1)} %copy-done.11) | copy-start | bytes 12292 | tf_op jit(solution)/shard_map/while
  734.2 86.0 %all-reduce.75.cloned.1.call-start = ((), (), s32[]{:S(2)}) async-start(), calls=%async_computation.2 | async-start | bytes 1572864
  734.8 30.4 %copy-start.17 = (u32[32]{0:T(128)S(1)}, u32[32]{0:T(128)}, u32[]{:S(2)}) copy-start(u32[32]{0:T(128)} %constant.1019) | copy-start | bytes 388
  (80 other events, 175.4 us)
Sparse Core Ops, SparseCore 0:
  734.4 24.0 reduce-scatter.1
  765.4 54.8 all-reduce.74
where the time goes:
time: 835 us; the launch traced here: 829 us
  other arithmetic  315 us (38%)
  local copies, waits for them, and re-layouts  197 us (24%)
  matrix products  164 us (20%)
  waiting for transfers between devices  77.4 us (9%)
  loops' own time  34.4 us (4%)
  blocking collectives  26 us (3%)
  between operations  15.1 us (2%)
    dot_general x24, matrix products, tile_kernel(): jnp.einsum('acp,bcp->abp', left_px, right_px, precision=lax.Precision.HIG...  164 us
    reduce_sum x24, other arithmetic, relu_expect(): slope_right * right_var  69.1 us
    add x16, other arithmetic, relu_expect(): return lax.stop_gradient(value - linear) + linear  67.3 us
    dot_general x24, local copies, waits for them, and re-layouts, tile_kernel(): jnp.einsum('acp,bcp->abp', left_px, right_px, precision=lax.Precision.HIG...  62.5 us
    unnamed x3, waiting for transfers between devices  53.8 us
    mul x72, other arithmetic, spatial_blur(): return WEIGHT_VAR * summed / 9.0 + BIAS_VAR  52 us
    transpose x8, local copies, waits for them, and re-layouts, tile_kernel(): jnp.einsum('acp,bcp->abp', left_px, right_px, precision=lax.Precision.HIG...  50.5 us
    another operation x1, loops' own time, body(): lax.fori_loop(0, most_load, own_step, start)  34.4 us
  transfers between devices with their start and end apart: 2, of which 2 were waited for; matrix products, arithmetic and copies ran while one was open for 0% of the time, Pallas kernels for 0%

commit v1 on v0

v1 whole, which is shorter than its diff:
```python
import functools, math
import jax, jax.numpy as jnp, numpy as np
from jax import lax
from jax.experimental import pallas as pl
from jax.experimental.pallas import tpu as pltpu
from jax.sharding import PartitionSpec as P

CHAN = 3
LAYERS = 3
WEIGHT_VAR = 2.0
BIAS_VAR = 0.1
LANES = 128
SUBS = 8
TINY = 1e-30
F32 = jnp.float32


def arccos_coefficients(degree):
    nodes = 0.5 + 0.5 * np.cos(np.pi * (np.arange(400) + 0.5) / 400)
    target = np.arccos(1.0 - nodes) / np.sqrt(nodes)
    fit = np.polynomial.chebyshev.Chebyshev.fit(nodes, target, degree, domain=[0.0, 1.0])
    return [float(c) for c in fit.convert(kind=np.polynomial.Polynomial).coef]


COEFFS = arccos_coefficients(6)


def row_sums(ref, v, cols):
    f = [ref[j, v] for j in range(cols)]
    sub = lax.broadcasted_iota(jnp.int32, (SUBS, LANES), 0)
    above = jnp.where(sub > 0, pltpu.roll(f[-1], 1, 0), 0.0)
    below = jnp.where(sub < SUBS - 1, pltpu.roll(f[0], SUBS - 1, 0), 0.0)
    g = [above] + f + [below]
    out = []
    for j in range(0, cols, 2):
        mid = g[j + 1] + g[j + 2]
        out.append(g[j] + mid)
        out.append(mid + g[j + 3])
    return out


def sweep(ref, side, cols, emit, carry=(), chunk=8):
    def body(i, state):
        prev, cur, extra = state
        base = i * chunk
        for o in range(0, chunk, 2):
            nxt = row_sums(ref, base + o + 2, cols)
            nxt2 = row_sums(ref, base + o + 3, cols)
            mid = [a + b for a, b in zip(cur, nxt)]
            extra = emit(base + o, [a + b for a, b in zip(prev, mid)], extra)
            extra = emit(base + o + 1, [a + b for a, b in zip(mid, nxt2)], extra)
            prev, cur = nxt, nxt2
        return prev, cur, extra

    zero = [jnp.zeros((SUBS, LANES), F32) for _ in range(cols)]
    first = row_sums(ref, 1, cols)
    return lax.fori_loop(0, side // chunk, body, (zero, first, carry))[2]


def one_hot(index, count):
    return (lax.broadcasted_iota(jnp.int32, (index.shape[0], count), 1) == index).astype(F32)


def reversed_bits(x, count):
    out = 0 * x
    bit = 1
    while bit < count:
        out = 2 * out + x // bit % 2
        bit *= 2
    return out


def exact_dot(a, b, dims):
    return lax.dot_general(a, b, (dims, ((), ())), precision=lax.Precision.HIGHEST,
                           preferred_element_type=F32)


def kernel_body(dims, mode_ref, xa_ref, xb_ref, ca_ref, cb_ref, pa_ref, pb_ref, ga_ref, gb_ref,
                t_ref, y_ref, xr_ref, v_ref, sg_ref, f_ref, phi_ref, sin_ref, d_ref, g_ref, w_ref, kv_ref):
    gs, npos, side, col_count, per_row, part = dims
    members = gs // (per_row * part)
    tile_rows = 2 * members * part
    rows_of_dev = 2 * tile_rows
    width = per_row * tile_rows
    two = 2 * gs
    cols = side // SUBS
    tiles = gs * gs // LANES
    apt = LANES // gs
    blocks = npos // LANES
    bts = gs // SUBS
    per = LANES // SUBS
    diag = mode_ref[0] == 1
    member = mode_ref[1]
    lane = lax.broadcasted_iota(jnp.int32, (SUBS, LANES), 1)

    def col_of(tile):
        return tile // side, tile % side + 1

    def places(col, half, axis):
        shape = (gs, 1) if axis == 0 else (1, gs)
        i = lax.broadcasted_iota(jnp.int32, shape, axis)
        k = i // part % per_row
        held = jnp.bitwise_xor(member, reversed_bits(i // (part * per_row), members))
        idx = (half * members + held) * part + i % part
        blk = k * col_count + col
        return blk, blk * tile_rows + idx, k * tile_rows + idx
    col_a, half_a, col_b, half_b = mode_ref[2], mode_ref[3], mode_ref[4], mode_ref[5]
    blk_a, row_a, at_a = places(col_a, half_a, 0)
    blk_b, row_b, at_b = places(col_b, half_b, 0)
    blk_al = places(col_a, half_a, 1)[0]
    blk_bl = places(col_b, half_b, 1)[0]
    total_rows = ca_ref.shape[0]
    eye = (lax.broadcasted_iota(jnp.int32, (gs, gs), 0) == lax.broadcasted_iota(jnp.int32, (gs, gs), 1))
    upper = (lax.broadcasted_iota(jnp.int32, (gs, gs), 0) < lax.broadcasted_iota(jnp.int32, (gs, gs), 1))
    row_hot_a, row_hot_b = one_hot(row_a, total_rows), one_hot(row_b, total_rows)
    col_hot_a, col_hot_b = one_hot(at_a, width), one_hot(at_b, width)
    keep_ab = (blk_a <= blk_bl).astype(F32)
    keep_ba = (blk_b <= blk_al).astype(F32)
    keep_aa = (blk_a <= blk_al).astype(F32)
    keep_bb = (blk_b <= blk_bl).astype(F32)

    def chosen(rows, table, columns):
        picked = jnp.dot(rows.astype(jnp.bfloat16), table, preferred_element_type=F32)
        return lax.dot_general(picked.astype(jnp.bfloat16), columns.astype(jnp.bfloat16),
                               (((1,), (1,)), ((), ())), preferred_element_type=F32)
    ca, cb = ca_ref[...], cb_ref[...]
    w_ab = chosen(row_hot_a, cb, col_hot_b) * keep_ab
    w_ba = chosen(row_hot_b, ca, col_hot_a) * keep_ba
    w_aa = chosen(row_hot_a, ca, col_hot_a) * keep_aa
    w_bb = chosen(row_hot_b, cb, col_hot_b) * keep_bb
    w_off = w_ab + w_ba.T
    w_diag = jnp.where(eye, 0.0, jnp.where(upper, w_aa + w_aa.T, w_bb + w_bb.T))
    w_all = jnp.where(diag, w_diag, w_off)
    hot_rows = lax.broadcasted_iota(jnp.int32, (tiles, gs), 0) * apt
    hot_cols = lax.broadcasted_iota(jnp.int32, (tiles, gs), 1)
    w_rows = jnp.concatenate(
        [exact_dot((hot_cols == hot_rows + i).astype(F32), w_all, ((1,), (0,))) for i in range(apt)], 1)
    for k in range(tiles):
        w_ref[k] = w_rows[k:k + 1]
    self_a = jnp.sum(jnp.where(eye, w_aa, 0.0), 0, keepdims=True)
    self_b = jnp.sum(jnp.where(eye, w_bb, 0.0), 0, keepdims=True)
    self_row = jnp.concatenate([jnp.zeros((1, two), F32), self_a, self_b], 1)
    self_row = jnp.where(diag, self_row, 0.0)

    for s in range(blocks):
        for h in range(2):
            parts = []
            for ch in (2 * h, 2 * h + 1):
                if ch < CHAN:
                    sl = pl.ds(ch * npos + s * LANES, LANES)
                    parts += [xa_ref[:, sl].astype(F32), xb_ref[:, sl].astype(F32)]
                else:
                    for ref in (xa_ref, xb_ref):
                        total = 0.0
                        for c in range(CHAN):
                            x = ref[:, pl.ds(c * npos + s * LANES, LANES)].astype(F32)
                            total = total + x * x
                        parts.append(total * (1.0 / CHAN))
            t_ref[h, pl.ds(s * LANES, LANES), :] = jnp.concatenate(parts, 0).T
    zeros = jnp.zeros((SUBS, LANES), F32)
    for j in range(cols):
        for v in (0, side + 1):
            f_ref[0, j, v] = zeros
            f_ref[1, j, v] = zeros
            y_ref[0, j, v] = zeros
            y_ref[1, j, v] = zeros
            for l in range(LAYERS):
                v_ref[l, j, v] = zeros
                phi_ref[l, j, v] = zeros
    def regroup(v, _):
        for j in range(cols):
            for h in range(2):
                y_ref[h, j, v + 1] = t_ref[h, pl.ds(j * side + v, SUBS, stride=LANES), :]
        return 0
    lax.fori_loop(0, side, regroup, 0)

    def block_of(ref_at, blk):
        vals = []
        for t in range(per):
            j, v = col_of(blk * per + t)
            vals.append(ref_at(j, v))
        return jnp.concatenate(vals, 0)

    for blk in range(blocks):
        for h in range(2):
            xr_ref[h, :, pl.ds(blk * LANES, LANES)] = block_of(lambda j, v: y_ref[h, j, v], blk).T
    def var_emit(l, scale):
        def emit(v, sums, extra):
            for j in range(cols):
                v_ref[l, j, v + 1] = sums[j] * scale + BIAS_VAR
            return extra
        return emit
    sweep(y_ref.at[1], side, cols, var_emit(0, WEIGHT_VAR / 9.0))
    sweep(v_ref.at[0], side, cols, var_emit(1, 0.5 * WEIGHT_VAR / 9.0))
    sweep(v_ref.at[1], side, cols, var_emit(2, 0.5 * WEIGHT_VAR / 9.0))
    for l in range(LAYERS):
        for blk in range(blocks):
            t = block_of(lambda j, v: v_ref[l, j, v], blk).T
            t = t[two:]
            sg_ref[l, :, pl.ds(blk * LANES, LANES)] = t * lax.rsqrt(t)
    total = jnp.zeros((SUBS, LANES), F32)
    for j in range(cols):
        for v in range(side):
            total = total + v_ref[LAYERS - 1, j, v + 1]
    kself = jnp.sum(total, 0, keepdims=True) * (0.5 * WEIGHT_VAR / npos) + BIAS_VAR

    def zero_acc(i, _):
        sl = pl.ds(pl.multiple_of(i * LANES, LANES), LANES)
        for l in range(LAYERS):
            d_ref[l, :, sl] = jnp.zeros((2 * two, LANES), F32)
        for h in range(2):
            g_ref[h, :, sl] = jnp.zeros((LANES, LANES), F32)
        return 0
    lax.fori_loop(0, blocks, zero_acc, 0)

    sub = lax.broadcasted_iota(jnp.int32, (SUBS, LANES), 0)

    def rows_of(ref, slot, base, k, sl):
        at = pl.multiple_of(base + k * apt // SUBS * SUBS, SUBS)
        t = pltpu.roll(ref[slot, pl.ds(at, SUBS), sl], (SUBS - k * apt % SUBS) % SUBS, 0)
        return [t[a:a + 1] for a in range(apt)]

    def add_rows(ref, slot, base, k, sl, rows):
        at = pl.multiple_of(base + k * apt // SUBS * SUBS, SUBS)
        t = jnp.concatenate(rows + [jnp.zeros((SUBS - apt, LANES), F32)], 0)
        ref[slot, pl.ds(at, SUBS), sl] = ref[slot, pl.ds(at, SUBS), sl] + pltpu.roll(t, k * apt % SUBS, 0)

    def xtile(ch, img, sl):
        return xr_ref[ch // 2, pl.ds((ch % 2) * two + img, SUBS), sl]

    def pair_tile(k, _):
        a0 = k * apt

        def cross_plain(blk, _):
            sl = pl.ds(pl.multiple_of(blk * LANES, LANES), LANES)
            rows = []
            lefts = [rows_of(xr_ref, ch // 2, (ch % 2) * two, k, sl) for ch in range(CHAN)]
            for a in range(apt):
                left = [lefts[ch][a] for ch in range(CHAN)]
                for bt in range(bts):
                    acc = left[0] * xtile(0, gs + bt * SUBS, sl)
                    for ch in range(1, CHAN):
                        acc = acc + left[ch] * xtile(ch, gs + bt * SUBS, sl)
                    rows.append(acc)
            put(blk, jnp.concatenate(rows, 0).T)
            return 0

        def cross_diag(blk, _):
            sl = pl.ds(pl.multiple_of(blk * LANES, LANES), LANES)
            rows = []
            lefts = [[rows_of(xr_ref, ch // 2, (ch % 2) * two + o, k, sl) for ch in range(CHAN)]
                     for o in (0, gs)]
            for a in range(apt):
                l0 = [lefts[0][ch][a] for ch in range(CHAN)]
                l1 = [lefts[1][ch][a] for ch in range(CHAN)]
                for bt in range(bts):
                    first = sub + bt * SUBS > a0 + a
                    acc = 0.0
                    for ch in range(CHAN):
                        acc = acc + jnp.where(first, l0[ch], l1[ch]) * jnp.where(
                            first, xtile(ch, bt * SUBS, sl), xtile(ch, gs + bt * SUBS, sl))
                    rows.append(acc)
            put(blk, jnp.concatenate(rows, 0).T)
            return 0

        def put(blk, t):
            half = blk * per
            j = half // side
            v = half % side + 1
            for i in range(per):
                f_ref[0, j, v + i] = t[i * SUBS:(i + 1) * SUBS]

        @pl.when(jnp.logical_not(diag))
        def _():
            lax.fori_loop(0, blocks, cross_plain, 0)

        @pl.when(diag)
        def _():
            lax.fori_loop(0, blocks, cross_diag, 0)

        ia = a0 + lane // gs
        ib = lane % gs
        second = jnp.logical_and(diag, ib <= ia)
        il = two + ia + jnp.where(second, gs, 0)
        ir = two + ib + jnp.where(jnp.logical_and(diag, ib > ia), 0, gs)

        def relu_emit(l, scale, dst):
            def emit(v, sums, extra):
                for j in range(cols):
                    k12 = sums[j] * scale + BIAS_VAR
                    var = v_ref[l, j, v + 1]
                    prod = jnp.take_along_axis(var, il, axis=1) * jnp.take_along_axis(var, ir, axis=1)
                    inv = lax.rsqrt(prod)
                    cosine = k12 * inv
                    w = jnp.maximum(1.0 - jnp.abs(cosine), TINY)
                    poly = COEFFS[-1]
                    for c in COEFFS[-2::-1]:
                        poly = poly * w + c
                    angle = (w * lax.rsqrt(w)) * poly
                    phi = jnp.where(cosine >= 0.0, math.pi - angle, angle)
                    rest = jnp.maximum(prod - k12 * k12, TINY)
                    root = rest * lax.rsqrt(rest)
                    value = root + phi * k12
                    phi_ref[l, j, v + 1] = phi
                    sin_ref[l, j, v + 1] = root * inv
                    if dst is None:
                        extra = extra + value
                    else:
                        f_ref[dst, j, v + 1] = value
                return extra
            return emit

        inner = WEIGHT_VAR / (9.0 * 2.0 * math.pi)
        sweep(f_ref.at[0], side, cols, relu_emit(0, WEIGHT_VAR / (9.0 * CHAN), 1))
        sweep(f_ref.at[1], side, cols, relu_emit(1, inner, 0))
        total = sweep(f_ref.at[0], side, cols, relu_emit(2, inner, None), jnp.zeros((SUBS, LANES), F32))
        kv_ref[k] = jnp.sum(total, 0, keepdims=True) * (
            WEIGHT_VAR / (2.0 * math.pi * npos)) + BIAS_VAR

        wrow = w_ref[k] * (WEIGHT_VAR / npos)
        wrow = jnp.broadcast_to(wrow, (SUBS, LANES))
        wscaled = wrow * inner

        def back_emit(l, dst, scaled):
            def emit(v, sums, extra):
                for j in range(cols):
                    grad = sums[j] * wscaled if scaled else sums[j]
                    sin_ref[l, j, v + 1] = sin_ref[l, j, v + 1] * grad
                    f_ref[dst, j, v + 1] = phi_ref[l, j, v + 1] * grad
                return extra
            return emit
        sweep(phi_ref.at[2], side, cols, back_emit(1, 0, True))
        sweep(f_ref.at[0], side, cols, back_emit(0, 1, False))

        def last_emit(v, sums, extra):
            for j in range(cols):
                f_ref[0, j, v + 1] = sums[j]
            return extra
        sweep(f_ref.at[1], side, cols, last_emit)

        def fold(is_diag):
            def body(blk, _):
                sl = pl.ds(pl.multiple_of(blk * LANES, LANES), LANES)
                half = blk * per
                j = half // side
                v = half % side + 1

                def turned(get):
                    return jnp.concatenate([get(j, v + i) for i in range(per)], 0).T

                for l in range(LAYERS + 1):
                    if l < LAYERS - 1:
                        h = turned(lambda j, v: sin_ref[l, j, v])
                    elif l == LAYERS - 1:
                        h = turned(lambda j, v: sin_ref[l, j, v] * wrow)
                    else:
                        h = turned(lambda j, v: f_ref[0, j, v])
                    h = [[h[(a * bts + bt) * SUBS:(a * bts + bt + 1) * SUBS] for bt in range(bts)]
                         for a in range(apt)]
                    if l < LAYERS:
                        terms = [(d_ref, l, two, sg_ref, l, 0)]
                    else:
                        terms = [(g_ref, ch // 2, (ch % 2) * two, xr_ref, ch // 2, (ch % 2) * two)
                                 for ch in range(CHAN)]
                    for acc, slot, base, src, at0, base0 in terms:
                        if not is_diag:
                            left = rows_of(src, at0, base0, k, sl)
                            sums = [0.0] * apt
                            for bt in range(bts):
                                right = src[at0, pl.ds(base0 + gs + bt * SUBS, SUBS), sl]
                                out = 0.0
                                for a in range(apt):
                                    out = out + h[a][bt] * left[a]
                                    sums[a] = sums[a] + h[a][bt] * right
                                at = pl.ds(base + gs + bt * SUBS, SUBS)
                                acc[slot, at, sl] = acc[slot, at, sl] + out
                            add_rows(acc, slot, base, k, sl, [jnp.sum(t, 0, keepdims=True) for t in sums])
                        else:
                            for side_set in range(2):
                                off = side_set * gs
                                left = rows_of(src, at0, base0 + off, k, sl)
                                sums = [0.0] * apt
                                for bt in range(bts):
                                    right = src[at0, pl.ds(base0 + off + bt * SUBS, SUBS), sl]
                                    out = 0.0
                                    for a in range(apt):
                                        row = sub + bt * SUBS
                                        keep = row < a0 + a if side_set else row > a0 + a
                                        part = jnp.where(keep, h[a][bt], 0.0)
                                        out = out + part * left[a]
                                        sums[a] = sums[a] + part * right
                                    at = pl.ds(base + off + bt * SUBS, SUBS)
                                    acc[slot, at, sl] = acc[slot, at, sl] + out
                                add_rows(acc, slot, base + off, k, sl, [jnp.sum(t, 0, keepdims=True) for t in sums])
                return 0
            lax.fori_loop(0, blocks, body, 0)

        @pl.when(jnp.logical_not(diag))
        def _():
            fold(False)

        @pl.when(diag)
        def _():
            fold(True)
        return 0

    lax.fori_loop(0, tiles, pair_tile, 0)

    step = WEIGHT_VAR / (9.0 * 2.0 * math.pi)
    for l in range(LAYERS):
        for blk in range(blocks):
            t = d_ref[l, :, pl.ds(blk * LANES, LANES)].T
            for i in range(per):
                j, v = col_of(blk * per + i)
                scale = (1.0 if l == 2 else 1.0 if l == 1 else step) / (4.0 * math.pi)
                sin_ref[l, j, v] = t[i * SUBS:(i + 1) * SUBS] * lax.rsqrt(v_ref[l, j, v]) * scale
    selfw = self_row * (0.5 * WEIGHT_VAR / npos)
    def seed(v, _):
        for j in range(cols):
            phi_ref[2, j, v + 1] = sin_ref[2, j, v + 1] + selfw
        return 0
    lax.fori_loop(0, side, seed, 0)
    def chain_emit(l):
        def emit(v, sums, extra):
            for j in range(cols):
                phi_ref[l, j, v + 1] = sin_ref[l, j, v + 1] + sums[j] * (0.5 * WEIGHT_VAR / 9.0)
            return extra
        return emit
    sweep(phi_ref.at[2], side, cols, chain_emit(1))
    sweep(phi_ref.at[1], side, cols, chain_emit(0))
    for h in range(2):
        for blk in range(blocks):
            t = g_ref[h, :, pl.ds(blk * LANES, LANES)].T
            for i in range(per):
                j, v = col_of(blk * per + i)
                f_ref[h, j, v] = t[i * SUBS:(i + 1) * SUBS]
    low = lane < two
    def final_emit(v, sums, extra):
        for j in range(cols):
            e = sums[j] * (WEIGHT_VAR / 9.0 * 2.0 / CHAN)
            e = jnp.where(low, pltpu.roll(e, two, 1), e)
            for h in range(2):
                t_ref[h, pl.ds(j * side + v, SUBS, stride=LANES), :] = (
                    f_ref[h, j, v + 1] * (step * step / CHAN) + y_ref[h, j, v + 1] * e)
        return extra
    sweep(phi_ref.at[0], side, cols, final_emit)
    for h in range(2):
        for s in range(blocks):
            t = t_ref[h, pl.ds(s * LANES, LANES), :].T
            for q in range(2):
                ch = 2 * h + q
                if ch < CHAN:
                    sl = pl.ds(ch * npos + s * LANES, LANES)
                    ga_ref[:, sl] = t[q * two:q * two + gs]
                    gb_ref[:, sl] = t[q * two + gs:(q + 1) * two]

    kv = jnp.concatenate([kv_ref[k] for k in range(tiles)], 0)
    values = 0.0
    for i in range(apt):
        values = values + exact_dot((hot_cols == hot_rows + i).astype(F32), kv[:, i * gs:(i + 1) * gs],
                                    ((0,), (0,)))
    self_va = jnp.where(eye, kself[:, two:two + gs], 0.0)
    self_vb = jnp.where(eye, kself[:, two + gs:], 0.0)
    up = jnp.where(upper, values, 0.0)
    lo = jnp.where(jnp.logical_or(upper, eye), 0.0, values)
    val_aa = (up + up.T + self_va) * keep_aa
    val_bb = (lo + lo.T + self_vb) * keep_bb
    def place(at_row, device):
        ahead = reversed_bits(jnp.bitwise_xor(at_row // rows_of_dev, device), total_rows // rows_of_dev)
        return ahead * rows_of_dev + at_row % rows_of_dev

    def spread(rows, vals, columns):
        return exact_dot(one_hot(rows, total_rows), exact_dot(vals, columns, ((1,), (0,))), ((0,), (0,)))
    rows_here = place(jnp.where(diag, row_a, row_b), mode_ref[6])
    pa_ref[...] = spread(rows_here, jnp.where(diag, val_aa, values.T * keep_ba), col_hot_a)
    rows_there = place(jnp.where(diag, row_b, row_a), mode_ref[7])
    pb_ref[...] = spread(rows_there, jnp.where(diag, val_bb, values * keep_ab), col_hot_b)


def pair_kernel(mode, xa, xb, ca, cb, col_count, per_row, part):
    gs, feat = xa.shape
    npos = feat // CHAN
    side = math.isqrt(npos)
    cols = side // SUBS
    tiles = gs * gs // LANES
    dims = (gs, npos, side, col_count, per_row, part)
    field = (cols, side + 2, SUBS, LANES)
    vm = pl.BlockSpec(memory_space=pltpu.VMEM)
    return pl.pallas_call(
        functools.partial(kernel_body, dims),
        out_shape=(jax.ShapeDtypeStruct(ca.shape, F32),
                   jax.ShapeDtypeStruct(cb.shape, F32),
                   jax.ShapeDtypeStruct((gs, feat), F32),
                   jax.ShapeDtypeStruct((gs, feat), F32)),
        in_specs=[pl.BlockSpec(memory_space=pltpu.SMEM), vm, vm, vm, vm],
        out_specs=(vm, vm, vm, vm),
        scratch_shapes=[
            pltpu.VMEM((2, npos, LANES), F32),
            pltpu.VMEM((2,) + field, F32),
            pltpu.VMEM((2, LANES, npos), F32),
            pltpu.VMEM((LAYERS,) + field, F32),
            pltpu.VMEM((LAYERS, 2 * gs, npos), F32),
            pltpu.VMEM((2,) + field, F32),
            pltpu.VMEM((LAYERS,) + field, F32),
            pltpu.VMEM((LAYERS,) + field, F32),
            pltpu.VMEM((LAYERS, 4 * gs, npos), F32),
            pltpu.VMEM((2, LANES, npos), F32),
            pltpu.VMEM((tiles, 1, LANES), F32),
            pltpu.VMEM((tiles, 1, LANES), F32),
        ],
        compiler_params=pltpu.CompilerParams(vmem_limit_bytes=48 * 1024 * 1024),
        cost_estimate=pl.CostEstimate(flops=2 * 10**8, bytes_accessed=2 * 10**6, transcendentals=10**6),
        name="pair_fields",
    )(mode, xa, xb, ca, cb)


def exchange(x, rows, cols, target):
    perm = []
    for r in range(rows):
        for c in range(cols):
            tr, tc = target(r, c)
            perm.append((r * cols + c, tr * cols + tc))
    return lax.ppermute(x, ("row", "col"), perm)


def body(images, cotangent):
    rows = lax.axis_size("row")
    cols = lax.axis_size("col")
    row = lax.axis_index("row")
    col = lax.axis_index("col")
    per_row, _, part, feat = images.shape
    members = rows // 2
    groups = 2 * cols
    assert members == cols and members & (members - 1) == 0
    tile_rows = part * rows
    own = images.reshape(per_row * part, feat)

    def partner_of(r, c):
        half, m = r // members, r % members
        other = (half * cols + c + 1 + m) % groups
        return other // cols * members + m, other % cols

    def holder_of(r, c):
        half, m = r // members, r % members
        other = (half * cols + c - 1 - m) % groups
        return other // cols * members + m, other % cols

    cot_col = lax.all_gather(cotangent.reshape(2 * tile_rows, per_row * tile_rows), "row", axis=0, tiled=True)
    mine = own
    step = members // 2
    while step:
        s = step
        mine = jnp.concatenate([mine, exchange(mine, rows, cols, lambda r, c: (r ^ s, c))], 0)
        step //= 2
    theirs = exchange(mine, rows, cols, holder_of)
    cot_theirs = exchange(cot_col, rows, cols, holder_of)
    p_row, p_col = partner_of(row, col)
    member = row % members
    half = row // members
    diag = jnp.logical_and(member == members - 1, half == 1)
    mode = jnp.stack([diag.astype(jnp.int32), member, col, half, p_col, p_row // members, row, p_row])
    mode = mode.astype(jnp.int32)
    pa, pb, ga, gb = pair_kernel(mode, mine, theirs, cot_col, cot_theirs, cols, per_row, part)
    grads = ga + exchange(gb, rows, cols, partner_of)
    table = pa + exchange(pb, rows, cols, partner_of)
    step = 1
    while step < rows:
        s = step
        n = table.shape[0] // 2
        table = table[:n] + exchange(table[n:], rows, cols, lambda r, c: (r ^ s, c))
        if s < members:
            n = grads.shape[0] // 2
            grads = grads[:n] + exchange(grads[n:], rows, cols, lambda r, c: (r ^ s, c))
        step *= 2
    return (table.reshape(2, tile_rows, per_row, 1, tile_rows),
            grads.reshape(per_row, 1, part, feat))


def solution(mesh):
    return jax.shard_map(
        body,
        mesh=mesh,
        in_specs=(P(None, "col", "row", None), P("row", None, None, "col", None)),
        out_specs=(P("row", None, None, "col", None), P(None, "col", "row", None)),
        check_vma=False,
    )
```

time: 835 us -> 111 us (0.13)
  other arithmetic: 315 us -> 0.12 us
  local copies, waits for them, and re-layouts: 197 us -> 2.49 us
  matrix products: 164 us -> 0 us
  Pallas kernels: 0 us -> 51.2 us
  waiting for transfers between devices: 77.4 us -> 27.8 us
  loops' own time: 34.4 us -> 0 us
  starting transfers between devices: 0.08 us -> 20 us
  blocking collectives: 26 us -> 8.21 us
  between operations: 15.1 us -> 0.75 us
    dot_general x24 -> x0, matrix products: 164 us -> none  [tile_kernel(): jnp.einsum('acp,bcp->abp', left_px, right_px, precision=lax.Precision.HIG...]
    mul x304 -> x0, other arithmetic: 90.6 us -> none  [the longest x72 52 us: spatial_blur(): return WEIGHT_VAR * summed / 9.0 + BIAS_VAR]
    add x80 -> x7, other arithmetic: 86.1 us -> 0.11 us  [the longest x1 0.04 us: body(): grads = ga + exchange(gb, rows, cols, partner_of)]
    reduce_sum x42 -> x0, other arithmetic: 71 us -> none  [the longest x24 69.1 us: relu_expect(): slope_right * right_var]
    dot_general x24 -> x0, local copies, waits for them, and re-layouts: 62.5 us -> none  [tile_kernel(): jnp.einsum('acp,bcp->abp', left_px, right_px, precision=lax.Precision.HIG...]
    unnamed x3 -> x0, waiting for transfers between devices: 53.8 us -> none
    pallas_call x0 -> x1, Pallas kernels: none -> 51.2 us  [pair_kernel(): pl.pallas_call(functools.partial(kernel_body, dims), out_shape=(jax.Shape...]
    transpose x8 -> x0, local copies, waits for them, and re-layouts: 50.5 us -> none  [tile_kernel(): jnp.einsum('acp,bcp->abp', left_px, right_px, precision=lax.Precision.HIG...]
  transfers between devices with their start and end apart: 2 -> 11, of which waited for: 2 -> 8; matrix products, arithmetic and copies ran while one was open for 0% -> 1% of each run, Pallas kernels for 0% -> 0%
where the time goes in v1:
time: 111 us
  Pallas kernels  51.2 us (46%)
  waiting for transfers between devices  27.8 us (25%)
  starting transfers between devices  20 us (18%)
  blocking collectives  8.21 us (7%)
  local copies, waits for them, and re-layouts  2.49 us (2%)
    pallas_call x1, Pallas kernels, pair_kernel(): pl.pallas_call(functools.partial(kernel_body, dims), out_shape=(jax.Shape...  51.2 us
    ppermute x11, waiting for transfers between devices, exchange(): return lax.ppermute(x, ('row', 'col'), perm)  27.8 us
    ppermute x11, starting transfers between devices, exchange(): return lax.ppermute(x, ('row', 'col'), perm)  20 us
    all_gather x1, blocking collectives, body(): lax.all_gather(cotangent.reshape(2 * tile_rows, per_row * tile_rows), 'ro...  8.21 us
  transfers between devices with their start and end apart: 11, of which 8 were waited for; matrix products, arithmetic and copies ran while one was open for 1% of the time, Pallas kernels for 0%

profile of v1, /device:TPU:0, one launch (start us, length us, event | category | flops | bytes accessed | tf_op | source)
XLA Modules:
  0.0 110.6 jit_solution(3767233923410733613)
XLA Ops:
  0.6 0.8 reshape.16
  1.5 3.0 %collective-permute-start = (bf16[8,3072]{1,0:T(8,128)(2,1)S(1)}, bf16[8,3072]{1,0:T(8,128)(2,1)S(1)}, u32[]{:S(2)}, u32[]{:S(2)}) collective-permute-start(bf16[8,3072]{1,0:T(8,128)(2,1)S(1)} %reshape.16), channel_id=1, source_target_pairs={{0,8},{1,9},{2,10},{3,11},{4,12},{5,13},{6,14},{7,15},{8,0},{9,1},... | collective-permute-start | bytes 147464 | tf_op jit(solution)/shard_map/ppermute | solution.py:523
  4.5 2.1 %collective-permute-done = bf16[8,3072]{1,0:T(8,128)(2,1)S(1)} collective-permute-done((bf16[8,3072]{1,0:T(8,128)(2,1)S(1)}, bf16[8,3072]{1,0:T(8,128)(2,1)S(1)}, u32[]{:S(2)}, u32[]{:S(2)}) %collective-permute-start) | collective-permute-done | bytes 49184 | tf_op jit(solution)/shard_map/ppermute | solution.py:523
  6.6 1.3 %collective-permute-done.1 = bf16[16,3072]{1,0:T(8,128)(2,1)S(1)} collective-permute-done((bf16[16,3072]{1,0:T(8,128)(2,1)S(1)}, bf16[16,3072]{1,0:T(8,128)(2,1)S(1)}, u32[]{:S(2)}, u32[]{:S(2)}) %collective-permute-start.1) | collective-permute-done | bytes 98336 | tf_op jit(solution)/shard_map/ppermute | solution.py:523
  7.9 5.1 %collective-permute-start.2 = (bf16[32,3072]{1,0:T(8,128)(2,1)S(1)}, bf16[32,3072]{1,0:T(8,128)(2,1)S(1)}, u32[]{:S(2)}, u32[]{:S(2)}) collective-permute-start(bf16[32,3072]{1,0:T(8,128)(2,1)S(1)} %constant_dynamic-update-slice_fusion.xa_ref), channel_id=1, source_target_pairs={{0,19},{1,0},{2,1},{3,2},{4,22},{5,23},{6,4},{7,5},{8,25},{9,26},{... | collective-permute-start | bytes 589832 | tf_op jit(solution)/shard_map/ppermute | solution.py:523
  13.1 0.1 reshape.17
  13.1 8.2 %all_gather.3.ca_ref = bf16[256,64]{1,0:T(8,128)(2,1)S(1)} all-gather(bf16[32,64]{1,0:T(8,128)(2,1)S(1)} %reshape.17), channel_id=1, replica_groups=mesh['row'=8,'col'=4] {'row'}, dimensions={0}, use_global_device_ids=true | all-gather | bytes 36864 | tf_op jit(solution)/shard_map/all_gather | solution.py:548
  21.4 3.4 %collective-permute-start.3 = (bf16[256,64]{1,0:T(8,128)(2,1)S(1)}, bf16[256,64]{1,0:T(8,128)(2,1)S(1)}, u32[]{:S(2)}, u32[]{:S(2)}) collective-permute-start(bf16[256,64]{1,0:T(8,128)(2,1)S(1)} %all_gather.3.ca_ref), channel_id=1, source_target_pairs={{0,19},{1,0},{2,1},{3,2},{4,22},{5,23},{6,4},{7,5},{8,25},{9,26},{... | collective-permute-start | bytes 98312 | tf_op jit(solution)/shard_map/ppermute | solution.py:523
  24.8 0.1 stack.39.mode_ref
  24.9 1.8 %collective-permute-done.3.cb_ref = bf16[256,64]{1,0:T(8,128)(2,1)S(1)} collective-permute-done((bf16[256,64]{1,0:T(8,128)(2,1)S(1)}, bf16[256,64]{1,0:T(8,128)(2,1)S(1)}, u32[]{:S(2)}, u32[]{:S(2)}) %collective-permute-start.3) | collective-permute-done | bytes 32800 | tf_op jit(solution)/shard_map/ppermute | solution.py:523
  26.7 51.2 %pair_fields.1 = (f32[256,64]{1,0:T(8,128)S(1)}, f32[256,64]{1,0:T(8,128)S(1)}, f32[32,3072]{1,0:T(8,128)S(1)}, f32[32,3072]{1,0:T(8,128)S(1)}) custom-call(s32[8]{0:T(128)S(1)} %stack.39.mode_ref, bf16[32,3072]{1,0:T(8,128)(2,1)S(1)} %constant_dynamic-update-slice_fusion.xa_ref, bf16[32,3072]{1,0:T(8,128)(2,1)S(1)} %collective-permute-done.2.xb_ref, ...), custom_call_target="tpu_custom_call" | custom-call | flops 200000000 | bytes 2000000 | tf_op jit(solution)/shard_map/pair_fields/pallas_call | solution.py:489
  77.9 0.7 collective-permute-start.8
  78.6 0.5 collective-permute-start.4
  79.0 14.5 %collective-permute-done.4 = f32[256,64]{1,0:T(8,128)S(1)} collective-permute-done((f32[256,64]{1,0:T(8,128)S(1)}, f32[256,64]{1,0:T(8,128)S(1)}, u32[]{:S(2)}, u32[]{:S(2)}) %collective-permute-start.4) | collective-permute-done | bytes 65568 | tf_op jit(solution)/shard_map/ppermute | solution.py:523
  93.5 5.4 %collective-permute-start.5 = (f32[128,64]{1,0:T(8,128)S(1)}, f32[128,64]{1,0:T(8,128)S(1)}, u32[]{:S(2)}, u32[]{:S(2)}) collective-permute-start(f32[128,64]{1,0:T(8,128)S(1)} %slice.41), channel_id=1, source_target_pairs={{0,4},{1,5},{2,6},{3,7},{4,0},{5,1},{6,2},{7,3},{8,12},{9,13},{10,... | collective-permute-start | bytes 98312 | tf_op jit(solution)/shard_map/ppermute | solution.py:523
  98.9 0.9 collective-permute-done.5
  100.0 0.4 collective-permute-start.9
  100.4 3.4 %collective-permute-done.6 = f32[64,64]{1,0:T(8,128)S(1)} collective-permute-done((f32[64,64]{1,0:T(8,128)S(1)}, f32[64,64]{1,0:T(8,128)S(1)}, u32[]{:S(2)}, u32[]{:S(2)}) %collective-permute-start.6) | collective-permute-done | bytes 16416 | tf_op jit(solution)/shard_map/ppermute | solution.py:523
  103.8 1.3 %collective-permute-start.7 = (f32[32,64]{1,0:T(8,128)S(1)}, f32[32,64]{1,0:T(8,128)S(1)}, u32[]{:S(2)}, u32[]{:S(2)}) collective-permute-start(f32[32,64]{1,0:T(8,128)S(1)} %slice.45), channel_id=1, source_target_pairs={{0,16},{1,17},{2,18},{3,19},{4,20},{5,21},{6,22},{7,23},{8,24},{9,... | collective-permute-start | bytes 24584 | tf_op jit(solution)/shard_map/ppermute | solution.py:523
  105.2 0.1 collective-permute-start.10
  105.2 2.4 %collective-permute-done.7 = f32[32,64]{1,0:T(8,128)S(1)} collective-permute-done((f32[32,64]{1,0:T(8,128)S(1)}, f32[32,64]{1,0:T(8,128)S(1)}, u32[]{:S(2)}, u32[]{:S(2)}) %collective-permute-start.7) | collective-permute-done | bytes 8224 | tf_op jit(solution)/shard_map/ppermute | solution.py:523
  107.7 0.7 reshape.18
  108.4 1.4 %collective-permute-done.10 = f32[8,3072]{1,0:T(8,128)S(1)} collective-permute-done((f32[8,3072]{1,0:T(8,128)S(1)}, f32[8,3072]{1,0:T(8,128)S(1)}, u32[]{:S(2)}, u32[]{:S(2)}) %collective-permute-start.10) | collective-permute-done | bytes 98336 | tf_op jit(solution)/shard_map/ppermute | solution.py:523
  109.8 0.7 reshape.19
  (23 shorter events, 0.3 us)
Async XLA Ops:
  1.5 5.1 %collective-permute-start = (bf16[8,3072]{1,0:T(8,128)(2,1)S(1)}, bf16[8,3072]{1,0:T(8,128)(2,1)S(1)}, u32[]{:S(2)}, u32[]{:S(2)}) collective-permute-start(bf16[8,3072]{1,0:T(8,128)(2,1)S(1)} %reshape.16), channel_id=1, source_target_pairs={{0,8},{1,9},{2,10},{3,11},{4,12},{5,13},{6,14},{7,15},{8,0},{9,1},... | collective-permute-start | bytes 147464 | tf_op jit(solution)/shard_map/ppermute | solution.py:523
  6.5 1.4 %collective-permute-start.1 = (bf16[16,3072]{1,0:T(8,128)(2,1)S(1)}, bf16[16,3072]{1,0:T(8,128)(2,1)S(1)}, u32[]{:S(2)}, u32[]{:S(2)}) collective-permute-start(bf16[16,3072]{1,0:T(8,128)(2,1)S(1)} %pad_maximum_fusion), channel_id=1, source_target_pairs={{0,4},{1,5},{2,6},{3,7},{4,0},{5,1},{6,2},{7,3},{8,12},{9,13},{10,... | collective-permute-start | bytes 294920 | tf_op jit(solution)/shard_map/ppermute | solution.py:523
  6.6 6.4 %copy-start = (bf16[2,16,4,1,16]{4,2,3,1,0:T(4,128)(2,1)S(1)}, bf16[2,16,4,1,16]{4,2,3,1,0:T(4,128)(2,1)}, u32[]{:S(2)}) copy-start(bf16[2,16,4,1,16]{4,2,3,1,0:T(4,128)(2,1)} %param.3) | copy-start | bytes 12292
  7.9 18.8 %collective-permute-start.2 = (bf16[32,3072]{1,0:T(8,128)(2,1)S(1)}, bf16[32,3072]{1,0:T(8,128)(2,1)S(1)}, u32[]{:S(2)}, u32[]{:S(2)}) collective-permute-start(bf16[32,3072]{1,0:T(8,128)(2,1)S(1)} %constant_dynamic-update-slice_fusion.xa_ref), channel_id=1, source_target_pairs={{0,19},{1,0},{2,1},{3,2},{4,22},{5,23},{6,4},{7,5},{8,25},{9,26},{... | collective-permute-start | bytes 589832 | tf_op jit(solution)/shard_map/ppermute | solution.py:523
  21.4 5.3 %collective-permute-start.3 = (bf16[256,64]{1,0:T(8,128)(2,1)S(1)}, bf16[256,64]{1,0:T(8,128)(2,1)S(1)}, u32[]{:S(2)}, u32[]{:S(2)}) collective-permute-start(bf16[256,64]{1,0:T(8,128)(2,1)S(1)} %all_gather.3.ca_ref), channel_id=1, source_target_pairs={{0,19},{1,0},{2,1},{3,2},{4,22},{5,23},{6,4},{7,5},{8,25},{9,26},{... | collective-permute-start | bytes 98312 | tf_op jit(solution)/shard_map/ppermute | solution.py:523
  77.9 22.0 %collective-permute-start.8 = (f32[32,3072]{1,0:T(8,128)S(1)}, f32[32,3072]{1,0:T(8,128)S(1)}, u32[]{:S(2)}, u32[]{:S(2)}) collective-permute-start(f32[32,3072]{1,0:T(8,128)S(1)} %get-tuple-element.9), channel_id=1, source_target_pairs={{0,1},{1,2},{2,3},{3,16},{4,6},{5,7},{6,20},{7,21},{8,11},{9,24},{... | collective-permute-start | bytes 1179656 | tf_op jit(solution)/shard_map/ppermute | solution.py:523
  78.6 14.9 %collective-permute-start.4 = (f32[256,64]{1,0:T(8,128)S(1)}, f32[256,64]{1,0:T(8,128)S(1)}, u32[]{:S(2)}, u32[]{:S(2)}) collective-permute-start(f32[256,64]{1,0:T(8,128)S(1)} %get-tuple-element.7), channel_id=1, source_target_pairs={{0,1},{1,2},{2,3},{3,16},{4,6},{5,7},{6,20},{7,21},{8,11},{9,24},{... | collective-permute-start | bytes 196616 | tf_op jit(solution)/shard_map/ppermute | solution.py:523
  93.5 6.3 %collective-permute-start.5 = (f32[128,64]{1,0:T(8,128)S(1)}, f32[128,64]{1,0:T(8,128)S(1)}, u32[]{:S(2)}, u32[]{:S(2)}) collective-permute-start(f32[128,64]{1,0:T(8,128)S(1)} %slice.41), channel_id=1, source_target_pairs={{0,4},{1,5},{2,6},{3,7},{4,0},{5,1},{6,2},{7,3},{8,12},{9,13},{10,... | collective-permute-start | bytes 98312 | tf_op jit(solution)/shard_map/ppermute | solution.py:523
  99.9 4.0 %collective-permute-start.6 = (f32[64,64]{1,0:T(8,128)S(1)}, f32[64,64]{1,0:T(8,128)S(1)}, u32[]{:S(2)}, u32[]{:S(2)}) collective-permute-start(f32[64,64]{1,0:T(8,128)S(1)} %slice.43), channel_id=1, source_target_pairs={{0,8},{1,9},{2,10},{3,11},{4,12},{5,13},{6,14},{7,15},{8,0},{9,1},... | collective-permute-start | bytes 49160 | tf_op jit(solution)/shard_map/ppermute | solution.py:523
  100.0 5.1 %collective-permute-start.9 = (f32[16,3072]{1,0:T(8,128)S(1)}, f32[16,3072]{1,0:T(8,128)S(1)}, u32[]{:S(2)}, u32[]{:S(2)}) collective-permute-start(f32[16,3072]{1,0:T(8,128)S(1)} %slice.47), channel_id=1, source_target_pairs={{0,4},{1,5},{2,6},{3,7},{4,0},{5,1},{6,2},{7,3},{8,12},{9,13},{10,... | collective-permute-start | bytes 589832 | tf_op jit(solution)/shard_map/ppermute | solution.py:523
  103.8 3.8 %collective-permute-start.7 = (f32[32,64]{1,0:T(8,128)S(1)}, f32[32,64]{1,0:T(8,128)S(1)}, u32[]{:S(2)}, u32[]{:S(2)}) collective-permute-start(f32[32,64]{1,0:T(8,128)S(1)} %slice.45), channel_id=1, source_target_pairs={{0,16},{1,17},{2,18},{3,19},{4,20},{5,21},{6,22},{7,23},{8,24},{9,... | collective-permute-start | bytes 24584 | tf_op jit(solution)/shard_map/ppermute | solution.py:523
  105.2 4.7 %collective-permute-start.10 = (f32[8,3072]{1,0:T(8,128)S(1)}, f32[8,3072]{1,0:T(8,128)S(1)}, u32[]{:S(2)}, u32[]{:S(2)}) collective-permute-start(f32[8,3072]{1,0:T(8,128)S(1)} %slice.49), channel_id=1, source_target_pairs={{0,8},{1,9},{2,10},{3,11},{4,12},{5,13},{6,14},{7,15},{8,0},{9,1},... | collective-permute-start | bytes 294920 | tf_op jit(solution)/shard_map/ppermute | solution.py:523

commit v2 on v1

v2 whole, which is shorter than its diff:
```python
import functools, math
import jax, jax.numpy as jnp, numpy as np
from jax import lax
from jax.experimental import pallas as pl
from jax.experimental.pallas import tpu as pltpu
from jax.sharding import PartitionSpec as P

CHAN = 3
LAYERS = 3
WEIGHT_VAR = 2.0
BIAS_VAR = 0.1
LANES = 128
SUBS = 8
TINY = 1e-30
F32 = jnp.float32


def arccos_coefficients(degree):
    nodes = 0.5 + 0.5 * np.cos(np.pi * (np.arange(400) + 0.5) / 400)
    target = np.arccos(1.0 - nodes) / np.sqrt(nodes)
    fit = np.polynomial.chebyshev.Chebyshev.fit(nodes, target, degree, domain=[0.0, 1.0])
    return [float(c) for c in fit.convert(kind=np.polynomial.Polynomial).coef]


COEFFS = arccos_coefficients(5)


def row_sums(ref, v, cols):
    f = [ref[j, v] for j in range(cols)]
    sub = lax.broadcasted_iota(jnp.int32, (SUBS, LANES), 0)
    above = jnp.where(sub > 0, pltpu.roll(f[-1], 1, 0), 0.0)
    below = jnp.where(sub < SUBS - 1, pltpu.roll(f[0], SUBS - 1, 0), 0.0)
    g = [above] + f + [below]
    out = []
    for j in range(0, cols, 2):
        mid = g[j + 1] + g[j + 2]
        out.append(g[j] + mid)
        out.append(mid + g[j + 3])
    return out


def sweep(ref, side, cols, emit, carry=(), chunk=32):
    def body(i, state):
        prev, cur, extra = state
        base = i * chunk
        for o in range(0, chunk, 2):
            nxt = row_sums(ref, base + o + 2, cols)
            nxt2 = row_sums(ref, base + o + 3, cols)
            mid = [a + b for a, b in zip(cur, nxt)]
            extra = emit(base + o, [a + b for a, b in zip(prev, mid)], extra)
            extra = emit(base + o + 1, [a + b for a, b in zip(mid, nxt2)], extra)
            prev, cur = nxt, nxt2
        return prev, cur, extra

    zero = [jnp.zeros((SUBS, LANES), F32) for _ in range(cols)]
    first = row_sums(ref, 1, cols)
    return lax.fori_loop(0, side // chunk, body, (zero, first, carry))[2]


def one_hot(index, count):
    return (lax.broadcasted_iota(jnp.int32, (index.shape[0], count), 1) == index).astype(F32)


def exact_dot(a, b, dims):
    return lax.dot_general(a, b, (dims, ((), ())), precision=lax.Precision.HIGHEST,
                           preferred_element_type=F32)


def fold_rows(tiles):
    sub = lax.broadcasted_iota(jnp.int32, (SUBS, LANES), 0)
    shift = SUBS // 2
    while shift:
        low = sub // shift % 2 == 0
        count = len(tiles) // 2
        tiles = [jnp.where(low, x + pltpu.roll(x, SUBS - shift, 0), y + pltpu.roll(y, shift, 0))
                 for x, y in zip(tiles[:count], tiles[count:])]
        shift //= 2
    return tiles[0]


def kernel_body(dims, call, *refs):
    gs, npos, side, col_count, per_row, part = dims
    mode_ref, a_refs, b_refs = refs[0], refs[1:3], refs[3:5]
    refs = refs[5:]
    outs = 2
    if call == 1:
        before_ref = refs[0]
        refs = refs[1:]
        outs = 3
    gl_ref, gr_ref = refs[:2]
    if call == 1:
        rest_ref = refs[2]
    x_ref, v_ref, kb_ref, sg_ref, f_ref, phi_ref, sin_ref, d_ref, r_ref, w_ref, kv_ref = refs[outs:]
    feat = CHAN * npos
    own_count = per_row * part
    members = gs // own_count
    tile_rows = 2 * members * part
    rows_of_dev = 2 * tile_rows
    width = per_row * tile_rows
    total_rows = 2 * members * rows_of_dev
    rs = gs // 2
    two = 2 * gs
    cols = side // SUBS
    tiles = gs * rs // LANES
    apt = LANES // rs
    blocks = npos // LANES
    per = LANES // SUBS
    diag = mode_ref[0] == 1
    member = mode_ref[1]
    own_row, their_row = mode_ref[6], mode_ref[7]
    lane = lax.broadcasted_iota(jnp.int32, (SUBS, LANES), 1)
    sub = lax.broadcasted_iota(jnp.int32, (SUBS, LANES), 0)

    def col_of(tile):
        return tile // side, tile % side + 1

    def places(col, half, axis, first, count):
        shape = (count, 1) if axis == 0 else (1, count)
        i = lax.broadcasted_iota(jnp.int32, shape, axis) + first
        k = i // part % per_row
        idx = (half * members + jnp.bitwise_xor(member, i // own_count)) * part + i % part
        blk = k * col_count + col
        return blk, blk * tile_rows + idx, k * tile_rows + idx

    def table_place(at_row, device):
        apart = jnp.bitwise_xor(at_row // rows_of_dev, device)
        return (apart % members * 2 + apart // members) * rows_of_dev + at_row % rows_of_dev

    def pack_table(rows):
        lines = []
        for q in range(rows.shape[0] // (2 * rows_of_dev)):
            first = q * 2 * rows_of_dev
            lines.append(jnp.concatenate([rows[first + t:first + t + own_count]
                                          for t in range(0, 2 * rows_of_dev, own_count)], 1))
        return jnp.concatenate(lines, 0)

    per_line = (a_refs[0].shape[1] - feat) // width

    def packet_place(at_row, device):
        apart = jnp.bitwise_xor(at_row // rows_of_dev, device)
        within = at_row % rows_of_dev
        line = apart % members * own_count + apart // members * (own_count // 2) + within // per_line
        return within % per_line * gs + line

    def packet_table(packets):
        rows = jnp.concatenate([ref[:, feat:].astype(F32) for ref in packets], 0)
        return jnp.concatenate([rows[:, i * width:(i + 1) * width] for i in range(per_line)], 0).astype(jnp.bfloat16)

    whole_a = (mode_ref[2], mode_ref[3])
    whole_b = (mode_ref[4], mode_ref[5])
    blk_a, row_a, at_a = places(*whole_a, 0, 0, gs)
    blk_al = places(*whole_a, 1, 0, gs)[0]
    blk_r, row_r, at_r = places(*whole_b, 0, call * rs, rs)
    blk_rl = places(*whole_b, 1, call * rs, rs)[0]
    ca = packet_table(a_refs)
    cb = packet_table(b_refs)
    if call == 0:
        blk_l, row_l, at_l = places(*whole_b, 0, 0, gs)
        blk_ll = places(*whole_b, 1, 0, gs)[0]
        table_l, device_l = cb, their_row
    else:
        blk_l, row_l, at_l, blk_ll = blk_a, row_a, at_a, blk_al
        table_l, device_l = ca, own_row
    hot_at_a, hot_at_r, hot_at_l = one_hot(at_a, width), one_hot(at_r, width), one_hot(at_l, width)
    keep_ar = (blk_a <= blk_rl).astype(F32)
    keep_ra = (blk_r <= blk_al).astype(F32)
    keep_ll = (blk_l <= blk_ll).astype(F32)

    def chosen(rows, table, columns):
        picked = jnp.dot(one_hot(rows, total_rows).astype(jnp.bfloat16), table, preferred_element_type=F32)
        return lax.dot_general(picked.astype(jnp.bfloat16), columns.astype(jnp.bfloat16),
                               (((1,), (1,)), ((), ())), preferred_element_type=F32)
    w_off = (chosen(packet_place(row_a, their_row), cb, hot_at_r) * keep_ar
             + (chosen(packet_place(row_r, own_row), ca, hot_at_a) * keep_ra).T)
    w_ll = chosen(packet_place(row_l, device_l), table_l, hot_at_l) * keep_ll
    w_sym = w_ll + w_ll.T
    eye = (lax.broadcasted_iota(jnp.int32, (gs, gs), 0) == lax.broadcasted_iota(jnp.int32, (gs, gs), 1))
    half_row = lax.broadcasted_iota(jnp.int32, (rs, rs), 0)
    half_col = lax.broadcasted_iota(jnp.int32, (rs, rs), 1)
    upper, lower = half_row < half_col, half_row > half_col
    w_diag = jnp.concatenate(
        [w_sym[:rs, rs:], jnp.where(upper, w_sym[rs:, rs:], jnp.where(lower, w_sym[:rs, :rs], 0.0))], 0)
    w_all = jnp.where(diag, w_diag, w_off)
    tile_hot = one_hot(lax.broadcasted_iota(jnp.int32, (gs, 1), 0) // apt, tiles)
    lane_hot = (lax.broadcasted_iota(jnp.int32, (rs, LANES), 1) // apt
                == lax.broadcasted_iota(jnp.int32, (rs, LANES), 0)).astype(F32)
    lane_match = (lax.broadcasted_iota(jnp.int32, (gs, LANES), 1) % apt
                  == lax.broadcasted_iota(jnp.int32, (gs, LANES), 0) % apt)
    w_lanes = jnp.where(lane_match, exact_dot(w_all, lane_hot, ((1,), (0,))), 0.0)
    w_rows = exact_dot(tile_hot, w_lanes, ((0,), (0,)))
    for k in range(tiles):
        w_ref[k] = w_rows[k:k + 1]
    self_l = jnp.sum(jnp.where(eye, w_ll, 0.0), 0, keepdims=True)
    self_row = jnp.concatenate([self_l, jnp.zeros((1, LANES - gs), F32)], 1)
    self_row = jnp.where(diag, self_row, 0.0)

    zeros = jnp.zeros((SUBS, LANES), F32)
    def image_rows(sl):
        left = jnp.concatenate([ref[:, sl].astype(F32) for ref in a_refs], 0)
        if call == 0:
            left = jnp.where(diag, jnp.concatenate([ref[:, sl].astype(F32) for ref in b_refs], 0), left)
        right = jnp.where(diag, left[rs:], b_refs[call][:, sl].astype(F32))
        return jnp.concatenate([left, right, jnp.zeros((two - gs - rs, LANES), F32)], 0)

    def to_fields(x, store):
        t = jnp.concatenate([x, x], 0).T
        return [store(i, t[i * SUBS:(i + 1) * SUBS]) for i in range(per)]

    for blk in range(blocks):
        total = 0.0
        for ch in range(CHAN):
            x = image_rows(pl.ds(ch * npos + blk * LANES, LANES))
            x_ref[ch, :, pl.ds(blk * LANES, LANES)] = x
            total = total + x * x

        def store(i, t):
            j, v = col_of(blk * per + i)
            f_ref[0, j, v] = t
        to_fields(total * (1.0 / CHAN), store)
    for j in range(cols):
        for v in (0, side + 1):
            for l in range(LAYERS):
                v_ref[l, j, v] = zeros
                phi_ref[l, j, v] = zeros
            f_ref[0, j, v] = zeros
            f_ref[1, j, v] = zeros

    def block_of(ref_at, blk):
        vals = []
        for t in range(per):
            j, v = col_of(blk * per + t)
            vals.append(ref_at(j, v))
        return jnp.concatenate(vals, 0)

    def var_emit(l, scale):
        def emit(v, sums, extra):
            for j in range(cols):
                v_ref[l, j, v + 1] = sums[j] * scale + BIAS_VAR
            return extra
        return emit
    sweep(f_ref.at[0], side, cols, var_emit(0, WEIGHT_VAR / 9.0))
    sweep(v_ref.at[0], side, cols, var_emit(1, 0.5 * WEIGHT_VAR / 9.0))
    sweep(v_ref.at[1], side, cols, var_emit(2, 0.5 * WEIGHT_VAR / 9.0))
    for l in range(LAYERS):
        for blk in range(blocks):
            t = block_of(lambda j, v: v_ref[l, j, v], blk).T[:two]
            sg_ref[l, :, pl.ds(blk * LANES, LANES)] = t * lax.rsqrt(t)
    totals = [zeros] * cols
    for j in range(cols):
        for v in range(side):
            totals[j] = totals[j] + v_ref[LAYERS - 1, j, v + 1]
    kself = jnp.sum(sum(totals), 0, keepdims=True) * (0.5 * WEIGHT_VAR / npos) + BIAS_VAR

    def clear(i, _):
        sl = pl.ds(pl.multiple_of(i * LANES, LANES), LANES)
        d_ref[:, :, sl] = jnp.zeros((LAYERS + CHAN, two, LANES), F32)
        return 0
    lax.fori_loop(0, blocks, clear, 0)

    def pair_tile(k, _):
        a0 = pl.multiple_of(k * apt, SUBS)
        masked = jnp.logical_and(diag, a0 >= rs)
        lo0 = pl.multiple_of(jnp.maximum(a0 - rs, 0), SUBS)

        def put(blk, t):
            half = blk * per
            j = half // side
            v = half % side + 1
            for i in range(per):
                f_ref[0, j, v + i] = t[i * SUBS:(i + 1) * SUBS]

        def cross_plain(blk, _):
            sl = pl.ds(pl.multiple_of(blk * LANES, LANES), LANES)
            rows = []
            left = [x_ref[ch, pl.ds(a0, SUBS), sl] for ch in range(CHAN)]
            for b in range(rs):
                acc = left[0] * x_ref[0, gs + b:gs + b + 1, sl]
                for ch in range(1, CHAN):
                    acc = acc + left[ch] * x_ref[ch, gs + b:gs + b + 1, sl]
                rows.append(acc)
            put(blk, jnp.concatenate(rows, 0).T)
            return 0

        def cross_masked(blk, _):
            sl = pl.ds(pl.multiple_of(blk * LANES, LANES), LANES)
            rows = []
            left = [x_ref[ch, pl.ds(a0, SUBS), sl] for ch in range(CHAN)]
            low = [x_ref[ch, pl.ds(lo0, SUBS), sl] for ch in range(CHAN)]
            for b in range(rs):
                first = sub + lo0 < b
                acc = 0.0
                for ch in range(CHAN):
                    acc = acc + jnp.where(first, left[ch] * x_ref[ch, gs + b:gs + b + 1, sl],
                                          low[ch] * x_ref[ch, b:b + 1, sl])
                rows.append(acc)
            put(blk, jnp.concatenate(rows, 0).T)
            return 0

        @pl.when(jnp.logical_not(masked))
        def _():
            lax.fori_loop(0, blocks, cross_plain, 0, unroll=True)

        @pl.when(masked)
        def _():
            lax.fori_loop(0, blocks, cross_masked, 0, unroll=True)

        ia, ib = lane % apt, lane // apt
        second = jnp.logical_and(masked, ib <= lo0 + ia)
        il = ia + jnp.where(second, lo0, a0)
        ir = ib + jnp.where(second, 0, gs)

        @pl.when(jnp.logical_or(k == 0, masked))
        def _():
            def gather(v, _):
                for l in range(LAYERS):
                    for j in range(cols):
                        kb_ref[l, j, v] = jnp.take_along_axis(v_ref[l, j, v + 1], ir, axis=1)
                return 0
            lax.fori_loop(0, side, gather, 0, unroll=4)

        def relu_emit(l, scale, dst):
            def emit(v, sums, extra):
                for j in range(cols):
                    k12 = sums[j] * scale + BIAS_VAR
                    prod = jnp.take_along_axis(v_ref[l, j, v + 1], il, axis=1) * kb_ref[l, j, v]
                    inv = lax.rsqrt(prod)
                    cosine = k12 * inv
                    w = jnp.maximum(1.0 - jnp.abs(cosine), TINY)
                    poly = COEFFS[-1]
                    for c in COEFFS[-2::-1]:
                        poly = poly * w + c
                    angle = (w * lax.rsqrt(w)) * poly
                    phi = jnp.where(cosine >= 0.0, math.pi - angle, angle)
                    rest = jnp.maximum(prod - k12 * k12, TINY)
                    root = rest * lax.rsqrt(rest)
                    value = root + phi * k12
                    phi_ref[l, j, v + 1] = phi
                    sin_ref[l, j, v + 1] = root * inv
                    if dst is None:
                        extra = extra + value
                    else:
                        f_ref[dst, j, v + 1] = value
                return extra
            return emit

        inner = WEIGHT_VAR / (9.0 * 2.0 * math.pi)
        sweep(f_ref.at[0], side, cols, relu_emit(0, WEIGHT_VAR / (9.0 * CHAN), 1))
        sweep(f_ref.at[1], side, cols, relu_emit(1, inner, 0))
        total = sweep(f_ref.at[0], side, cols, relu_emit(2, inner, None), zeros)
        kv_ref[k] = jnp.sum(total, 0, keepdims=True) * (WEIGHT_VAR / (2.0 * math.pi * npos)) + BIAS_VAR

        wrow = jnp.broadcast_to(w_ref[k] * (WEIGHT_VAR / npos), (SUBS, LANES))
        wscaled = wrow * inner

        def back_emit(l, dst, scaled):
            def emit(v, sums, extra):
                for j in range(cols):
                    grad = sums[j] * wscaled if scaled else sums[j]
                    sin_ref[l, j, v + 1] = sin_ref[l, j, v + 1] * grad
                    f_ref[dst, j, v + 1] = phi_ref[l, j, v + 1] * grad
                return extra
            return emit
        sweep(phi_ref.at[2], side, cols, back_emit(1, 0, True))
        sweep(f_ref.at[0], side, cols, back_emit(0, 1, False))

        def last_emit(v, sums, extra):
            for j in range(cols):
                f_ref[0, j, v + 1] = sums[j]
            return extra
        sweep(f_ref.at[1], side, cols, last_emit)

        def fold(is_masked):
            def body(blk, _):
                sl = pl.ds(pl.multiple_of(blk * LANES, LANES), LANES)
                half = blk * per
                j = half // side
                v = half % side + 1

                def turned(get):
                    t = jnp.concatenate([get(j, v + i) for i in range(per)], 0).T
                    return [t[b * SUBS:(b + 1) * SUBS] for b in range(rs)]

                for l in range(LAYERS + 1):
                    if l < LAYERS - 1:
                        h = turned(lambda j, v: sin_ref[l, j, v])
                    elif l == LAYERS - 1:
                        h = turned(lambda j, v: sin_ref[l, j, v] * wrow)
                    else:
                        h = turned(lambda j, v: f_ref[0, j, v])
                    terms = [(l, sg_ref, l)] if l < LAYERS else [(LAYERS + ch, x_ref, ch) for ch in range(CHAN)]
                    if is_masked:
                        first = [jnp.where(sub + lo0 < b, h[b], 0.0) for b in range(rs)]
                        other = [jnp.where(sub + lo0 > b, h[b], 0.0) for b in range(rs)]
                    for slot, src, at in terms:
                        left = src[at, pl.ds(a0, SUBS), sl]
                        total = 0.0
                        if is_masked:
                            low = src[at, pl.ds(lo0, SUBS), sl]
                            low_total = 0.0
                            for b in range(rs):
                                total = total + first[b] * src[at, gs + b:gs + b + 1, sl]
                                low_total = low_total + other[b] * src[at, b:b + 1, sl]
                                r_ref[k, slot, b, :, sl] = first[b] * left + other[b] * low
                            d_ref[slot, pl.ds(lo0, SUBS), sl] = d_ref[slot, pl.ds(lo0, SUBS), sl] + low_total
                        else:
                            for b in range(rs):
                                total = total + h[b] * src[at, gs + b:gs + b + 1, sl]
                                r_ref[k, slot, b, :, sl] = h[b] * left
                        d_ref[slot, pl.ds(a0, SUBS), sl] = d_ref[slot, pl.ds(a0, SUBS), sl] + total
                return 0
            lax.fori_loop(0, blocks, body, 0, unroll=True)

        @pl.when(jnp.logical_not(masked))
        def _():
            fold(False)

        @pl.when(masked)
        def _():
            fold(True)
        return 0

    lax.fori_loop(0, tiles, pair_tile, 0)

    def gather_right(low):
        def body(blk, _):
            sl = pl.ds(pl.multiple_of(blk * LANES, LANES), LANES)
            for slot in range(LAYERS + CHAN):
                for b0 in range(0, rs, SUBS):
                    sums = []
                    for b in range(b0, b0 + SUBS):
                        t = 0.0
                        for k in range(tiles):
                            if low is None:
                                t = t + r_ref[k, slot, b, :, sl]
                            elif k * apt < rs:
                                t = t if low else t + r_ref[k, slot, b, :, sl]
                            else:
                                i = sub + (k * apt - rs)
                                t = t + jnp.where(i > b if low else i < b, r_ref[k, slot, b, :, sl], 0.0)
                        sums.append(t)
                    at = pl.ds(b0 if low else gs + b0, SUBS)
                    d_ref[slot, at, sl] = d_ref[slot, at, sl] + fold_rows(sums)
            return 0
        lax.fori_loop(0, blocks, body, 0, unroll=2)

    @pl.when(jnp.logical_not(diag))
    def _():
        gather_right(None)

    @pl.when(diag)
    def _():
        gather_right(0)
        gather_right(1)

    step = WEIGHT_VAR / (9.0 * 2.0 * math.pi)
    selfw = self_row * (0.5 * WEIGHT_VAR / npos)
    for l in range(LAYERS):
        dest = phi_ref if l == LAYERS - 1 else sin_ref
        scale = (step if l == 0 else 1.0) / (4.0 * math.pi)
        for blk in range(blocks):
            def store(i, t):
                j, v = col_of(blk * per + i)
                t = t * (lax.rsqrt(v_ref[l, j, v]) * scale)
                dest[l, j, v] = t + selfw if l == LAYERS - 1 else t
            to_fields(d_ref[l, :, pl.ds(blk * LANES, LANES)], store)

    def chain_emit(l):
        def emit(v, sums, extra):
            for j in range(cols):
                phi_ref[l, j, v + 1] = sin_ref[l, j, v + 1] + sums[j] * (0.5 * WEIGHT_VAR / 9.0)
            return extra
        return emit
    sweep(phi_ref.at[2], side, cols, chain_emit(1))
    sweep(phi_ref.at[1], side, cols, chain_emit(0))

    def final_emit(v, sums, extra):
        for j in range(cols):
            f_ref[0, j, v + 1] = sums[j] * (WEIGHT_VAR / 9.0 * 2.0 / CHAN)
        return extra
    sweep(phi_ref.at[0], side, cols, final_emit)
    for blk in range(blocks):
        e = block_of(lambda j, v: f_ref[0, j, v], blk).T[:two]
        at = pl.ds(blk * LANES, LANES)
        for ch in range(CHAN):
            sl = pl.ds(ch * npos + blk * LANES, LANES)
            grad = d_ref[LAYERS + ch, :, at] * (step * step / CHAN) + x_ref[ch, :, at] * e
            right = grad[gs:gs + rs]
            left = jnp.concatenate([grad[:rs], grad[rs:gs] + jnp.where(diag, right, 0.0)], 0)
            if call == 0:
                gl_ref[:, sl] = left
                gr_ref[:, sl] = jnp.where(diag, left[:rs], right)
            else:
                before = before_ref[:, sl]
                gl_ref[:, sl] = left + jnp.where(diag, 0.0, before)
                gr_ref[:, sl] = jnp.where(diag, before[rs:], right)

    kv = jnp.concatenate([kv_ref[k] for k in range(tiles)], 0)
    values = exact_dot(jnp.where(lane_match, exact_dot(tile_hot, kv, ((1,), (0,))), 0.0), lane_hot, ((1,), (1,)))
    across, within = values[:rs], values[rs:]
    low_part, high_part = jnp.where(lower, within, 0.0), jnp.where(upper, within, 0.0)
    val_ll = jnp.concatenate([jnp.concatenate([low_part + low_part.T, across], 1),
                              jnp.concatenate([across.T, high_part + high_part.T], 1)], 0)
    val_ll = jnp.where(eye, kself[:, :gs], val_ll) * keep_ll

    def spread(rows, vals, columns):
        return exact_dot(one_hot(rows, total_rows), exact_dot(vals, columns, ((1,), (0,))), ((0,), (0,)))
    far_row = jnp.bitwise_xor(their_row, members // 2)
    rows_l, rows_a = table_place(row_l, far_row if call == 0 else own_row), table_place(row_a, far_row)
    diagonal = spread(rows_l, val_ll, hot_at_l)
    ours = spread(table_place(row_r, own_row), values.T * keep_ra, hot_at_a)
    theirs = spread(rows_a, values * keep_ar, hot_at_r)
    ours = jnp.where(diag, 0.0 if call == 0 else diagonal, ours)
    theirs = jnp.where(diag, diagonal if call == 0 else 0.0, theirs)
    ours = pack_table(ours)
    theirs = pack_table(theirs)
    if call == 0:
        gl_ref[:, feat:] = ours
        gr_ref[:, feat:] = jnp.concatenate([theirs[rs:], theirs[:rs]], 1)
    else:
        gl_ref[:, feat:] = ours + before_ref[:, feat:]
        gr_ref[:, feat:] = theirs[:rs]
        rest_ref[...] = theirs[rs:]


def pair_kernel(call, mode, packets, dims, before=()):
    gs, npos, side, col_count, per_row, part = dims
    cols = side // SUBS
    tiles = gs * gs // 2 // LANES
    terms = LAYERS + CHAN
    field = (cols, side + 2, SUBS, LANES)
    feat = CHAN * npos
    tile_rows = 2 * gs // per_row
    lines = 4 * tile_rows * per_row * tile_rows // (per_row * part)
    rs = gs // 2
    shapes = [(gs, feat + lines)] + ([(rs, feat + 2 * lines)] if call == 0 else [(rs, feat + lines), (rs, lines)])
    vm = pl.BlockSpec(memory_space=pltpu.VMEM)
    operands = (mode, *packets, *before)
    return pl.pallas_call(
        functools.partial(kernel_body, dims, call),
        out_shape=[jax.ShapeDtypeStruct(shape, F32) for shape in shapes],
        in_specs=[pl.BlockSpec(memory_space=pltpu.SMEM)] + [vm] * (len(operands) - 1),
        out_specs=[vm] * len(shapes),
        scratch_shapes=[
            pltpu.VMEM((CHAN, 2 * gs, npos), F32),
            pltpu.VMEM((LAYERS,) + field, F32),
            pltpu.VMEM((LAYERS, cols, side, SUBS, LANES), F32),
            pltpu.VMEM((LAYERS, 2 * gs, npos), F32),
            pltpu.VMEM((2,) + field, F32),
            pltpu.VMEM((LAYERS,) + field, F32),
            pltpu.VMEM((LAYERS,) + field, F32),
            pltpu.VMEM((terms, 2 * gs, npos), F32),
            pltpu.VMEM((tiles, terms, rs, SUBS, npos), F32),
            pltpu.VMEM((tiles, 1, LANES), F32),
            pltpu.VMEM((tiles, 1, LANES), F32),
        ],
        compiler_params=pltpu.CompilerParams(vmem_limit_bytes=40 * 1024 * 1024),
        cost_estimate=pl.CostEstimate(flops=2 * 10**10, bytes_accessed=5 * 10**7, transcendentals=10**6),
        name="pair_fields",
    )(*operands)


def exchange(x, rows, cols, target):
    perm = []
    for r in range(rows):
        for c in range(cols):
            tr, tc = target(r, c)
            perm.append((r * cols + c, tr * cols + tc))
    return lax.ppermute(x, ("row", "col"), perm)


def body(images, cotangent):
    rows = lax.axis_size("row")
    cols = lax.axis_size("col")
    row = lax.axis_index("row")
    col = lax.axis_index("col")
    per_row, _, part, feat = images.shape
    members = rows // 2
    groups = 2 * cols
    assert members == cols and members & (members - 1) == 0
    tile_rows = part * rows
    npos = feat // CHAN
    side = math.isqrt(npos)
    count = per_row * part
    gs = members * count
    own = images.reshape(count * CHAN, SUBS, npos // SUBS).transpose(0, 2, 1).reshape(count, feat)

    def partner_of(r, c, flip=0, turn=0):
        half, m = r // members, r % members
        other = (half * cols + c + 1 + m) % groups
        return (other // cols ^ turn) * members + (m ^ flip), other % cols

    holders = {}
    for r in range(rows):
        for c in range(cols):
            holders[partner_of(r, c)] = (r, c)

    def holder_of(r, c, flip=0, turn=0):
        return holders[r ^ flip ^ turn * members, c]

    def swap(x, bit):
        return exchange(x, rows, cols, lambda r, c: (r ^ bit, c))

    cot_own = cotangent.reshape(count // 2, -1)
    packet = jnp.concatenate([own, jnp.concatenate([cot_own, swap(cot_own, members)], 0)], 1)
    bits = []
    while 1 << len(bits) < members:
        bits.append(1 << len(bits))
    near, last = packet, bits[-1]
    for bit in bits[:-1]:
        near = jnp.concatenate([near, swap(near, bit)], 0)
    packets = [near, swap(near, last)]
    packets += [exchange(near, rows, cols, functools.partial(holder_of, flip=f)) for f in (0, last)]
    p_row, p_col = partner_of(row, col)
    member = row % members
    half = row // members
    diag = jnp.logical_and(member == members - 1, half == 1)
    mode = jnp.stack([diag.astype(jnp.int32), member, col, half, p_col, p_row // members, row, p_row])
    mode = mode.astype(jnp.int32)

    dims = (gs, npos, side, cols, per_row, part)
    half_count = gs // 2
    gl, gr = pair_kernel(0, mode, packets, dims)
    first = exchange(gr, rows, cols, functools.partial(partner_of, flip=last))
    gl, gr, rest = pair_kernel(1, mode, packets, dims, before=(gl,))
    lines = rest.shape[1]
    gr = exchange(gr, rows, cols, functools.partial(partner_of, flip=last))
    rest = exchange(rest, rows, cols, partner_of)
    met = swap(gl[half_count:] + first[:, :feat + lines], last)
    out = gl[:half_count] + met + gr + jnp.pad(first[:, feat + lines:] + rest, ((0, 0), (feat, 0)))
    for bit in bits[-2::-1]:
        n = out.shape[0] // 2
        out = out[:n] + swap(out[n:], bit)
    table = out[:, feat:]
    n = lines // 2
    table = table[:, :n] + swap(table[:, n:], members)
    width = per_row * tile_rows
    table = table.reshape(count, n // width, width).transpose(1, 0, 2)
    grads = out[:, :feat].reshape(count * CHAN, npos // SUBS, SUBS).transpose(0, 2, 1)
    return (table.reshape(2, tile_rows, per_row, 1, tile_rows),
            grads.reshape(per_row, 1, part, feat))


def solution(mesh):
    return jax.shard_map(
        body,
        mesh=mesh,
        in_specs=(P(None, "col", "row", None), P("row", None, None, "col", None)),
        out_specs=(P("row", None, None, "col", None), P(None, "col", "row", None)),
        check_vma=False,
    )
```

time: 111 us -> 80.4 us (0.72)
  Pallas kernels: 51.2 us -> 37.4 us
  waiting for transfers between devices: 27.8 us -> 17.4 us
  blocking collectives: 8.21 us -> 0 us
  local copies, waits for them, and re-layouts: 2.49 us -> 6.07 us
  starting transfers between devices: 20 us -> 18.5 us
    pallas_call x1 -> x2, Pallas kernels: 51.2 us -> 37.4 us  [pair_kernel(): pl.pallas_call(functools.partial(kernel_body, dims, call), out_shape=[jax...]
    ppermute x11, waiting for transfers between devices: 27.8 us -> 17.4 us  [exchange(): return lax.ppermute(x, ('row', 'col'), perm)]
    all_gather x1 -> x0, blocking collectives: 8.21 us -> none  [body(): lax.all_gather(cotangent.reshape(2 * tile_rows, per_row * tile_rows), 'ro...]
    reshape x2 -> x6, local copies, waits for them, and re-layouts: 0.91 us -> 4.05 us  [the longest x3 2.25 us: body(): images.reshape(count * CHAN, SUBS, npos // SUBS).transpose(0, 2, 1)]
    ppermute x11, starting transfers between devices: 20 us -> 18.5 us  [exchange(): return lax.ppermute(x, ('row', 'col'), perm)]
  transfers between devices with their start and end apart: 11 -> 11, of which waited for: 8 -> 9; matrix products, arithmetic and copies ran while one was open for 1% -> 5% of each run, Pallas kernels for 0% -> 23%
where the time goes in v2:
time: 80.4 us; the launch traced here: 80.2 us
  Pallas kernels  37.4 us (47%)
  starting transfers between devices  18.5 us (23%)
  waiting for transfers between devices  17.4 us (22%)
  local copies, waits for them, and re-layouts  6.07 us (8%)
    pallas_call x2, Pallas kernels, pair_kernel(): pl.pallas_call(functools.partial(kernel_body, dims, call), out_shape=[jax...  37.4 us
    ppermute x11, starting transfers between devices, exchange(): return lax.ppermute(x, ('row', 'col'), perm)  18.5 us
    ppermute x11, waiting for transfers between devices, exchange(): return lax.ppermute(x, ('row', 'col'), perm)  17.4 us
    reshape x3, local copies, waits for them, and re-layouts, body(): images.reshape(count * CHAN, SUBS, npos // SUBS).transpose(0, 2, 1)  2.25 us
  transfers between devices with their start and end apart: 11, of which 9 were waited for; matrix products, arithmetic and copies ran while one was open for 5% of the time, Pallas kernels for 23%

profile of v2, /device:TPU:0, one launch (start us, length us, event | category | flops | bytes accessed | tf_op | source)
XLA Modules:
  0.0 80.2 jit_solution(745429383820644407)
XLA Ops:
  0.6 0.9 %reshape.27 = bf16[4,512]{1,0:T(4,128)(2,1)S(1)} reshape(bf16[2,16,4,1,16]{4,2,3,1,0:T(4,128)(2,1)} %param.3) | data formatting | bytes 8192 | tf_op jit(solution)/shard_map/reshape | solution.py:603
  1.5 3.0 %collective-permute-start = (bf16[4,512]{1,0:T(4,128)(2,1)S(1)}, bf16[4,512]{1,0:T(4,128)(2,1)S(1)}, u32[]{:S(2)}, u32[]{:S(2)}) collective-permute-start(bf16[4,512]{1,0:T(4,128)(2,1)S(1)} %reshape.27), channel_id=1, source_target_pairs={{0,16},{1,17},{2,18},{3,19},{4,20},{5,21},{6,22},{7,23},{8,24},{9,... | collective-permute-start | bytes 12296 | tf_op jit(solution)/shard_map/ppermute | solution.py:568
  4.5 0.8 %reshape.25 = bf16[24,8,128]{2,1,0:T(8,128)(2,1)S(1)} reshape(bf16[4,1,2,3072]{3,2,1,0:T(2,128)(2,1)} %param.2) | data formatting | bytes 98304 | tf_op jit(solution)/shard_map/reshape | solution.py:585
  5.7 1.0 %reshape.26 = bf16[8,3072]{1,0:T(8,128)(2,1)S(1)} reshape(bf16[24,128,8]{2,1,0:T(8,128)(2,1)S(1)} %bitcast.15) | data formatting | bytes 98304 | tf_op jit(solution)/shard_map/reshape | solution.py:585
  6.9 1.2 %collective-permute-done.1 = bf16[8,3584]{1,0:T(8,128)(2,1)S(1)} collective-permute-done((bf16[8,3584]{1,0:T(8,128)(2,1)S(1)}, bf16[8,3584]{1,0:T(8,128)(2,1)S(1)}, u32[]{:S(2)}, u32[]{:S(2)}) %collective-permute-start.1) | collective-permute-done | bytes 57376 | tf_op jit(solution)/shard_map/ppermute | solution.py:568
  8.1 3.3 %collective-permute-start.4 = (bf16[16,3584]{1,0:T(8,128)(2,1)S(1)}, bf16[16,3584]{1,0:T(8,128)(2,1)S(1)}, u32[]{:S(2)}, u32[]{:S(2)}) collective-permute-start(bf16[16,3584]{1,0:T(8,128)(2,1)S(1)} %pad_maximum_fusion.refs_1_), channel_id=1, source_target_pairs={{0,25},{1,26},{2,27},{3,8},{4,28},{5,29},{6,30},{7,31},{8,19},{9,0... | collective-permute-start | bytes 344072 | tf_op jit(solution)/shard_map/ppermute | solution.py:568
  11.5 2.2 %collective-permute-start.3 = (bf16[16,3584]{1,0:T(8,128)(2,1)S(1)}, bf16[16,3584]{1,0:T(8,128)(2,1)S(1)}, u32[]{:S(2)}, u32[]{:S(2)}) collective-permute-start(bf16[16,3584]{1,0:T(8,128)(2,1)S(1)} %pad_maximum_fusion.refs_1_), channel_id=1, source_target_pairs={{0,19},{1,0},{2,1},{3,2},{4,22},{5,23},{6,4},{7,5},{8,25},{9,26},{... | collective-permute-start | bytes 344072 | tf_op jit(solution)/shard_map/ppermute | solution.py:568
  14.1 0.8 collective-permute-done.4.refs_4_
  14.9 2.2 %collective-permute-done.3.refs_3_ = bf16[16,3584]{1,0:T(8,128)(2,1)S(1)} collective-permute-done((bf16[16,3584]{1,0:T(8,128)(2,1)S(1)}, bf16[16,3584]{1,0:T(8,128)(2,1)S(1)}, u32[]{:S(2)}, u32[]{:S(2)}) %collective-permute-start.3) | collective-permute-done | bytes 114720 | tf_op jit(solution)/shard_map/ppermute | solution.py:568
  17.1 1.4 %collective-permute-done.2.refs_2_ = bf16[16,3584]{1,0:T(8,128)(2,1)S(1)} collective-permute-done((bf16[16,3584]{1,0:T(8,128)(2,1)S(1)}, bf16[16,3584]{1,0:T(8,128)(2,1)S(1)}, u32[]{:S(2)}, u32[]{:S(2)}) %collective-permute-start.2) | collective-permute-done | bytes 114720 | tf_op jit(solution)/shard_map/ppermute | solution.py:568
  18.5 18.7 %pair_fields.2 = (f32[32,3584]{1,0:T(8,128)S(1)}, f32[16,4096]{1,0:T(8,128)S(1)}) custom-call(s32[8]{0:T(128)S(1)} %stack.39.refs_0_, bf16[16,3584]{1,0:T(8,128)(2,1)S(1)} %pad_maximum_fusion.refs_1_, bf16[16,3584]{1,0:T(8,128)(2,1)S(1)} %collective-permute-done.2.refs_2_, bf16[16,3584]{1,0:T(8,128)(2,1)S(1)} %collective-permute-done.3.refs_3_, ...), custom_call_target="tpu_custom_call" | custom-call | flops 20000000000 | bytes 50000000 | tf_op jit(solution)/shard_map/pair_fields/pallas_call | solution.py:538
  37.2 1.6 %collective-permute-start.5 = (f32[16,4096]{1,0:T(8,128)S(1)}, f32[16,4096]{1,0:T(8,128)S(1)}, u32[]{:S(2)}, u32[]{:S(2)}) collective-permute-start(f32[16,4096]{1,0:T(8,128)S(1)} %get-tuple-element.9), channel_id=1, source_target_pairs={{0,9},{1,10},{2,11},{3,24},{4,14},{5,15},{6,28},{7,29},{8,3},{9,16... | collective-permute-start | bytes 786440 | tf_op jit(solution)/shard_map/ppermute | solution.py:568
  38.7 18.7 %pair_fields.3 = (f32[32,3584]{1,0:T(8,128)S(1)}, f32[16,3584]{1,0:T(8,128)S(1)}, f32[16,512]{1,0:T(8,128)S(1)}) custom-call(s32[8]{0:T(128)S(1)} %stack.39.refs_0_, bf16[16,3584]{1,0:T(8,128)(2,1)S(1)} %pad_maximum_fusion.refs_1_, bf16[16,3584]{1,0:T(8,128)(2,1)S(1)} %collective-permute-done.2.refs_2_, bf16[16,3584]{1,0:T(8,128)(2,1)S(1)} %collective-permute-done.3.refs_3_, ...), custom_call_target="tpu_custom_call" | custom-call | flops 20000000000 | bytes 50000000 | tf_op jit(solution)/shard_map/pair_fields/pallas_call | solution.py:538
  57.4 1.9 %collective-permute-start.8 = (f32[16,512]{1,0:T(8,128)S(1)}, f32[16,512]{1,0:T(8,128)S(1)}, u32[]{:S(2)}, u32[]{:S(2)}) collective-permute-start(f32[16,512]{1,0:T(8,128)S(1)} %get-tuple-element.11), channel_id=1, source_target_pairs={{0,1},{1,2},{2,3},{3,16},{4,6},{5,7},{6,20},{7,21},{8,11},{9,24},{... | collective-permute-start | bytes 98312 | tf_op jit(solution)/shard_map/ppermute | solution.py:568
  59.4 3.8 %collective-permute-start.7 = (f32[16,3584]{1,0:T(8,128)S(1)}, f32[16,3584]{1,0:T(8,128)S(1)}, u32[]{:S(2)}, u32[]{:S(2)}) collective-permute-start(f32[16,3584]{1,0:T(8,128)S(1)} %get-tuple-element.10), channel_id=1, source_target_pairs={{0,9},{1,10},{2,11},{3,24},{4,14},{5,15},{6,28},{7,29},{8,3},{9,16... | collective-permute-start | bytes 688136 | tf_op jit(solution)/shard_map/ppermute | solution.py:568
  63.4 0.9 %collective-permute-done.8 = f32[16,512]{1,0:T(8,128)S(1)} collective-permute-done((f32[16,512]{1,0:T(8,128)S(1)}, f32[16,512]{1,0:T(8,128)S(1)}, u32[]{:S(2)}, u32[]{:S(2)}) %collective-permute-start.8) | collective-permute-done | bytes 32800 | tf_op jit(solution)/shard_map/ppermute | solution.py:568
  64.3 4.6 %collective-permute-done.7 = f32[16,3584]{1,0:T(8,128)S(1)} collective-permute-done((f32[16,3584]{1,0:T(8,128)S(1)}, f32[16,3584]{1,0:T(8,128)S(1)}, u32[]{:S(2)}, u32[]{:S(2)}) %collective-permute-start.7) | collective-permute-done | bytes 229408 | tf_op jit(solution)/shard_map/ppermute | solution.py:568
  68.9 5.1 %collective-permute-done.6 = f32[16,3584]{1,0:T(8,128)S(1)} collective-permute-done((f32[16,3584]{1,0:T(8,128)S(1)}, f32[16,3584]{1,0:T(8,128)S(1)}, u32[]{:S(2)}, u32[]{:S(2)}) %collective-permute-start.6) | collective-permute-done | bytes 229408 | tf_op jit(solution)/shard_map/ppermute | solution.py:568
  74.1 0.5 collective-permute-start.9
  74.6 1.0 %collective-permute-done.9 = f32[8,3584]{1,0:T(8,128)S(1)} collective-permute-done((f32[8,3584]{1,0:T(8,128)S(1)}, f32[8,3584]{1,0:T(8,128)S(1)}, u32[]{:S(2)}, u32[]{:S(2)}) %collective-permute-start.9) | collective-permute-done | bytes 114720 | tf_op jit(solution)/shard_map/ppermute | solution.py:568
  75.6 1.5 %collective-permute-start.10 = (f32[8,256]{1,0:T(8,128)S(1)}, f32[8,256]{1,0:T(8,128)S(1)}, u32[]{:S(2)}, u32[]{:S(2)}) collective-permute-start(f32[8,256]{1,0:T(8,128)S(1)} %slice.44), channel_id=1, source_target_pairs={{0,16},{1,17},{2,18},{3,19},{4,20},{5,21},{6,22},{7,23},{8,24},{9,... | collective-permute-start | bytes 24584 | tf_op jit(solution)/shard_map/ppermute | solution.py:568
  77.1 0.9 %reshape.30 = f32[24,128,8]{2,1,0:T(8,128)S(1)} reshape(f32[8,3072]{1,0:T(8,128)S(1)} %slice.45) | data formatting | bytes 196608 | tf_op jit(solution)/shard_map/reshape | solution.py:638
  78.4 0.7 reshape.31
  79.4 0.8 reshape.29
  (21 shorter events, 2.0 us)
Async XLA Ops:
  1.5 5.3 %collective-permute-start = (bf16[4,512]{1,0:T(4,128)(2,1)S(1)}, bf16[4,512]{1,0:T(4,128)(2,1)S(1)}, u32[]{:S(2)}, u32[]{:S(2)}) collective-permute-start(bf16[4,512]{1,0:T(4,128)(2,1)S(1)} %reshape.27), channel_id=1, source_target_pairs={{0,16},{1,17},{2,18},{3,19},{4,20},{5,21},{6,22},{7,23},{8,24},{9,... | collective-permute-start | bytes 12296 | tf_op jit(solution)/shard_map/ppermute | solution.py:568
  6.8 1.3 %collective-permute-start.1 = (bf16[8,3584]{1,0:T(8,128)(2,1)S(1)}, bf16[8,3584]{1,0:T(8,128)(2,1)S(1)}, u32[]{:S(2)}, u32[]{:S(2)}) collective-permute-start(bf16[8,3584]{1,0:T(8,128)(2,1)S(1)} %maximum_maximum_fusion), channel_id=1, source_target_pairs={{0,4},{1,5},{2,6},{3,7},{4,0},{5,1},{6,2},{7,3},{8,12},{9,13},{10,... | collective-permute-start | bytes 172040 | tf_op jit(solution)/shard_map/ppermute | solution.py:568
  8.1 6.8 %collective-permute-start.4 = (bf16[16,3584]{1,0:T(8,128)(2,1)S(1)}, bf16[16,3584]{1,0:T(8,128)(2,1)S(1)}, u32[]{:S(2)}, u32[]{:S(2)}) collective-permute-start(bf16[16,3584]{1,0:T(8,128)(2,1)S(1)} %pad_maximum_fusion.refs_1_), channel_id=1, source_target_pairs={{0,25},{1,26},{2,27},{3,8},{4,28},{5,29},{6,30},{7,31},{8,19},{9,0... | collective-permute-start | bytes 344072 | tf_op jit(solution)/shard_map/ppermute | solution.py:568
  11.5 5.7 %collective-permute-start.3 = (bf16[16,3584]{1,0:T(8,128)(2,1)S(1)}, bf16[16,3584]{1,0:T(8,128)(2,1)S(1)}, u32[]{:S(2)}, u32[]{:S(2)}) collective-permute-start(bf16[16,3584]{1,0:T(8,128)(2,1)S(1)} %pad_maximum_fusion.refs_1_), channel_id=1, source_target_pairs={{0,19},{1,0},{2,1},{3,2},{4,22},{5,23},{6,4},{7,5},{8,25},{9,26},{... | collective-permute-start | bytes 344072 | tf_op jit(solution)/shard_map/ppermute | solution.py:568
  13.7 4.8 %collective-permute-start.2 = (bf16[16,3584]{1,0:T(8,128)(2,1)S(1)}, bf16[16,3584]{1,0:T(8,128)(2,1)S(1)}, u32[]{:S(2)}, u32[]{:S(2)}) collective-permute-start(bf16[16,3584]{1,0:T(8,128)(2,1)S(1)} %pad_maximum_fusion.refs_1_), channel_id=1, source_target_pairs={{0,8},{1,9},{2,10},{3,11},{4,12},{5,13},{6,14},{7,15},{8,0},{9,1},... | collective-permute-start | bytes 344072 | tf_op jit(solution)/shard_map/ppermute | solution.py:568
  37.2 25.9 %collective-permute-start.5 = (f32[16,4096]{1,0:T(8,128)S(1)}, f32[16,4096]{1,0:T(8,128)S(1)}, u32[]{:S(2)}, u32[]{:S(2)}) collective-permute-start(f32[16,4096]{1,0:T(8,128)S(1)} %get-tuple-element.9), channel_id=1, source_target_pairs={{0,9},{1,10},{2,11},{3,24},{4,14},{5,15},{6,28},{7,29},{8,3},{9,16... | collective-permute-start | bytes 786440 | tf_op jit(solution)/shard_map/ppermute | solution.py:568
  57.4 6.9 %collective-permute-start.8 = (f32[16,512]{1,0:T(8,128)S(1)}, f32[16,512]{1,0:T(8,128)S(1)}, u32[]{:S(2)}, u32[]{:S(2)}) collective-permute-start(f32[16,512]{1,0:T(8,128)S(1)} %get-tuple-element.11), channel_id=1, source_target_pairs={{0,1},{1,2},{2,3},{3,16},{4,6},{5,7},{6,20},{7,21},{8,11},{9,24},{... | collective-permute-start | bytes 98312 | tf_op jit(solution)/shard_map/ppermute | solution.py:568
  59.4 9.5 %collective-permute-start.7 = (f32[16,3584]{1,0:T(8,128)S(1)}, f32[16,3584]{1,0:T(8,128)S(1)}, u32[]{:S(2)}, u32[]{:S(2)}) collective-permute-start(f32[16,3584]{1,0:T(8,128)S(1)} %get-tuple-element.10), channel_id=1, source_target_pairs={{0,9},{1,10},{2,11},{3,24},{4,14},{5,15},{6,28},{7,29},{8,3},{9,16... | collective-permute-start | bytes 688136 | tf_op jit(solution)/shard_map/ppermute | solution.py:568
  63.2 10.8 %collective-permute-start.6 = (f32[16,3584]{1,0:T(8,128)S(1)}, f32[16,3584]{1,0:T(8,128)S(1)}, u32[]{:S(2)}, u32[]{:S(2)}) collective-permute-start(f32[16,3584]{1,0:T(8,128)S(1)} %slice_add_fusion), channel_id=1, source_target_pairs={{0,8},{1,9},{2,10},{3,11},{4,12},{5,13},{6,14},{7,15},{8,0},{9,1},... | collective-permute-start | bytes 688136 | tf_op jit(solution)/shard_map/ppermute | solution.py:568
  74.1 1.5 %collective-permute-start.9 = (f32[8,3584]{1,0:T(8,128)S(1)}, f32[8,3584]{1,0:T(8,128)S(1)}, u32[]{:S(2)}, u32[]{:S(2)}) collective-permute-start(f32[8,3584]{1,0:T(8,128)S(1)} %slice.42), channel_id=1, source_target_pairs={{0,4},{1,5},{2,6},{3,7},{4,0},{5,1},{6,2},{7,3},{8,12},{9,13},{10,... | collective-permute-start | bytes 344072 | tf_op jit(solution)/shard_map/ppermute | solution.py:568
  75.6 3.7 %collective-permute-start.10 = (f32[8,256]{1,0:T(8,128)S(1)}, f32[8,256]{1,0:T(8,128)S(1)}, u32[]{:S(2)}, u32[]{:S(2)}) collective-permute-start(f32[8,256]{1,0:T(8,128)S(1)} %slice.44), channel_id=1, source_target_pairs={{0,16},{1,17},{2,18},{3,19},{4,20},{5,21},{6,22},{7,23},{8,24},{9,... | collective-permute-start | bytes 24584 | tf_op jit(solution)/shard_map/ppermute | solution.py:568

commit v3 on v2

--- a/solution.py
+++ b/solution.py
@@ -61,9 +61,15 @@
     return (lax.broadcasted_iota(jnp.int32, (index.shape[0], count), 1) == index).astype(F32)
 
 
-def exact_dot(a, b, dims):
-    return lax.dot_general(a, b, (dims, ((), ())), precision=lax.Precision.HIGHEST,
-                           preferred_element_type=F32)
+def pick(hot, values, dims):
+    high = values.astype(jnp.bfloat16)
+    rest = values - high.astype(F32)
+    mid = rest.astype(jnp.bfloat16)
+    low = (rest - mid.astype(F32)).astype(jnp.bfloat16)
+    hot = hot.astype(jnp.bfloat16)
+    (left,), (right,) = dims
+    return lax.dot_general(jnp.concatenate([hot] * 3, left), jnp.concatenate([high, mid, low], right),
+                           (dims, ((), ())), preferred_element_type=F32)
 
 
 def fold_rows(tiles):
@@ -82,15 +88,11 @@
     gs, npos, side, col_count, per_row, part = dims
     mode_ref, a_refs, b_refs = refs[0], refs[1:3], refs[3:5]
     refs = refs[5:]
-    outs = 2
     if call == 1:
-        before_ref = refs[0]
-        refs = refs[1:]
-        outs = 3
-    gl_ref, gr_ref = refs[:2]
-    if call == 1:
-        rest_ref = refs[2]
-    x_ref, v_ref, kb_ref, sg_ref, f_ref, phi_ref, sin_ref, d_ref, r_ref, w_ref, kv_ref = refs[outs:]
+        before_l_ref, before_r_ref = refs[:2]
+        refs = refs[2:]
+    gl_ref, gr_ref, rest_ref = refs[:3]
+    x_ref, v_ref, kb_ref, sg_ref, f_ref, phi_ref, sin_ref, d_ref, r_ref, w_ref, kv_ref = refs[3:]
     feat = CHAN * npos
     own_count = per_row * part
     members = gs // own_count
@@ -105,7 +107,9 @@
     apt = LANES // rs
     blocks = npos // LANES
     per = LANES // SUBS
-    diag = mode_ref[0] == 1
+    flag = mode_ref[0] == 1
+    diag = flag if call == 1 else None
+    swapped = jnp.logical_and(flag, mode_ref[3] == 1)
     member = mode_ref[1]
     own_row, their_row = mode_ref[6], mode_ref[7]
     lane = lax.broadcasted_iota(jnp.int32, (SUBS, LANES), 1)
@@ -146,60 +150,67 @@
         rows = jnp.concatenate([ref[:, feat:].astype(F32) for ref in packets], 0)
         return jnp.concatenate([rows[:, i * width:(i + 1) * width] for i in range(per_line)], 0).astype(jnp.bfloat16)
 
-    whole_a = (mode_ref[2], mode_ref[3])
-    whole_b = (mode_ref[4], mode_ref[5])
-    blk_a, row_a, at_a = places(*whole_a, 0, 0, gs)
-    blk_al = places(*whole_a, 1, 0, gs)[0]
-    blk_r, row_r, at_r = places(*whole_b, 0, call * rs, rs)
-    blk_rl = places(*whole_b, 1, call * rs, rs)[0]
+    ours_at = (mode_ref[2], mode_ref[3], own_row)
+    theirs_at = (mode_ref[4], mode_ref[5], their_row)
     ca = packet_table(a_refs)
     cb = packet_table(b_refs)
     if call == 0:
-        blk_l, row_l, at_l = places(*whole_b, 0, 0, gs)
-        blk_ll = places(*whole_b, 1, 0, gs)[0]
-        table_l, device_l = cb, their_row
+        col_l, half_l, device_l = [jnp.where(swapped, t, o) for o, t in zip(ours_at, theirs_at)]
+        col_r, half_r, device_r = [jnp.where(swapped, o, t) for o, t in zip(ours_at, theirs_at)]
+        first_r = jnp.where(swapped, 0, rs)
+        table_l, table_r = jnp.where(swapped, cb, ca), jnp.where(swapped, ca, cb)
     else:
-        blk_l, row_l, at_l, blk_ll = blk_a, row_a, at_a, blk_al
-        table_l, device_l = ca, own_row
-    hot_at_a, hot_at_r, hot_at_l = one_hot(at_a, width), one_hot(at_r, width), one_hot(at_l, width)
-    keep_ar = (blk_a <= blk_rl).astype(F32)
-    keep_ra = (blk_r <= blk_al).astype(F32)
-    keep_ll = (blk_l <= blk_ll).astype(F32)
+        (col_l, half_l, device_l), (col_r, half_r, device_r) = ours_at, theirs_at
+        first_r = 0
+        table_l, table_r = ca, cb
+    blk_l, row_l, at_l = places(col_l, half_l, 0, 0, gs)
+    blk_ll = places(col_l, half_l, 1, 0, gs)[0]
+    blk_r, row_r, at_r = places(col_r, half_r, 0, first_r, rs)
+    blk_rl = places(col_r, half_r, 1, first_r, rs)[0]
+    hot_at_l, hot_at_r = one_hot(at_l, width), one_hot(at_r, width)
+    keep_lr = (blk_l <= blk_rl).astype(F32)
+    keep_rl = (blk_r <= blk_ll).astype(F32)
 
     def chosen(rows, table, columns):
-        picked = jnp.dot(one_hot(rows, total_rows).astype(jnp.bfloat16), table, preferred_element_type=F32)
+        picked = jnp.dot(one_hot(rows, total_rows).astype(jnp.bfloat16), table.astype(jnp.bfloat16),
+                         preferred_element_type=F32)
         return lax.dot_general(picked.astype(jnp.bfloat16), columns.astype(jnp.bfloat16),
                                (((1,), (1,)), ((), ())), preferred_element_type=F32)
-    w_off = (chosen(packet_place(row_a, their_row), cb, hot_at_r) * keep_ar
-             + (chosen(packet_place(row_r, own_row), ca, hot_at_a) * keep_ra).T)
-    w_ll = chosen(packet_place(row_l, device_l), table_l, hot_at_l) * keep_ll
-    w_sym = w_ll + w_ll.T
-    eye = (lax.broadcasted_iota(jnp.int32, (gs, gs), 0) == lax.broadcasted_iota(jnp.int32, (gs, gs), 1))
-    half_row = lax.broadcasted_iota(jnp.int32, (rs, rs), 0)
-    half_col = lax.broadcasted_iota(jnp.int32, (rs, rs), 1)
-    upper, lower = half_row < half_col, half_row > half_col
-    w_diag = jnp.concatenate(
-        [w_sym[:rs, rs:], jnp.where(upper, w_sym[rs:, rs:], jnp.where(lower, w_sym[:rs, :rs], 0.0))], 0)
-    w_all = jnp.where(diag, w_diag, w_off)
+    w_all = (chosen(packet_place(row_l, device_r), table_r, hot_at_r) * keep_lr
+             + (chosen(packet_place(row_r, device_l), table_l, hot_at_l) * keep_rl).T)
+    if call == 1:
+        keep_ll = (blk_l <= blk_ll).astype(F32)
+        w_ll = chosen(packet_place(row_l, device_l), table_l, hot_at_l) * keep_ll
+        w_sym = w_ll + w_ll.T
+        eye = (lax.broadcasted_iota(jnp.int32, (gs, gs), 0) == lax.broadcasted_iota(jnp.int32, (gs, gs), 1))
+        half_row = lax.broadcasted_iota(jnp.int32, (rs, rs), 0)
+        half_col = lax.broadcasted_iota(jnp.int32, (rs, rs), 1)
+        upper, lower = half_row < half_col, half_row > half_col
+        w_diag = jnp.concatenate(
+            [w_sym[:rs, rs:], jnp.where(upper, w_sym[rs:, rs:], jnp.where(lower, w_sym[:rs, :rs], 0.0))], 0)
+        w_all = jnp.where(diag, w_diag, w_all)
+        self_l = jnp.sum(jnp.where(eye, w_ll, 0.0), 0, keepdims=True)
+        self_row = jnp.concatenate([self_l, jnp.zeros((1, LANES - gs), F32)], 1)
+        self_row = jnp.where(diag, self_row, 0.0)
     tile_hot = one_hot(lax.broadcasted_iota(jnp.int32, (gs, 1), 0) // apt, tiles)
     lane_hot = (lax.broadcasted_iota(jnp.int32, (rs, LANES), 1) // apt
                 == lax.broadcasted_iota(jnp.int32, (rs, LANES), 0)).astype(F32)
     lane_match = (lax.broadcasted_iota(jnp.int32, (gs, LANES), 1) % apt
                   == lax.broadcasted_iota(jnp.int32, (gs, LANES), 0) % apt)
-    w_lanes = jnp.where(lane_match, exact_dot(w_all, lane_hot, ((1,), (0,))), 0.0)
-    w_rows = exact_dot(tile_hot, w_lanes, ((0,), (0,)))
+    w_lanes = jnp.where(lane_match, pick(lane_hot.T, w_all.T, ((1,), (0,))).T, 0.0)
+    w_rows = pick(tile_hot.T, w_lanes, ((1,), (0,)))
     for k in range(tiles):
         w_ref[k] = w_rows[k:k + 1]
-    self_l = jnp.sum(jnp.where(eye, w_ll, 0.0), 0, keepdims=True)
-    self_row = jnp.concatenate([self_l, jnp.zeros((1, LANES - gs), F32)], 1)
-    self_row = jnp.where(diag, self_row, 0.0)
-
     zeros = jnp.zeros((SUBS, LANES), F32)
     def image_rows(sl):
-        left = jnp.concatenate([ref[:, sl].astype(F32) for ref in a_refs], 0)
+        a = [ref[:, sl].astype(F32) for ref in a_refs]
         if call == 0:
-            left = jnp.where(diag, jnp.concatenate([ref[:, sl].astype(F32) for ref in b_refs], 0), left)
-        right = jnp.where(diag, left[rs:], b_refs[call][:, sl].astype(F32))
+            b = [ref[:, sl].astype(F32) for ref in b_refs]
+            left = jnp.where(swapped, jnp.concatenate(b, 0), jnp.concatenate(a, 0))
+            right = jnp.where(swapped, a[0], b[1])
+        else:
+            left = jnp.concatenate(a, 0)
+            right = jnp.where(diag, a[1], b_refs[0][:, sl].astype(F32))
         return jnp.concatenate([left, right, jnp.zeros((two - gs - rs, LANES), F32)], 0)
 
     def to_fields(x, store):
@@ -232,15 +243,20 @@
             vals.append(ref_at(j, v))
         return jnp.concatenate(vals, 0)
 
+    inner = WEIGHT_VAR / (9.0 * 2.0 * math.pi)
+    scales = [WEIGHT_VAR / (9.0 * CHAN)]
+    while len(scales) < LAYERS:
+        scales.append(scales[-1] * inner)
+
     def var_emit(l, scale):
         def emit(v, sums, extra):
             for j in range(cols):
-                v_ref[l, j, v + 1] = sums[j] * scale + BIAS_VAR
+                v_ref[l, j, v + 1] = sums[j] * (scale / scales[l]) + BIAS_VAR / scales[l]
             return extra
         return emit
     sweep(f_ref.at[0], side, cols, var_emit(0, WEIGHT_VAR / 9.0))
-    sweep(v_ref.at[0], side, cols, var_emit(1, 0.5 * WEIGHT_VAR / 9.0))
-    sweep(v_ref.at[1], side, cols, var_emit(2, 0.5 * WEIGHT_VAR / 9.0))
+    for l in range(1, LAYERS):
+        sweep(v_ref.at[l - 1], side, cols, var_emit(l, 0.5 * WEIGHT_VAR / 9.0 * scales[l - 1]))
     for l in range(LAYERS):
         for blk in range(blocks):
             t = block_of(lambda j, v: v_ref[l, j, v], blk).T[:two]
@@ -249,7 +265,7 @@
     for j in range(cols):
         for v in range(side):
             totals[j] = totals[j] + v_ref[LAYERS - 1, j, v + 1]
-    kself = jnp.sum(sum(totals), 0, keepdims=True) * (0.5 * WEIGHT_VAR / npos) + BIAS_VAR
+    kself = jnp.sum(sum(totals), 0, keepdims=True) * (0.5 * WEIGHT_VAR / npos * scales[-1]) + BIAS_VAR
 
     def clear(i, _):
         sl = pl.ds(pl.multiple_of(i * LANES, LANES), LANES)
@@ -259,7 +275,7 @@
 
     def pair_tile(k, _):
         a0 = pl.multiple_of(k * apt, SUBS)
-        masked = jnp.logical_and(diag, a0 >= rs)
+        masked = jnp.logical_and(diag, a0 >= rs) if call == 1 else False
         lo0 = pl.multiple_of(jnp.maximum(a0 - rs, 0), SUBS)
 
         def put(blk, t):
@@ -296,32 +312,42 @@
             put(blk, jnp.concatenate(rows, 0).T)
             return 0
 
-        @pl.when(jnp.logical_not(masked))
-        def _():
-            lax.fori_loop(0, blocks, cross_plain, 0, unroll=True)
-
-        @pl.when(masked)
-        def _():
-            lax.fori_loop(0, blocks, cross_masked, 0, unroll=True)
+        def either(plain, with_mask):
+            if call == 0:
+                plain()
+                return
+
+            @pl.when(jnp.logical_not(masked))
+            def _():
+                plain()
+
+            @pl.when(masked)
+            def _():
+                with_mask()
+
+        either(lambda: lax.fori_loop(0, blocks, cross_plain, 0, unroll=True),
+               lambda: lax.fori_loop(0, blocks, cross_masked, 0, unroll=True))
 
         ia, ib = lane % apt, lane // apt
-        second = jnp.logical_and(masked, ib <= lo0 + ia)
-        il = ia + jnp.where(second, lo0, a0)
-        ir = ib + jnp.where(second, 0, gs)
-
-        @pl.when(jnp.logical_or(k == 0, masked))
+        il, ir = ia + a0, ib + gs
+        if call == 1:
+            second = jnp.logical_and(masked, ib <= lo0 + ia)
+            il = jnp.where(second, ia + lo0, il)
+            ir = jnp.where(second, ib, ir)
+
+        @pl.when(jnp.logical_or(k == 0, masked) if call == 1 else k == 0)
         def _():
             def gather(v, _):
                 for l in range(LAYERS):
                     for j in range(cols):
                         kb_ref[l, j, v] = jnp.take_along_axis(v_ref[l, j, v + 1], ir, axis=1)
                 return 0
-            lax.fori_loop(0, side, gather, 0, unroll=4)
-
-        def relu_emit(l, scale, dst):
+            lax.fori_loop(0, side, gather, 0, unroll=True)
+
+        def relu_emit(l, dst):
             def emit(v, sums, extra):
                 for j in range(cols):
-                    k12 = sums[j] * scale + BIAS_VAR
+                    k12 = sums[j] + BIAS_VAR / scales[l]
                     prod = jnp.take_along_axis(v_ref[l, j, v + 1], il, axis=1) * kb_ref[l, j, v]
                     inv = lax.rsqrt(prod)
                     cosine = k12 * inv
@@ -343,11 +369,10 @@
                 return extra
             return emit
 
-        inner = WEIGHT_VAR / (9.0 * 2.0 * math.pi)
-        sweep(f_ref.at[0], side, cols, relu_emit(0, WEIGHT_VAR / (9.0 * CHAN), 1))
-        sweep(f_ref.at[1], side, cols, relu_emit(1, inner, 0))
-        total = sweep(f_ref.at[0], side, cols, relu_emit(2, inner, None), zeros)
-        kv_ref[k] = jnp.sum(total, 0, keepdims=True) * (WEIGHT_VAR / (2.0 * math.pi * npos)) + BIAS_VAR
+        sweep(f_ref.at[0], side, cols, relu_emit(0, 1))
+        sweep(f_ref.at[1], side, cols, relu_emit(1, 0))
+        total = sweep(f_ref.at[0], side, cols, relu_emit(2, None), zeros)
+        kv_ref[k] = jnp.sum(total, 0, keepdims=True) * (WEIGHT_VAR / (2.0 * math.pi * npos) * scales[-1]) + BIAS_VAR
 
         wrow = jnp.broadcast_to(w_ref[k] * (WEIGHT_VAR / npos), (SUBS, LANES))
         wscaled = wrow * inner
@@ -410,13 +435,7 @@
                 return 0
             lax.fori_loop(0, blocks, body, 0, unroll=True)
 
-        @pl.when(jnp.logical_not(masked))
-        def _():
-            fold(False)
-
-        @pl.when(masked)
-        def _():
-            fold(True)
+        either(lambda: fold(False), lambda: fold(True))
         return 0
 
     lax.fori_loop(0, tiles, pair_tile, 0)
@@ -441,22 +460,24 @@
                     at = pl.ds(b0 if low else gs + b0, SUBS)
                     d_ref[slot, at, sl] = d_ref[slot, at, sl] + fold_rows(sums)
             return 0
-        lax.fori_loop(0, blocks, body, 0, unroll=2)
-
-    @pl.when(jnp.logical_not(diag))
-    def _():
+        lax.fori_loop(0, blocks, body, 0, unroll=True)
+
+    if call == 0:
         gather_right(None)
-
-    @pl.when(diag)
-    def _():
-        gather_right(0)
-        gather_right(1)
-
-    step = WEIGHT_VAR / (9.0 * 2.0 * math.pi)
-    selfw = self_row * (0.5 * WEIGHT_VAR / npos)
+    else:
+        @pl.when(jnp.logical_not(diag))
+        def _():
+            gather_right(None)
+
+        @pl.when(diag)
+        def _():
+            gather_right(0)
+            gather_right(1)
+
+    selfw = self_row * (0.5 * WEIGHT_VAR / npos) if call == 1 else 0.0
     for l in range(LAYERS):
         dest = phi_ref if l == LAYERS - 1 else sin_ref
-        scale = (step if l == 0 else 1.0) / (4.0 * math.pi)
+        scale = (inner if l == 0 else 1.0) / (4.0 * math.pi)
         for blk in range(blocks):
             def store(i, t):
                 j, v = col_of(blk * per + i)
@@ -483,41 +504,43 @@
         at = pl.ds(blk * LANES, LANES)
         for ch in range(CHAN):
             sl = pl.ds(ch * npos + blk * LANES, LANES)
-            grad = d_ref[LAYERS + ch, :, at] * (step * step / CHAN) + x_ref[ch, :, at] * e
-            right = grad[gs:gs + rs]
-            left = jnp.concatenate([grad[:rs], grad[rs:gs] + jnp.where(diag, right, 0.0)], 0)
+            grad = d_ref[LAYERS + ch, :, at] * (inner * inner / CHAN) + x_ref[ch, :, at] * e
+            left, right = grad[:gs], grad[gs:gs + rs]
             if call == 0:
-                gl_ref[:, sl] = left
-                gr_ref[:, sl] = jnp.where(diag, left[:rs], right)
+                near = jnp.where(swapped, right, left[:rs])
+                gl_ref[:, sl] = jnp.concatenate([near, jnp.where(swapped, 0.0, left[rs:])], 0)
+                gr_ref[:, sl] = jnp.where(swapped, left[rs:], right)
+                rest_ref[:, sl] = jnp.where(swapped, left[:rs], 0.0)
             else:
-                before = before_ref[:, sl]
-                gl_ref[:, sl] = left + jnp.where(diag, 0.0, before)
-                gr_ref[:, sl] = jnp.where(diag, before[rs:], right)
+                far = left[rs:] + jnp.where(diag, right, 0.0)
+                gl_ref[:, sl] = jnp.concatenate([left[:rs], far], 0) + before_l_ref[:, sl]
+                gr_ref[:, sl] = jnp.where(diag, before_r_ref[:, sl], right)
 
     kv = jnp.concatenate([kv_ref[k] for k in range(tiles)], 0)
-    values = exact_dot(jnp.where(lane_match, exact_dot(tile_hot, kv, ((1,), (0,))), 0.0), lane_hot, ((1,), (1,)))
-    across, within = values[:rs], values[rs:]
-    low_part, high_part = jnp.where(lower, within, 0.0), jnp.where(upper, within, 0.0)
-    val_ll = jnp.concatenate([jnp.concatenate([low_part + low_part.T, across], 1),
-                              jnp.concatenate([across.T, high_part + high_part.T], 1)], 0)
-    val_ll = jnp.where(eye, kself[:, :gs], val_ll) * keep_ll
+    values = pick(lane_hot, jnp.where(lane_match, pick(tile_hot, kv, ((1,), (0,))), 0.0).T, ((1,), (0,))).T
 
     def spread(rows, vals, columns):
-        return exact_dot(one_hot(rows, total_rows), exact_dot(vals, columns, ((1,), (0,))), ((0,), (0,)))
-    far_row = jnp.bitwise_xor(their_row, members // 2)
-    rows_l, rows_a = table_place(row_l, far_row if call == 0 else own_row), table_place(row_a, far_row)
-    diagonal = spread(rows_l, val_ll, hot_at_l)
-    ours = spread(table_place(row_r, own_row), values.T * keep_ra, hot_at_a)
-    theirs = spread(rows_a, values * keep_ar, hot_at_r)
-    ours = jnp.where(diag, 0.0 if call == 0 else diagonal, ours)
-    theirs = jnp.where(diag, diagonal if call == 0 else 0.0, theirs)
-    ours = pack_table(ours)
-    theirs = pack_table(theirs)
+        placed = pick(columns.T, vals.T, ((1,), (0,))).T
+        return pick(one_hot(rows, total_rows).T, placed, ((1,), (0,)))
     if call == 0:
+        in_l = spread(table_place(row_r, device_l), values.T * keep_rl, hot_at_l)
+        in_r = spread(table_place(row_l, device_r), values * keep_lr, hot_at_r)
+        ours = pack_table(jnp.where(swapped, in_r, in_l))
+        theirs = pack_table(jnp.where(swapped, in_l, in_r))
         gl_ref[:, feat:] = ours
         gr_ref[:, feat:] = jnp.concatenate([theirs[rs:], theirs[:rs]], 1)
     else:
-        gl_ref[:, feat:] = ours + before_ref[:, feat:]
+        across, within = values[:rs], values[rs:]
+        low_part, high_part = jnp.where(lower, within, 0.0), jnp.where(upper, within, 0.0)
+        val_ll = jnp.concatenate([jnp.concatenate([low_part + low_part.T, across], 1),
+                                  jnp.concatenate([across.T, high_part + high_part.T], 1)], 0)
+        val_ll = jnp.where(eye, kself[:, :gs], val_ll) * keep_ll
+        rows = jnp.where(diag, table_place(row_l, device_l),
+                         jnp.concatenate([table_place(row_r, device_l)] * 2, 0))
+        vals = jnp.where(diag, val_ll, jnp.concatenate([values.T * keep_rl, jnp.zeros((rs, gs), F32)], 0))
+        ours = pack_table(spread(rows, vals, hot_at_l))
+        theirs = pack_table(jnp.where(diag, 0.0, spread(table_place(row_l, device_r), values * keep_lr, hot_at_r)))
+        gl_ref[:, feat:] = ours + before_l_ref[:, feat:]
         gr_ref[:, feat:] = theirs[:rs]
         rest_ref[...] = theirs[rs:]
 
@@ -532,7 +555,7 @@
     tile_rows = 2 * gs // per_row
     lines = 4 * tile_rows * per_row * tile_rows // (per_row * part)
     rs = gs // 2
-    shapes = [(gs, feat + lines)] + ([(rs, feat + 2 * lines)] if call == 0 else [(rs, feat + lines), (rs, lines)])
+    shapes = [(gs, feat + lines)] + ([(rs, feat + 2 * lines), (rs, feat)] if call == 0 else [(rs, feat + lines), (rs, lines)])
     vm = pl.BlockSpec(memory_space=pltpu.VMEM)
     operands = (mode, *packets, *before)
     return pl.pallas_call(
@@ -578,6 +601,7 @@
     groups = 2 * cols
     assert members == cols and members & (members - 1) == 0
     tile_rows = part * rows
+    last = members // 2
     npos = feat // CHAN
     side = math.isqrt(npos)
     count = per_row * part
@@ -586,7 +610,8 @@
 
     def partner_of(r, c, flip=0, turn=0):
         half, m = r // members, r % members
-        other = (half * cols + c + 1 + m) % groups
+        step = m // last * (2 * m + 1 - members) + (1 - m // last) * (2 * m + 2)
+        other = (half * cols + c + step) % groups
         return (other // cols ^ turn) * members + (m ^ flip), other % cols
 
     holders = {}
@@ -605,7 +630,7 @@
     bits = []
     while 1 << len(bits) < members:
         bits.append(1 << len(bits))
-    near, last = packet, bits[-1]
+    near = packet
     for bit in bits[:-1]:
         near = jnp.concatenate([near, swap(near, bit)], 0)
     packets = [near, swap(near, last)]
@@ -613,18 +638,18 @@
     p_row, p_col = partner_of(row, col)
     member = row % members
     half = row // members
-    diag = jnp.logical_and(member == members - 1, half == 1)
-    mode = jnp.stack([diag.astype(jnp.int32), member, col, half, p_col, p_row // members, row, p_row])
+    flag = member == last - 1
+    mode = jnp.stack([flag.astype(jnp.int32), member, col, half, p_col, p_row // members, row, p_row])
     mode = mode.astype(jnp.int32)
 
     dims = (gs, npos, side, cols, per_row, part)
     half_count = gs // 2
-    gl, gr = pair_kernel(0, mode, packets, dims)
-    first = exchange(gr, rows, cols, functools.partial(partner_of, flip=last))
-    gl, gr, rest = pair_kernel(1, mode, packets, dims, before=(gl,))
+    gl, gr, rest = pair_kernel(0, mode, packets, dims)
+    first = exchange(gr, rows, cols, partner_of)
+    gl, gr, rest = pair_kernel(1, mode, packets, dims, before=(gl, rest))
     lines = rest.shape[1]
-    gr = exchange(gr, rows, cols, functools.partial(partner_of, flip=last))
-    rest = exchange(rest, rows, cols, partner_of)
+    gr = exchange(gr, rows, cols, partner_of)
+    rest = exchange(rest, rows, cols, functools.partial(partner_of, flip=last))
     met = swap(gl[half_count:] + first[:, :feat + lines], last)
     out = gl[:half_count] + met + gr + jnp.pad(first[:, feat + lines:] + rest, ((0, 0), (feat, 0)))
     for bit in bits[-2::-1]:

time: 80.4 us -> 74.7 us (0.929)
  Pallas kernels: 37.4 us -> 35 us
  starting transfers between devices: 18.5 us -> 16.3 us
  waiting for transfers between devices: 17.4 us -> 16.2 us
    pallas_call x2, Pallas kernels: 37.4 us -> 35 us  [pair_kernel(): pl.pallas_call(functools.partial(kernel_body, dims, call), out_shape=[jax...]
    ppermute x11, starting transfers between devices: 18.5 us -> 16.3 us  [exchange(): return lax.ppermute(x, ('row', 'col'), perm)]
    ppermute x11, waiting for transfers between devices: 17.4 us -> 16.2 us  [exchange(): return lax.ppermute(x, ('row', 'col'), perm)]
  transfers between devices with their start and end apart: 11 -> 11, of which waited for: 9 -> 7; matrix products, arithmetic and copies ran while one was open for 5% -> 6% of each run, Pallas kernels for 23% -> 25%
where the time goes in v3:
time: 74.7 us; the launch traced here: 74.5 us
  Pallas kernels  35 us (47%)
  starting transfers between devices  16.3 us (22%)
  waiting for transfers between devices  16.2 us (22%)
  local copies, waits for them, and re-layouts  6.07 us (8%)
    pallas_call x2, Pallas kernels, pair_kernel(): pl.pallas_call(functools.partial(kernel_body, dims, call), out_shape=[jax...  35 us
    ppermute x11, starting transfers between devices, exchange(): return lax.ppermute(x, ('row', 'col'), perm)  16.3 us
    ppermute x11, waiting for transfers between devices, exchange(): return lax.ppermute(x, ('row', 'col'), perm)  16.2 us
    reshape x3, local copies, waits for them, and re-layouts, body(): images.reshape(count * CHAN, SUBS, npos // SUBS).transpose(0, 2, 1)  2.25 us
  transfers between devices with their start and end apart: 11, of which 7 were waited for; matrix products, arithmetic and copies ran while one was open for 6% of the time, Pallas kernels for 25%

profile of v3, /device:TPU:0, one launch (start us, length us, event | category | flops | bytes accessed | tf_op | source)
XLA Modules:
  0.0 74.5 jit_solution(11802984732901790285)
XLA Ops:
  0.6 0.9 %reshape.27 = bf16[4,512]{1,0:T(4,128)(2,1)S(1)} reshape(bf16[2,16,4,1,16]{4,2,3,1,0:T(4,128)(2,1)} %param.3) | data formatting | bytes 8192 | tf_op jit(solution)/shard_map/reshape | solution.py:628
  1.5 3.0 %collective-permute-start = (bf16[4,512]{1,0:T(4,128)(2,1)S(1)}, bf16[4,512]{1,0:T(4,128)(2,1)S(1)}, u32[]{:S(2)}, u32[]{:S(2)}) collective-permute-start(bf16[4,512]{1,0:T(4,128)(2,1)S(1)} %reshape.27), channel_id=1, source_target_pairs={{0,16},{1,17},{2,18},{3,19},{4,20},{5,21},{6,22},{7,23},{8,24},{9,... | collective-permute-start | bytes 12296 | tf_op jit(solution)/shard_map/ppermute | solution.py:591
  4.5 0.8 %reshape.25 = bf16[24,8,128]{2,1,0:T(8,128)(2,1)S(1)} reshape(bf16[4,1,2,3072]{3,2,1,0:T(2,128)(2,1)} %param.2) | data formatting | bytes 98304 | tf_op jit(solution)/shard_map/reshape | solution.py:609
  5.4 0.4 copy.9
  5.7 1.0 %reshape.26 = bf16[8,3072]{1,0:T(8,128)(2,1)S(1)} reshape(bf16[24,128,8]{2,1,0:T(8,128)(2,1)S(1)} %bitcast.15) | data formatting | bytes 98304 | tf_op jit(solution)/shard_map/reshape | solution.py:609
  6.9 1.2 %collective-permute-done.1 = bf16[8,3584]{1,0:T(8,128)(2,1)S(1)} collective-permute-done((bf16[8,3584]{1,0:T(8,128)(2,1)S(1)}, bf16[8,3584]{1,0:T(8,128)(2,1)S(1)}, u32[]{:S(2)}, u32[]{:S(2)}) %collective-permute-start.1) | collective-permute-done | bytes 57376 | tf_op jit(solution)/shard_map/ppermute | solution.py:591
  8.1 5.4 %collective-permute-start.4 = (bf16[16,3584]{1,0:T(8,128)(2,1)S(1)}, bf16[16,3584]{1,0:T(8,128)(2,1)S(1)}, u32[]{:S(2)}, u32[]{:S(2)}) collective-permute-start(bf16[16,3584]{1,0:T(8,128)(2,1)S(1)} %pad_maximum_fusion.refs_1_), channel_id=1, source_target_pairs={{0,27},{1,8},{2,9},{3,10},{4,29},{5,30},{6,31},{7,12},{8,18},{9,19... | collective-permute-start | bytes 344072 | tf_op jit(solution)/shard_map/ppermute | solution.py:591
  13.5 0.9 %collective-permute-start.2 = (bf16[16,3584]{1,0:T(8,128)(2,1)S(1)}, bf16[16,3584]{1,0:T(8,128)(2,1)S(1)}, u32[]{:S(2)}, u32[]{:S(2)}) collective-permute-start(bf16[16,3584]{1,0:T(8,128)(2,1)S(1)} %pad_maximum_fusion.refs_1_), channel_id=1, source_target_pairs={{0,8},{1,9},{2,10},{3,11},{4,12},{5,13},{6,14},{7,15},{8,0},{9,1},... | collective-permute-start | bytes 344072 | tf_op jit(solution)/shard_map/ppermute | solution.py:591
  14.4 2.9 %collective-permute-done.4.refs_4_ = bf16[16,3584]{1,0:T(8,128)(2,1)S(1)} collective-permute-done((bf16[16,3584]{1,0:T(8,128)(2,1)S(1)}, bf16[16,3584]{1,0:T(8,128)(2,1)S(1)}, u32[]{:S(2)}, u32[]{:S(2)}) %collective-permute-start.4) | collective-permute-done | bytes 114720 | tf_op jit(solution)/shard_map/ppermute | solution.py:591
  17.3 1.9 %collective-permute-done.3.refs_3_ = bf16[16,3584]{1,0:T(8,128)(2,1)S(1)} collective-permute-done((bf16[16,3584]{1,0:T(8,128)(2,1)S(1)}, bf16[16,3584]{1,0:T(8,128)(2,1)S(1)}, u32[]{:S(2)}, u32[]{:S(2)}) %collective-permute-start.3) | collective-permute-done | bytes 114720 | tf_op jit(solution)/shard_map/ppermute | solution.py:591
  19.2 16.6 %pair_fields.2 = (f32[32,3584]{1,0:T(8,128)S(1)}, f32[16,4096]{1,0:T(8,128)S(1)}, f32[16,3072]{1,0:T(8,128)S(1)}) custom-call(s32[8]{0:T(128)S(1)} %stack.39.refs_0_, bf16[16,3584]{1,0:T(8,128)(2,1)S(1)} %pad_maximum_fusion.refs_1_, bf16[16,3584]{1,0:T(8,128)(2,1)S(1)} %collective-permute-done.2.refs_2_, ...), custom_call_target="tpu_custom_call" | custom-call | flops 20000000000 | bytes 50000000 | tf_op jit(solution)/shard_map/pair_fields/pallas_call | solution.py:561
  35.8 2.3 %collective-permute-start.5 = (f32[16,4096]{1,0:T(8,128)S(1)}, f32[16,4096]{1,0:T(8,128)S(1)}, u32[]{:S(2)}, u32[]{:S(2)}) collective-permute-start(f32[16,4096]{1,0:T(8,128)S(1)} %get-tuple-element.11), channel_id=1, source_target_pairs={{0,2},{1,3},{2,16},{3,17},{4,20},{5,21},{6,22},{7,23},{8,9},{9,10}... | collective-permute-start | bytes 786440 | tf_op jit(solution)/shard_map/ppermute | solution.py:591
  38.0 18.4 %pair_fields.3 = (f32[32,3584]{1,0:T(8,128)S(1)}, f32[16,3584]{1,0:T(8,128)S(1)}, f32[16,512]{1,0:T(8,128)S(1)}) custom-call(s32[8]{0:T(128)S(1)} %stack.39.refs_0_, bf16[16,3584]{1,0:T(8,128)(2,1)S(1)} %pad_maximum_fusion.refs_1_, bf16[16,3584]{1,0:T(8,128)(2,1)S(1)} %collective-permute-done.2.refs_2_, bf16[16,3584]{1,0:T(8,128)(2,1)S(1)} %collective-permute-done.3.refs_3_, ...), custom_call_target="tpu_custom_call" | custom-call | flops 20000000000 | bytes 50000000 | tf_op jit(solution)/shard_map/pair_fields/pallas_call | solution.py:561
  56.4 1.7 %collective-permute-start.8 = (f32[16,512]{1,0:T(8,128)S(1)}, f32[16,512]{1,0:T(8,128)S(1)}, u32[]{:S(2)}, u32[]{:S(2)}) collective-permute-start(f32[16,512]{1,0:T(8,128)S(1)} %get-tuple-element.13), channel_id=1, source_target_pairs={{0,10},{1,11},{2,24},{3,25},{4,28},{5,29},{6,30},{7,31},{8,1},{9,2... | collective-permute-start | bytes 98312 | tf_op jit(solution)/shard_map/ppermute | solution.py:591
  58.5 1.8 %collective-permute-start.6 = (f32[16,3584]{1,0:T(8,128)S(1)}, f32[16,3584]{1,0:T(8,128)S(1)}, u32[]{:S(2)}, u32[]{:S(2)}) collective-permute-start(f32[16,3584]{1,0:T(8,128)S(1)} %slice_add_fusion), channel_id=1, source_target_pairs={{0,8},{1,9},{2,10},{3,11},{4,12},{5,13},{6,14},{7,15},{8,0},{9,1},... | collective-permute-start | bytes 688136 | tf_op jit(solution)/shard_map/ppermute | solution.py:591
  60.3 4.1 %collective-permute-done.8 = f32[16,512]{1,0:T(8,128)S(1)} collective-permute-done((f32[16,512]{1,0:T(8,128)S(1)}, f32[16,512]{1,0:T(8,128)S(1)}, u32[]{:S(2)}, u32[]{:S(2)}) %collective-permute-start.8) | collective-permute-done | bytes 32800 | tf_op jit(solution)/shard_map/ppermute | solution.py:591
  64.4 4.0 %collective-permute-done.7 = f32[16,3584]{1,0:T(8,128)S(1)} collective-permute-done((f32[16,3584]{1,0:T(8,128)S(1)}, f32[16,3584]{1,0:T(8,128)S(1)}, u32[]{:S(2)}, u32[]{:S(2)}) %collective-permute-start.7) | collective-permute-done | bytes 229408 | tf_op jit(solution)/shard_map/ppermute | solution.py:591
  68.6 1.3 %collective-permute-done.9 = f32[8,3584]{1,0:T(8,128)S(1)} collective-permute-done((f32[8,3584]{1,0:T(8,128)S(1)}, f32[8,3584]{1,0:T(8,128)S(1)}, u32[]{:S(2)}, u32[]{:S(2)}) %collective-permute-start.9) | collective-permute-done | bytes 114720 | tf_op jit(solution)/shard_map/ppermute | solution.py:591
  69.9 0.9 %collective-permute-start.10 = (f32[8,256]{1,0:T(8,128)S(1)}, f32[8,256]{1,0:T(8,128)S(1)}, u32[]{:S(2)}, u32[]{:S(2)}) collective-permute-start(f32[8,256]{1,0:T(8,128)S(1)} %slice.44), channel_id=1, source_target_pairs={{0,16},{1,17},{2,18},{3,19},{4,20},{5,21},{6,22},{7,23},{8,24},{9,... | collective-permute-start | bytes 24584 | tf_op jit(solution)/shard_map/ppermute | solution.py:591
  70.8 0.9 %reshape.30 = f32[24,128,8]{2,1,0:T(8,128)S(1)} reshape(f32[8,3072]{1,0:T(8,128)S(1)} %slice.45) | data formatting | bytes 196608 | tf_op jit(solution)/shard_map/reshape | solution.py:663
  71.6 0.4 copy.11
  72.1 0.7 reshape.31
  72.8 0.8 %collective-permute-done.10 = f32[8,256]{1,0:T(8,128)S(1)} collective-permute-done((f32[8,256]{1,0:T(8,128)S(1)}, f32[8,256]{1,0:T(8,128)S(1)}, u32[]{:S(2)}, u32[]{:S(2)}) %collective-permute-start.10) | collective-permute-done | bytes 8224 | tf_op jit(solution)/shard_map/ppermute | solution.py:591
  73.7 0.8 %reshape.29 = f32[2,16,4,1,16]{4,3,2,1,0:T(1,128)} reshape(f32[4,8,64]{2,1,0:T(8,128)S(1)} %copy.10) | data formatting | bytes 16384 | tf_op jit(solution)/shard_map/reshape | solution.py:664
  (21 shorter events, 0.8 us)
Async XLA Ops:
  1.5 5.3 %collective-permute-start = (bf16[4,512]{1,0:T(4,128)(2,1)S(1)}, bf16[4,512]{1,0:T(4,128)(2,1)S(1)}, u32[]{:S(2)}, u32[]{:S(2)}) collective-permute-start(bf16[4,512]{1,0:T(4,128)(2,1)S(1)} %reshape.27), channel_id=1, source_target_pairs={{0,16},{1,17},{2,18},{3,19},{4,20},{5,21},{6,22},{7,23},{8,24},{9,... | collective-permute-start | bytes 12296 | tf_op jit(solution)/shard_map/ppermute | solution.py:591
  6.8 1.3 %collective-permute-start.1 = (bf16[8,3584]{1,0:T(8,128)(2,1)S(1)}, bf16[8,3584]{1,0:T(8,128)(2,1)S(1)}, u32[]{:S(2)}, u32[]{:S(2)}) collective-permute-start(bf16[8,3584]{1,0:T(8,128)(2,1)S(1)} %maximum_maximum_fusion), channel_id=1, source_target_pairs={{0,4},{1,5},{2,6},{3,7},{4,0},{5,1},{6,2},{7,3},{8,12},{9,13},{10,... | collective-permute-start | bytes 172040 | tf_op jit(solution)/shard_map/ppermute | solution.py:591
  8.1 9.2 %collective-permute-start.4 = (bf16[16,3584]{1,0:T(8,128)(2,1)S(1)}, bf16[16,3584]{1,0:T(8,128)(2,1)S(1)}, u32[]{:S(2)}, u32[]{:S(2)}) collective-permute-start(bf16[16,3584]{1,0:T(8,128)(2,1)S(1)} %pad_maximum_fusion.refs_1_), channel_id=1, source_target_pairs={{0,27},{1,8},{2,9},{3,10},{4,29},{5,30},{6,31},{7,12},{8,18},{9,19... | collective-permute-start | bytes 344072 | tf_op jit(solution)/shard_map/ppermute | solution.py:591
  13.5 5.7 %collective-permute-start.3 = (bf16[16,3584]{1,0:T(8,128)(2,1)S(1)}, bf16[16,3584]{1,0:T(8,128)(2,1)S(1)}, u32[]{:S(2)}, u32[]{:S(2)}) collective-permute-start(bf16[16,3584]{1,0:T(8,128)(2,1)S(1)} %pad_maximum_fusion.refs_1_), channel_id=1, source_target_pairs={{0,18},{1,19},{2,0},{3,1},{4,20},{5,21},{6,22},{7,23},{8,27},{9,8}... | collective-permute-start | bytes 344072 | tf_op jit(solution)/shard_map/ppermute | solution.py:591
  13.5 5.7 %collective-permute-start.2 = (bf16[16,3584]{1,0:T(8,128)(2,1)S(1)}, bf16[16,3584]{1,0:T(8,128)(2,1)S(1)}, u32[]{:S(2)}, u32[]{:S(2)}) collective-permute-start(bf16[16,3584]{1,0:T(8,128)(2,1)S(1)} %pad_maximum_fusion.refs_1_), channel_id=1, source_target_pairs={{0,8},{1,9},{2,10},{3,11},{4,12},{5,13},{6,14},{7,15},{8,0},{9,1},... | collective-permute-start | bytes 344072 | tf_op jit(solution)/shard_map/ppermute | solution.py:591
  35.8 22.7 %collective-permute-start.5 = (f32[16,4096]{1,0:T(8,128)S(1)}, f32[16,4096]{1,0:T(8,128)S(1)}, u32[]{:S(2)}, u32[]{:S(2)}) collective-permute-start(f32[16,4096]{1,0:T(8,128)S(1)} %get-tuple-element.11), channel_id=1, source_target_pairs={{0,2},{1,3},{2,16},{3,17},{4,20},{5,21},{6,22},{7,23},{8,9},{9,10}... | collective-permute-start | bytes 786440 | tf_op jit(solution)/shard_map/ppermute | solution.py:591
  56.4 8.0 %collective-permute-start.8 = (f32[16,512]{1,0:T(8,128)S(1)}, f32[16,512]{1,0:T(8,128)S(1)}, u32[]{:S(2)}, u32[]{:S(2)}) collective-permute-start(f32[16,512]{1,0:T(8,128)S(1)} %get-tuple-element.13), channel_id=1, source_target_pairs={{0,10},{1,11},{2,24},{3,25},{4,28},{5,29},{6,30},{7,31},{8,1},{9,2... | collective-permute-start | bytes 98312 | tf_op jit(solution)/shard_map/ppermute | solution.py:591
  58.1 10.3 %collective-permute-start.7 = (f32[16,3584]{1,0:T(8,128)S(1)}, f32[16,3584]{1,0:T(8,128)S(1)}, u32[]{:S(2)}, u32[]{:S(2)}) collective-permute-start(f32[16,3584]{1,0:T(8,128)S(1)} %get-tuple-element.12), channel_id=1, source_target_pairs={{0,2},{1,3},{2,16},{3,17},{4,20},{5,21},{6,22},{7,23},{8,9},{9,10}... | collective-permute-start | bytes 688136 | tf_op jit(solution)/shard_map/ppermute | solution.py:591
  58.5 9.9 %collective-permute-start.6 = (f32[16,3584]{1,0:T(8,128)S(1)}, f32[16,3584]{1,0:T(8,128)S(1)}, u32[]{:S(2)}, u32[]{:S(2)}) collective-permute-start(f32[16,3584]{1,0:T(8,128)S(1)} %slice_add_fusion), channel_id=1, source_target_pairs={{0,8},{1,9},{2,10},{3,11},{4,12},{5,13},{6,14},{7,15},{8,0},{9,1},... | collective-permute-start | bytes 688136 | tf_op jit(solution)/shard_map/ppermute | solution.py:591
  68.5 1.4 %collective-permute-start.9 = (f32[8,3584]{1,0:T(8,128)S(1)}, f32[8,3584]{1,0:T(8,128)S(1)}, u32[]{:S(2)}, u32[]{:S(2)}) collective-permute-start(f32[8,3584]{1,0:T(8,128)S(1)} %slice.42), channel_id=1, source_target_pairs={{0,4},{1,5},{2,6},{3,7},{4,0},{5,1},{6,2},{7,3},{8,12},{9,13},{10,... | collective-permute-start | bytes 344072 | tf_op jit(solution)/shard_map/ppermute | solution.py:591
  69.9 3.7 %collective-permute-start.10 = (f32[8,256]{1,0:T(8,128)S(1)}, f32[8,256]{1,0:T(8,128)S(1)}, u32[]{:S(2)}, u32[]{:S(2)}) collective-permute-start(f32[8,256]{1,0:T(8,128)S(1)} %slice.44), channel_id=1, source_target_pairs={{0,16},{1,17},{2,18},{3,19},{4,20},{5,21},{6,22},{7,23},{8,24},{9,... | collective-permute-start | bytes 24584 | tf_op jit(solution)/shard_map/ppermute | solution.py:591

commit v4 on v3

--- a/solution.py
+++ b/solution.py
@@ -344,6 +344,8 @@
                 return 0
             lax.fori_loop(0, side, gather, 0, unroll=True)
 
+        parity = k % 2
+
         def relu_emit(l, dst):
             def emit(v, sums, extra):
                 for j in range(cols):
@@ -361,7 +363,7 @@
                     root = rest * lax.rsqrt(rest)
                     value = root + phi * k12
                     phi_ref[l, j, v + 1] = phi
-                    sin_ref[l, j, v + 1] = root * inv
+                    sin_ref[parity, l, j, v + 1] = root * inv
                     if dst is None:
                         extra = extra + value
                     else:
@@ -381,7 +383,7 @@
             def emit(v, sums, extra):
                 for j in range(cols):
                     grad = sums[j] * wscaled if scaled else sums[j]
-                    sin_ref[l, j, v + 1] = sin_ref[l, j, v + 1] * grad
+                    sin_ref[parity, l, j, v + 1] = sin_ref[parity, l, j, v + 1] * grad
                     f_ref[dst, j, v + 1] = phi_ref[l, j, v + 1] * grad
                 return extra
             return emit
@@ -390,9 +392,13 @@
 
         def last_emit(v, sums, extra):
             for j in range(cols):
-                f_ref[0, j, v + 1] = sums[j]
+                sin_ref[parity, LAYERS, j, v + 1] = sums[j]
             return extra
         sweep(f_ref.at[1], side, cols, last_emit)
+
+        starts = [pl.multiple_of(a0 - apt, SUBS), a0]
+        lows = [pl.multiple_of(jnp.maximum(a0 - apt - rs, 0), SUBS), lo0]
+        wrows = [jnp.broadcast_to(w_ref[jnp.maximum(k - 1, 0)] * (WEIGHT_VAR / npos), (SUBS, LANES)), wrow]
 
         def fold(is_masked):
             def body(blk, _):
@@ -401,41 +407,52 @@
                 j = half // side
                 v = half % side + 1
 
-                def turned(get):
-                    t = jnp.concatenate([get(j, v + i) for i in range(per)], 0).T
-                    return [t[b * SUBS:(b + 1) * SUBS] for b in range(rs)]
+                def turned(t, l):
+                    rows = [sin_ref[t, l, j, v + i] for i in range(per)]
+                    if l == LAYERS - 1:
+                        rows = [row * wrows[t] for row in rows]
+                    h = jnp.concatenate(rows, 0).T
+                    return [h[b * SUBS:(b + 1) * SUBS] for b in range(rs)]
 
                 for l in range(LAYERS + 1):
-                    if l < LAYERS - 1:
-                        h = turned(lambda j, v: sin_ref[l, j, v])
-                    elif l == LAYERS - 1:
-                        h = turned(lambda j, v: sin_ref[l, j, v] * wrow)
-                    else:
-                        h = turned(lambda j, v: f_ref[0, j, v])
+                    h = [turned(t, l) for t in range(2)]
                     terms = [(l, sg_ref, l)] if l < LAYERS else [(LAYERS + ch, x_ref, ch) for ch in range(CHAN)]
-                    if is_masked:
-                        first = [jnp.where(sub + lo0 < b, h[b], 0.0) for b in range(rs)]
-                        other = [jnp.where(sub + lo0 > b, h[b], 0.0) for b in range(rs)]
                     for slot, src, at in terms:
-                        left = src[at, pl.ds(a0, SUBS), sl]
-                        total = 0.0
+                        left = [src[at, pl.ds(start, SUBS), sl] for start in starts]
+                        totals = [0.0, 0.0]
                         if is_masked:
-                            low = src[at, pl.ds(lo0, SUBS), sl]
-                            low_total = 0.0
-                            for b in range(rs):
-                                total = total + first[b] * src[at, gs + b:gs + b + 1, sl]
-                                low_total = low_total + other[b] * src[at, b:b + 1, sl]
-                                r_ref[k, slot, b, :, sl] = first[b] * left + other[b] * low
-                            d_ref[slot, pl.ds(lo0, SUBS), sl] = d_ref[slot, pl.ds(lo0, SUBS), sl] + low_total
+                            for t in range(2):
+                                i = sub + t * apt
+                                low = src[at, pl.ds(lows[t], SUBS), sl]
+                                low_total = 0.0
+                                for b in range(rs):
+                                    terms_b = []
+                                    if b > t * apt:
+                                        first = h[t][b] if b >= (t + 1) * apt else jnp.where(i < b, h[t][b], 0.0)
+                                        totals[t] = totals[t] + first * src[at, gs + b:gs + b + 1, sl]
+                                        terms_b.append(first * left[t])
+                                    if b < (t + 1) * apt - 1:
+                                        other = h[t][b] if b < t * apt else jnp.where(i > b, h[t][b], 0.0)
+                                        low_total = low_total + other * src[at, b:b + 1, sl]
+                                        terms_b.append(other * low)
+                                    r_ref[1 + t, slot, b, :, sl] = sum(terms_b)
+                                at_rows = pl.ds(lows[t], SUBS)
+                                d_ref[slot, at_rows, sl] = d_ref[slot, at_rows, sl] + low_total
                         else:
                             for b in range(rs):
-                                total = total + h[b] * src[at, gs + b:gs + b + 1, sl]
-                                r_ref[k, slot, b, :, sl] = h[b] * left
-                        d_ref[slot, pl.ds(a0, SUBS), sl] = d_ref[slot, pl.ds(a0, SUBS), sl] + total
+                                right = src[at, gs + b:gs + b + 1, sl]
+                                for t in range(2):
+                                    totals[t] = totals[t] + h[t][b] * right
+                                r_ref[k // 2, slot, b, :, sl] = h[0][b] * left[0] + h[1][b] * left[1]
+                        for t in range(2):
+                            at_rows = pl.ds(starts[t], SUBS)
+                            d_ref[slot, at_rows, sl] = d_ref[slot, at_rows, sl] + totals[t]
                 return 0
             lax.fori_loop(0, blocks, body, 0, unroll=True)
 
-        either(lambda: fold(False), lambda: fold(True))
+        @pl.when(parity == 1)
+        def _():
+            either(lambda: fold(False), lambda: fold(True))
         return 0
 
     lax.fori_loop(0, tiles, pair_tile, 0)
@@ -447,15 +464,17 @@
                 for b0 in range(0, rs, SUBS):
                     sums = []
                     for b in range(b0, b0 + SUBS):
-                        t = 0.0
-                        for k in range(tiles):
-                            if low is None:
-                                t = t + r_ref[k, slot, b, :, sl]
-                            elif k * apt < rs:
-                                t = t if low else t + r_ref[k, slot, b, :, sl]
-                            else:
-                                i = sub + (k * apt - rs)
-                                t = t + jnp.where(i > b if low else i < b, r_ref[k, slot, b, :, sl], 0.0)
+                        if low is None:
+                            t = r_ref[0, slot, b, :, sl] + r_ref[1, slot, b, :, sl]
+                        else:
+                            t = 0.0 if low else r_ref[0, slot, b, :, sl]
+                            for n in range(2):
+                                part = r_ref[1 + n, slot, b, :, sl]
+                                if n * apt <= b < (n + 1) * apt:
+                                    i = sub + n * apt
+                                    t = t + jnp.where(i > b if low else i < b, part, 0.0)
+                                elif (b < n * apt) == bool(low):
+                                    t = t + part
                         sums.append(t)
                     at = pl.ds(b0 if low else gs + b0, SUBS)
                     d_ref[slot, at, sl] = d_ref[slot, at, sl] + fold_rows(sums)
@@ -476,7 +495,7 @@
 
     selfw = self_row * (0.5 * WEIGHT_VAR / npos) if call == 1 else 0.0
     for l in range(LAYERS):
-        dest = phi_ref if l == LAYERS - 1 else sin_ref
+        dest = phi_ref if l == LAYERS - 1 else sin_ref.at[0]
         scale = (inner if l == 0 else 1.0) / (4.0 * math.pi)
         for blk in range(blocks):
             def store(i, t):
@@ -488,7 +507,7 @@
     def chain_emit(l):
         def emit(v, sums, extra):
             for j in range(cols):
-                phi_ref[l, j, v + 1] = sin_ref[l, j, v + 1] + sums[j] * (0.5 * WEIGHT_VAR / 9.0)
+                phi_ref[l, j, v + 1] = sin_ref[0, l, j, v + 1] + sums[j] * (0.5 * WEIGHT_VAR / 9.0)
             return extra
         return emit
     sweep(phi_ref.at[2], side, cols, chain_emit(1))
@@ -570,9 +589,9 @@
             pltpu.VMEM((LAYERS, 2 * gs, npos), F32),
             pltpu.VMEM((2,) + field, F32),
             pltpu.VMEM((LAYERS,) + field, F32),
-            pltpu.VMEM((LAYERS,) + field, F32),
+            pltpu.VMEM((2, LAYERS + 1) + field, F32),
             pltpu.VMEM((terms, 2 * gs, npos), F32),
-            pltpu.VMEM((tiles, terms, rs, SUBS, npos), F32),
+            pltpu.VMEM((3, terms, rs, SUBS, npos), F32),
             pltpu.VMEM((tiles, 1, LANES), F32),
             pltpu.VMEM((tiles, 1, LANES), F32),
         ],

time: 74.7 us -> 72.9 us (0.976)
  Pallas kernels: 35 us -> 33.2 us
    pallas_call x2, Pallas kernels: 35 us -> 33.2 us  [pair_kernel(): pl.pallas_call(functools.partial(kernel_body, dims, call), out_shape=[jax...]
  transfers between devices with their start and end apart: 11 -> 11, of which waited for: 7 -> 7; matrix products, arithmetic and copies ran while one was open for 6% -> 6% of each run, Pallas kernels for 25% -> 24%
where the time goes in v4:
time: 72.9 us; the launch traced here: 72.7 us
  Pallas kernels  33.2 us (46%)
  starting transfers between devices  16.3 us (22%)
  waiting for transfers between devices  16.2 us (22%)
  local copies, waits for them, and re-layouts  6.07 us (8%)
  between operations  0.73 us (1%)
    pallas_call x2, Pallas kernels, pair_kernel(): pl.pallas_call(functools.partial(kernel_body, dims, call), out_shape=[jax...  33.2 us
    ppermute x11, starting transfers between devices, exchange(): return lax.ppermute(x, ('row', 'col'), perm)  16.3 us
    ppermute x11, waiting for transfers between devices, exchange(): return lax.ppermute(x, ('row', 'col'), perm)  16.2 us
    reshape x3, local copies, waits for them, and re-layouts, body(): images.reshape(count * CHAN, SUBS, npos // SUBS).transpose(0, 2, 1)  2.25 us
  transfers between devices with their start and end apart: 11, of which 7 were waited for; matrix products, arithmetic and copies ran while one was open for 6% of the time, Pallas kernels for 24%

profile of v4, /device:TPU:0, one launch (start us, length us, event | category | flops | bytes accessed | tf_op | source)
XLA Modules:
  0.0 72.7 jit_solution(2845909600017632456)
XLA Ops:
  0.6 0.9 %reshape.27 = bf16[4,512]{1,0:T(4,128)(2,1)S(1)} reshape(bf16[2,16,4,1,16]{4,2,3,1,0:T(4,128)(2,1)} %param.3) | data formatting | bytes 8192 | tf_op jit(solution)/shard_map/reshape | solution.py:647
  1.5 3.0 %collective-permute-start = (bf16[4,512]{1,0:T(4,128)(2,1)S(1)}, bf16[4,512]{1,0:T(4,128)(2,1)S(1)}, u32[]{:S(2)}, u32[]{:S(2)}) collective-permute-start(bf16[4,512]{1,0:T(4,128)(2,1)S(1)} %reshape.27), channel_id=1, source_target_pairs={{0,16},{1,17},{2,18},{3,19},{4,20},{5,21},{6,22},{7,23},{8,24},{9,... | collective-permute-start | bytes 12296 | tf_op jit(solution)/shard_map/ppermute | solution.py:610
  4.5 0.8 %reshape.25 = bf16[24,8,128]{2,1,0:T(8,128)(2,1)S(1)} reshape(bf16[4,1,2,3072]{3,2,1,0:T(2,128)(2,1)} %param.2) | data formatting | bytes 98304 | tf_op jit(solution)/shard_map/reshape | solution.py:628
  5.4 0.4 copy.9
  5.7 1.0 %reshape.26 = bf16[8,3072]{1,0:T(8,128)(2,1)S(1)} reshape(bf16[24,128,8]{2,1,0:T(8,128)(2,1)S(1)} %bitcast.15) | data formatting | bytes 98304 | tf_op jit(solution)/shard_map/reshape | solution.py:628
  6.9 1.2 %collective-permute-done.1 = bf16[8,3584]{1,0:T(8,128)(2,1)S(1)} collective-permute-done((bf16[8,3584]{1,0:T(8,128)(2,1)S(1)}, bf16[8,3584]{1,0:T(8,128)(2,1)S(1)}, u32[]{:S(2)}, u32[]{:S(2)}) %collective-permute-start.1) | collective-permute-done | bytes 57376 | tf_op jit(solution)/shard_map/ppermute | solution.py:610
  8.1 5.4 %collective-permute-start.4 = (bf16[16,3584]{1,0:T(8,128)(2,1)S(1)}, bf16[16,3584]{1,0:T(8,128)(2,1)S(1)}, u32[]{:S(2)}, u32[]{:S(2)}) collective-permute-start(bf16[16,3584]{1,0:T(8,128)(2,1)S(1)} %pad_maximum_fusion.refs_1_), channel_id=1, source_target_pairs={{0,27},{1,8},{2,9},{3,10},{4,29},{5,30},{6,31},{7,12},{8,18},{9,19... | collective-permute-start | bytes 344072 | tf_op jit(solution)/shard_map/ppermute | solution.py:610
  13.5 0.9 %collective-permute-start.2 = (bf16[16,3584]{1,0:T(8,128)(2,1)S(1)}, bf16[16,3584]{1,0:T(8,128)(2,1)S(1)}, u32[]{:S(2)}, u32[]{:S(2)}) collective-permute-start(bf16[16,3584]{1,0:T(8,128)(2,1)S(1)} %pad_maximum_fusion.refs_1_), channel_id=1, source_target_pairs={{0,8},{1,9},{2,10},{3,11},{4,12},{5,13},{6,14},{7,15},{8,0},{9,1},... | collective-permute-start | bytes 344072 | tf_op jit(solution)/shard_map/ppermute | solution.py:610
  14.4 2.9 %collective-permute-done.4.refs_4_ = bf16[16,3584]{1,0:T(8,128)(2,1)S(1)} collective-permute-done((bf16[16,3584]{1,0:T(8,128)(2,1)S(1)}, bf16[16,3584]{1,0:T(8,128)(2,1)S(1)}, u32[]{:S(2)}, u32[]{:S(2)}) %collective-permute-start.4) | collective-permute-done | bytes 114720 | tf_op jit(solution)/shard_map/ppermute | solution.py:610
  17.3 1.9 %collective-permute-done.3.refs_3_ = bf16[16,3584]{1,0:T(8,128)(2,1)S(1)} collective-permute-done((bf16[16,3584]{1,0:T(8,128)(2,1)S(1)}, bf16[16,3584]{1,0:T(8,128)(2,1)S(1)}, u32[]{:S(2)}, u32[]{:S(2)}) %collective-permute-start.3) | collective-permute-done | bytes 114720 | tf_op jit(solution)/shard_map/ppermute | solution.py:610
  19.2 16.0 %pair_fields.2 = (f32[32,3584]{1,0:T(8,128)S(1)}, f32[16,4096]{1,0:T(8,128)S(1)}, f32[16,3072]{1,0:T(8,128)S(1)}) custom-call(s32[8]{0:T(128)S(1)} %stack.39.refs_0_, bf16[16,3584]{1,0:T(8,128)(2,1)S(1)} %pad_maximum_fusion.refs_1_, bf16[16,3584]{1,0:T(8,128)(2,1)S(1)} %collective-permute-done.2.refs_2_, ...), custom_call_target="tpu_custom_call" | custom-call | flops 20000000000 | bytes 50000000 | tf_op jit(solution)/shard_map/pair_fields/pallas_call | solution.py:580
  35.2 2.3 %collective-permute-start.5 = (f32[16,4096]{1,0:T(8,128)S(1)}, f32[16,4096]{1,0:T(8,128)S(1)}, u32[]{:S(2)}, u32[]{:S(2)}) collective-permute-start(f32[16,4096]{1,0:T(8,128)S(1)} %get-tuple-element.11), channel_id=1, source_target_pairs={{0,2},{1,3},{2,16},{3,17},{4,20},{5,21},{6,22},{7,23},{8,9},{9,10}... | collective-permute-start | bytes 786440 | tf_op jit(solution)/shard_map/ppermute | solution.py:610
  37.5 17.2 %pair_fields.3 = (f32[32,3584]{1,0:T(8,128)S(1)}, f32[16,3584]{1,0:T(8,128)S(1)}, f32[16,512]{1,0:T(8,128)S(1)}) custom-call(s32[8]{0:T(128)S(1)} %stack.39.refs_0_, bf16[16,3584]{1,0:T(8,128)(2,1)S(1)} %pad_maximum_fusion.refs_1_, bf16[16,3584]{1,0:T(8,128)(2,1)S(1)} %collective-permute-done.2.refs_2_, bf16[16,3584]{1,0:T(8,128)(2,1)S(1)} %collective-permute-done.3.refs_3_, ...), custom_call_target="tpu_custom_call" | custom-call | flops 20000000000 | bytes 50000000 | tf_op jit(solution)/shard_map/pair_fields/pallas_call | solution.py:580
  54.7 1.7 %collective-permute-start.8 = (f32[16,512]{1,0:T(8,128)S(1)}, f32[16,512]{1,0:T(8,128)S(1)}, u32[]{:S(2)}, u32[]{:S(2)}) collective-permute-start(f32[16,512]{1,0:T(8,128)S(1)} %get-tuple-element.13), channel_id=1, source_target_pairs={{0,10},{1,11},{2,24},{3,25},{4,28},{5,29},{6,30},{7,31},{8,1},{9,2... | collective-permute-start | bytes 98312 | tf_op jit(solution)/shard_map/ppermute | solution.py:610
  56.8 1.8 %collective-permute-start.6 = (f32[16,3584]{1,0:T(8,128)S(1)}, f32[16,3584]{1,0:T(8,128)S(1)}, u32[]{:S(2)}, u32[]{:S(2)}) collective-permute-start(f32[16,3584]{1,0:T(8,128)S(1)} %slice_add_fusion), channel_id=1, source_target_pairs={{0,8},{1,9},{2,10},{3,11},{4,12},{5,13},{6,14},{7,15},{8,0},{9,1},... | collective-permute-start | bytes 688136 | tf_op jit(solution)/shard_map/ppermute | solution.py:610
  58.5 4.1 %collective-permute-done.8 = f32[16,512]{1,0:T(8,128)S(1)} collective-permute-done((f32[16,512]{1,0:T(8,128)S(1)}, f32[16,512]{1,0:T(8,128)S(1)}, u32[]{:S(2)}, u32[]{:S(2)}) %collective-permute-start.8) | collective-permute-done | bytes 32800 | tf_op jit(solution)/shard_map/ppermute | solution.py:610
  62.6 4.0 %collective-permute-done.7 = f32[16,3584]{1,0:T(8,128)S(1)} collective-permute-done((f32[16,3584]{1,0:T(8,128)S(1)}, f32[16,3584]{1,0:T(8,128)S(1)}, u32[]{:S(2)}, u32[]{:S(2)}) %collective-permute-start.7) | collective-permute-done | bytes 229408 | tf_op jit(solution)/shard_map/ppermute | solution.py:610
  66.8 1.3 %collective-permute-done.9 = f32[8,3584]{1,0:T(8,128)S(1)} collective-permute-done((f32[8,3584]{1,0:T(8,128)S(1)}, f32[8,3584]{1,0:T(8,128)S(1)}, u32[]{:S(2)}, u32[]{:S(2)}) %collective-permute-start.9) | collective-permute-done | bytes 114720 | tf_op jit(solution)/shard_map/ppermute | solution.py:610
  68.1 0.9 %collective-permute-start.10 = (f32[8,256]{1,0:T(8,128)S(1)}, f32[8,256]{1,0:T(8,128)S(1)}, u32[]{:S(2)}, u32[]{:S(2)}) collective-permute-start(f32[8,256]{1,0:T(8,128)S(1)} %slice.44), channel_id=1, source_target_pairs={{0,16},{1,17},{2,18},{3,19},{4,20},{5,21},{6,22},{7,23},{8,24},{9,... | collective-permute-start | bytes 24584 | tf_op jit(solution)/shard_map/ppermute | solution.py:610
  69.0 0.9 %reshape.30 = f32[24,128,8]{2,1,0:T(8,128)S(1)} reshape(f32[8,3072]{1,0:T(8,128)S(1)} %slice.45) | data formatting | bytes 196608 | tf_op jit(solution)/shard_map/reshape | solution.py:682
  69.8 0.4 copy.11
  70.3 0.7 reshape.31
  71.0 0.8 %collective-permute-done.10 = f32[8,256]{1,0:T(8,128)S(1)} collective-permute-done((f32[8,256]{1,0:T(8,128)S(1)}, f32[8,256]{1,0:T(8,128)S(1)}, u32[]{:S(2)}, u32[]{:S(2)}) %collective-permute-start.10) | collective-permute-done | bytes 8224 | tf_op jit(solution)/shard_map/ppermute | solution.py:610
  71.9 0.8 %reshape.29 = f32[2,16,4,1,16]{4,3,2,1,0:T(1,128)} reshape(f32[4,8,64]{2,1,0:T(8,128)S(1)} %copy.10) | data formatting | bytes 16384 | tf_op jit(solution)/shard_map/reshape | solution.py:683
  (21 shorter events, 0.8 us)
Async XLA Ops:
  1.5 5.3 %collective-permute-start = (bf16[4,512]{1,0:T(4,128)(2,1)S(1)}, bf16[4,512]{1,0:T(4,128)(2,1)S(1)}, u32[]{:S(2)}, u32[]{:S(2)}) collective-permute-start(bf16[4,512]{1,0:T(4,128)(2,1)S(1)} %reshape.27), channel_id=1, source_target_pairs={{0,16},{1,17},{2,18},{3,19},{4,20},{5,21},{6,22},{7,23},{8,24},{9,... | collective-permute-start | bytes 12296 | tf_op jit(solution)/shard_map/ppermute | solution.py:610
  6.8 1.3 %collective-permute-start.1 = (bf16[8,3584]{1,0:T(8,128)(2,1)S(1)}, bf16[8,3584]{1,0:T(8,128)(2,1)S(1)}, u32[]{:S(2)}, u32[]{:S(2)}) collective-permute-start(bf16[8,3584]{1,0:T(8,128)(2,1)S(1)} %maximum_maximum_fusion), channel_id=1, source_target_pairs={{0,4},{1,5},{2,6},{3,7},{4,0},{5,1},{6,2},{7,3},{8,12},{9,13},{10,... | collective-permute-start | bytes 172040 | tf_op jit(solution)/shard_map/ppermute | solution.py:610
  8.1 9.2 %collective-permute-start.4 = (bf16[16,3584]{1,0:T(8,128)(2,1)S(1)}, bf16[16,3584]{1,0:T(8,128)(2,1)S(1)}, u32[]{:S(2)}, u32[]{:S(2)}) collective-permute-start(bf16[16,3584]{1,0:T(8,128)(2,1)S(1)} %pad_maximum_fusion.refs_1_), channel_id=1, source_target_pairs={{0,27},{1,8},{2,9},{3,10},{4,29},{5,30},{6,31},{7,12},{8,18},{9,19... | collective-permute-start | bytes 344072 | tf_op jit(solution)/shard_map/ppermute | solution.py:610
  13.5 5.7 %collective-permute-start.3 = (bf16[16,3584]{1,0:T(8,128)(2,1)S(1)}, bf16[16,3584]{1,0:T(8,128)(2,1)S(1)}, u32[]{:S(2)}, u32[]{:S(2)}) collective-permute-start(bf16[16,3584]{1,0:T(8,128)(2,1)S(1)} %pad_maximum_fusion.refs_1_), channel_id=1, source_target_pairs={{0,18},{1,19},{2,0},{3,1},{4,20},{5,21},{6,22},{7,23},{8,27},{9,8}... | collective-permute-start | bytes 344072 | tf_op jit(solution)/shard_map/ppermute | solution.py:610
  13.5 5.7 %collective-permute-start.2 = (bf16[16,3584]{1,0:T(8,128)(2,1)S(1)}, bf16[16,3584]{1,0:T(8,128)(2,1)S(1)}, u32[]{:S(2)}, u32[]{:S(2)}) collective-permute-start(bf16[16,3584]{1,0:T(8,128)(2,1)S(1)} %pad_maximum_fusion.refs_1_), channel_id=1, source_target_pairs={{0,8},{1,9},{2,10},{3,11},{4,12},{5,13},{6,14},{7,15},{8,0},{9,1},... | collective-permute-start | bytes 344072 | tf_op jit(solution)/shard_map/ppermute | solution.py:610
  35.2 21.5 %collective-permute-start.5 = (f32[16,4096]{1,0:T(8,128)S(1)}, f32[16,4096]{1,0:T(8,128)S(1)}, u32[]{:S(2)}, u32[]{:S(2)}) collective-permute-start(f32[16,4096]{1,0:T(8,128)S(1)} %get-tuple-element.11), channel_id=1, source_target_pairs={{0,2},{1,3},{2,16},{3,17},{4,20},{5,21},{6,22},{7,23},{8,9},{9,10}... | collective-permute-start | bytes 786440 | tf_op jit(solution)/shard_map/ppermute | solution.py:610
  54.7 8.0 %collective-permute-start.8 = (f32[16,512]{1,0:T(8,128)S(1)}, f32[16,512]{1,0:T(8,128)S(1)}, u32[]{:S(2)}, u32[]{:S(2)}) collective-permute-start(f32[16,512]{1,0:T(8,128)S(1)} %get-tuple-element.13), channel_id=1, source_target_pairs={{0,10},{1,11},{2,24},{3,25},{4,28},{5,29},{6,30},{7,31},{8,1},{9,2... | collective-permute-start | bytes 98312 | tf_op jit(solution)/shard_map/ppermute | solution.py:610
  56.4 10.3 %collective-permute-start.7 = (f32[16,3584]{1,0:T(8,128)S(1)}, f32[16,3584]{1,0:T(8,128)S(1)}, u32[]{:S(2)}, u32[]{:S(2)}) collective-permute-start(f32[16,3584]{1,0:T(8,128)S(1)} %get-tuple-element.12), channel_id=1, source_target_pairs={{0,2},{1,3},{2,16},{3,17},{4,20},{5,21},{6,22},{7,23},{8,9},{9,10}... | collective-permute-start | bytes 688136 | tf_op jit(solution)/shard_map/ppermute | solution.py:610
  56.8 9.9 %collective-permute-start.6 = (f32[16,3584]{1,0:T(8,128)S(1)}, f32[16,3584]{1,0:T(8,128)S(1)}, u32[]{:S(2)}, u32[]{:S(2)}) collective-permute-start(f32[16,3584]{1,0:T(8,128)S(1)} %slice_add_fusion), channel_id=1, source_target_pairs={{0,8},{1,9},{2,10},{3,11},{4,12},{5,13},{6,14},{7,15},{8,0},{9,1},... | collective-permute-start | bytes 688136 | tf_op jit(solution)/shard_map/ppermute | solution.py:610
  66.7 1.4 %collective-permute-start.9 = (f32[8,3584]{1,0:T(8,128)S(1)}, f32[8,3584]{1,0:T(8,128)S(1)}, u32[]{:S(2)}, u32[]{:S(2)}) collective-permute-start(f32[8,3584]{1,0:T(8,128)S(1)} %slice.42), channel_id=1, source_target_pairs={{0,4},{1,5},{2,6},{3,7},{4,0},{5,1},{6,2},{7,3},{8,12},{9,13},{10,... | collective-permute-start | bytes 344072 | tf_op jit(solution)/shard_map/ppermute | solution.py:610
  68.1 3.7 %collective-permute-start.10 = (f32[8,256]{1,0:T(8,128)S(1)}, f32[8,256]{1,0:T(8,128)S(1)}, u32[]{:S(2)}, u32[]{:S(2)}) collective-permute-start(f32[8,256]{1,0:T(8,128)S(1)} %slice.44), channel_id=1, source_target_pairs={{0,16},{1,17},{2,18},{3,19},{4,20},{5,21},{6,22},{7,23},{8,24},{9,... | collective-permute-start | bytes 24584 | tf_op jit(solution)/shard_map/ppermute | solution.py:610

commit v5 on v4

--- a/solution.py
+++ b/solution.py
@@ -176,31 +176,46 @@
                          preferred_element_type=F32)
         return lax.dot_general(picked.astype(jnp.bfloat16), columns.astype(jnp.bfloat16),
                                (((1,), (1,)), ((), ())), preferred_element_type=F32)
-    w_all = (chosen(packet_place(row_l, device_r), table_r, hot_at_r) * keep_lr
-             + (chosen(packet_place(row_r, device_l), table_l, hot_at_l) * keep_rl).T)
-    if call == 1:
-        keep_ll = (blk_l <= blk_ll).astype(F32)
-        w_ll = chosen(packet_place(row_l, device_l), table_l, hot_at_l) * keep_ll
-        w_sym = w_ll + w_ll.T
-        eye = (lax.broadcasted_iota(jnp.int32, (gs, gs), 0) == lax.broadcasted_iota(jnp.int32, (gs, gs), 1))
-        half_row = lax.broadcasted_iota(jnp.int32, (rs, rs), 0)
-        half_col = lax.broadcasted_iota(jnp.int32, (rs, rs), 1)
-        upper, lower = half_row < half_col, half_row > half_col
-        w_diag = jnp.concatenate(
-            [w_sym[:rs, rs:], jnp.where(upper, w_sym[rs:, rs:], jnp.where(lower, w_sym[:rs, :rs], 0.0))], 0)
-        w_all = jnp.where(diag, w_diag, w_all)
-        self_l = jnp.sum(jnp.where(eye, w_ll, 0.0), 0, keepdims=True)
-        self_row = jnp.concatenate([self_l, jnp.zeros((1, LANES - gs), F32)], 1)
-        self_row = jnp.where(diag, self_row, 0.0)
     tile_hot = one_hot(lax.broadcasted_iota(jnp.int32, (gs, 1), 0) // apt, tiles)
     lane_hot = (lax.broadcasted_iota(jnp.int32, (rs, LANES), 1) // apt
                 == lax.broadcasted_iota(jnp.int32, (rs, LANES), 0)).astype(F32)
     lane_match = (lax.broadcasted_iota(jnp.int32, (gs, LANES), 1) % apt
                   == lax.broadcasted_iota(jnp.int32, (gs, LANES), 0) % apt)
-    w_lanes = jnp.where(lane_match, pick(lane_hot.T, w_all.T, ((1,), (0,))).T, 0.0)
-    w_rows = pick(tile_hot.T, w_lanes, ((1,), (0,)))
-    for k in range(tiles):
-        w_ref[k] = w_rows[k:k + 1]
+
+    def set_weights(w_all):
+        w_lanes = jnp.where(lane_match, pick(lane_hot.T, w_all.T, ((1,), (0,))).T, 0.0)
+        w_rows = pick(tile_hot.T, w_lanes, ((1,), (0,)))
+        for k in range(tiles):
+            w_ref[k] = w_rows[k:k + 1]
+
+    def met_weights():
+        set_weights(chosen(packet_place(row_l, device_r), table_r, hot_at_r) * keep_lr
+                    + (chosen(packet_place(row_r, device_l), table_l, hot_at_l) * keep_rl).T)
+
+    if call == 0:
+        met_weights()
+    else:
+        keep_ll = (blk_l <= blk_ll).astype(F32)
+        eye = (lax.broadcasted_iota(jnp.int32, (gs, gs), 0) == lax.broadcasted_iota(jnp.int32, (gs, gs), 1))
+        half_row = lax.broadcasted_iota(jnp.int32, (rs, rs), 0)
+        half_col = lax.broadcasted_iota(jnp.int32, (rs, rs), 1)
+        upper, lower = half_row < half_col, half_row > half_col
+
+        @pl.when(jnp.logical_not(diag))
+        def _():
+            met_weights()
+            w_ref[tiles] = jnp.zeros((1, LANES), F32)
+
+        @pl.when(diag)
+        def _():
+            w_ll = chosen(packet_place(row_l, device_l), table_l, hot_at_l) * keep_ll
+            w_sym = w_ll + w_ll.T
+            set_weights(jnp.concatenate(
+                [w_sym[:rs, rs:],
+                 jnp.where(upper, w_sym[rs:, rs:], jnp.where(lower, w_sym[:rs, :rs], 0.0))], 0))
+            self_l = jnp.sum(jnp.where(eye, w_ll, 0.0), 0, keepdims=True)
+            w_ref[tiles] = jnp.concatenate([self_l, jnp.zeros((1, LANES - gs), F32)], 1)
+
     zeros = jnp.zeros((SUBS, LANES), F32)
     def image_rows(sl):
         a = [ref[:, sl].astype(F32) for ref in a_refs]
@@ -457,43 +472,45 @@
 
     lax.fori_loop(0, tiles, pair_tile, 0)
 
-    def gather_right(low):
+    def gather_right(within):
         def body(blk, _):
             sl = pl.ds(pl.multiple_of(blk * LANES, LANES), LANES)
             for slot in range(LAYERS + CHAN):
                 for b0 in range(0, rs, SUBS):
-                    sums = []
+                    sums = ([], [])
                     for b in range(b0, b0 + SUBS):
-                        if low is None:
-                            t = r_ref[0, slot, b, :, sl] + r_ref[1, slot, b, :, sl]
-                        else:
-                            t = 0.0 if low else r_ref[0, slot, b, :, sl]
-                            for n in range(2):
-                                part = r_ref[1 + n, slot, b, :, sl]
-                                if n * apt <= b < (n + 1) * apt:
-                                    i = sub + n * apt
-                                    t = t + jnp.where(i > b if low else i < b, part, 0.0)
-                                elif (b < n * apt) == bool(low):
-                                    t = t + part
-                        sums.append(t)
-                    at = pl.ds(b0 if low else gs + b0, SUBS)
-                    d_ref[slot, at, sl] = d_ref[slot, at, sl] + fold_rows(sums)
+                        t = [r_ref[0, slot, b, :, sl], 0.0]
+                        if not within:
+                            t[0] = t[0] + r_ref[1, slot, b, :, sl]
+                        for n in range(2 if within else 0):
+                            part = r_ref[1 + n, slot, b, :, sl]
+                            if n * apt <= b < (n + 1) * apt:
+                                i = sub + n * apt
+                                t[0] = t[0] + jnp.where(i < b, part, 0.0)
+                                t[1] = t[1] + jnp.where(i > b, part, 0.0)
+                            else:
+                                low = int(b < n * apt)
+                                t[low] = t[low] + part
+                        sums[0].append(t[0])
+                        sums[1].append(t[1])
+                    for low in range(2 if within else 1):
+                        at = pl.ds(b0 if low else gs + b0, SUBS)
+                        d_ref[slot, at, sl] = d_ref[slot, at, sl] + fold_rows(sums[low])
             return 0
         lax.fori_loop(0, blocks, body, 0, unroll=True)
 
     if call == 0:
-        gather_right(None)
+        gather_right(False)
     else:
         @pl.when(jnp.logical_not(diag))
         def _():
-            gather_right(None)
+            gather_right(False)
 
         @pl.when(diag)
         def _():
-            gather_right(0)
-            gather_right(1)
-
-    selfw = self_row * (0.5 * WEIGHT_VAR / npos) if call == 1 else 0.0
+            gather_right(True)
+
+    selfw = w_ref[tiles] * (0.5 * WEIGHT_VAR / npos) if call == 1 else 0.0
     for l in range(LAYERS):
         dest = phi_ref if l == LAYERS - 1 else sin_ref.at[0]
         scale = (inner if l == 0 else 1.0) / (4.0 * math.pi)
@@ -549,19 +566,26 @@
         gl_ref[:, feat:] = ours
         gr_ref[:, feat:] = jnp.concatenate([theirs[rs:], theirs[:rs]], 1)
     else:
-        across, within = values[:rs], values[rs:]
-        low_part, high_part = jnp.where(lower, within, 0.0), jnp.where(upper, within, 0.0)
-        val_ll = jnp.concatenate([jnp.concatenate([low_part + low_part.T, across], 1),
-                                  jnp.concatenate([across.T, high_part + high_part.T], 1)], 0)
-        val_ll = jnp.where(eye, kself[:, :gs], val_ll) * keep_ll
-        rows = jnp.where(diag, table_place(row_l, device_l),
-                         jnp.concatenate([table_place(row_r, device_l)] * 2, 0))
-        vals = jnp.where(diag, val_ll, jnp.concatenate([values.T * keep_rl, jnp.zeros((rs, gs), F32)], 0))
-        ours = pack_table(spread(rows, vals, hot_at_l))
-        theirs = pack_table(jnp.where(diag, 0.0, spread(table_place(row_l, device_r), values * keep_lr, hot_at_r)))
-        gl_ref[:, feat:] = ours + before_l_ref[:, feat:]
-        gr_ref[:, feat:] = theirs[:rs]
-        rest_ref[...] = theirs[rs:]
+        @pl.when(jnp.logical_not(diag))
+        def _():
+            in_l = spread(table_place(row_r, device_l), values.T * keep_rl, hot_at_l)
+            in_r = spread(table_place(row_l, device_r), values * keep_lr, hot_at_r)
+            theirs = pack_table(in_r)
+            gl_ref[:, feat:] = pack_table(in_l) + before_l_ref[:, feat:]
+            gr_ref[:, feat:] = theirs[:rs]
+            rest_ref[...] = theirs[rs:]
+
+        @pl.when(diag)
+        def _():
+            across, within = values[:rs], values[rs:]
+            low_part, high_part = jnp.where(lower, within, 0.0), jnp.where(upper, within, 0.0)
+            val_ll = jnp.concatenate([jnp.concatenate([low_part + low_part.T, across], 1),
+                                      jnp.concatenate([across.T, high_part + high_part.T], 1)], 0)
+            val_ll = jnp.where(eye, kself[:, :gs], val_ll) * keep_ll
+            ours = spread(table_place(row_l, device_l), val_ll, hot_at_l)
+            gl_ref[:, feat:] = pack_table(ours) + before_l_ref[:, feat:]
+            gr_ref[:, feat:] = jnp.zeros((rs, gr_ref.shape[1] - feat), F32)
+            rest_ref[...] = jnp.zeros(rest_ref.shape, F32)
 
 
 def pair_kernel(call, mode, packets, dims, before=()):
@@ -592,7 +616,7 @@
             pltpu.VMEM((2, LAYERS + 1) + field, F32),
             pltpu.VMEM((terms, 2 * gs, npos), F32),
             pltpu.VMEM((3, terms, rs, SUBS, npos), F32),
-            pltpu.VMEM((tiles, 1, LANES), F32),
+            pltpu.VMEM((tiles + 1, 1, LANES), F32),
             pltpu.VMEM((tiles, 1, LANES), F32),
         ],
         compiler_params=pltpu.CompilerParams(vmem_limit_bytes=40 * 1024 * 1024),

time: 72.9 us -> 73.1 us (level)
  no operation moved by 1% of the time
where the time goes in v5:
time: 73.1 us; the launch traced here: 72.8 us
  Pallas kernels  33.5 us (46%)
  waiting for transfers between devices  16.2 us (22%)
  starting transfers between devices  16.1 us (22%)
  local copies, waits for them, and re-layouts  6.07 us (8%)
    pallas_call x2, Pallas kernels, pair_kernel(): pl.pallas_call(functools.partial(kernel_body, dims, call), out_shape=[jax...  33.5 us
    ppermute x11, waiting for transfers between devices, exchange(): return lax.ppermute(x, ('row', 'col'), perm)  16.2 us
    ppermute x11, starting transfers between devices, exchange(): return lax.ppermute(x, ('row', 'col'), perm)  16.1 us
    reshape x3, local copies, waits for them, and re-layouts, body(): images.reshape(count * CHAN, SUBS, npos // SUBS).transpose(0, 2, 1)  2.25 us
  transfers between devices with their start and end apart: 11, of which 7 were waited for; matrix products, arithmetic and copies ran while one was open for 6% of the time, Pallas kernels for 24%

profile of v5, /device:TPU:0, one launch (start us, length us, event | category | flops | bytes accessed | tf_op | source)
XLA Modules:
  0.0 72.8 jit_solution(5742629289719996680)
XLA Ops:
  0.6 0.9 %reshape.27 = bf16[4,512]{1,0:T(4,128)(2,1)S(1)} reshape(bf16[2,16,4,1,16]{4,2,3,1,0:T(4,128)(2,1)} %param.3) | data formatting | bytes 8192 | tf_op jit(solution)/shard_map/reshape | solution.py:671
  1.5 3.0 %collective-permute-start = (bf16[4,512]{1,0:T(4,128)(2,1)S(1)}, bf16[4,512]{1,0:T(4,128)(2,1)S(1)}, u32[]{:S(2)}, u32[]{:S(2)}) collective-permute-start(bf16[4,512]{1,0:T(4,128)(2,1)S(1)} %reshape.27), channel_id=1, source_target_pairs={{0,16},{1,17},{2,18},{3,19},{4,20},{5,21},{6,22},{7,23},{8,24},{9,... | collective-permute-start | bytes 12296 | tf_op jit(solution)/shard_map/ppermute | solution.py:634
  4.5 0.8 %reshape.25 = bf16[24,8,128]{2,1,0:T(8,128)(2,1)S(1)} reshape(bf16[4,1,2,3072]{3,2,1,0:T(2,128)(2,1)} %param.2) | data formatting | bytes 98304 | tf_op jit(solution)/shard_map/reshape | solution.py:652
  5.4 0.4 copy.9
  5.7 1.0 %reshape.26 = bf16[8,3072]{1,0:T(8,128)(2,1)S(1)} reshape(bf16[24,128,8]{2,1,0:T(8,128)(2,1)S(1)} %bitcast.15) | data formatting | bytes 98304 | tf_op jit(solution)/shard_map/reshape | solution.py:652
  6.9 1.2 %collective-permute-done.1 = bf16[8,3584]{1,0:T(8,128)(2,1)S(1)} collective-permute-done((bf16[8,3584]{1,0:T(8,128)(2,1)S(1)}, bf16[8,3584]{1,0:T(8,128)(2,1)S(1)}, u32[]{:S(2)}, u32[]{:S(2)}) %collective-permute-start.1) | collective-permute-done | bytes 57376 | tf_op jit(solution)/shard_map/ppermute | solution.py:634
  8.1 5.4 %collective-permute-start.4 = (bf16[16,3584]{1,0:T(8,128)(2,1)S(1)}, bf16[16,3584]{1,0:T(8,128)(2,1)S(1)}, u32[]{:S(2)}, u32[]{:S(2)}) collective-permute-start(bf16[16,3584]{1,0:T(8,128)(2,1)S(1)} %pad_maximum_fusion.refs_1_), channel_id=1, source_target_pairs={{0,27},{1,8},{2,9},{3,10},{4,29},{5,30},{6,31},{7,12},{8,18},{9,19... | collective-permute-start | bytes 344072 | tf_op jit(solution)/shard_map/ppermute | solution.py:634
  13.5 0.9 %collective-permute-start.2 = (bf16[16,3584]{1,0:T(8,128)(2,1)S(1)}, bf16[16,3584]{1,0:T(8,128)(2,1)S(1)}, u32[]{:S(2)}, u32[]{:S(2)}) collective-permute-start(bf16[16,3584]{1,0:T(8,128)(2,1)S(1)} %pad_maximum_fusion.refs_1_), channel_id=1, source_target_pairs={{0,8},{1,9},{2,10},{3,11},{4,12},{5,13},{6,14},{7,15},{8,0},{9,1},... | collective-permute-start | bytes 344072 | tf_op jit(solution)/shard_map/ppermute | solution.py:634
  14.4 2.9 %collective-permute-done.4.refs_4_ = bf16[16,3584]{1,0:T(8,128)(2,1)S(1)} collective-permute-done((bf16[16,3584]{1,0:T(8,128)(2,1)S(1)}, bf16[16,3584]{1,0:T(8,128)(2,1)S(1)}, u32[]{:S(2)}, u32[]{:S(2)}) %collective-permute-start.4) | collective-permute-done | bytes 114720 | tf_op jit(solution)/shard_map/ppermute | solution.py:634
  17.3 1.9 %collective-permute-done.3.refs_3_ = bf16[16,3584]{1,0:T(8,128)(2,1)S(1)} collective-permute-done((bf16[16,3584]{1,0:T(8,128)(2,1)S(1)}, bf16[16,3584]{1,0:T(8,128)(2,1)S(1)}, u32[]{:S(2)}, u32[]{:S(2)}) %collective-permute-start.3) | collective-permute-done | bytes 114720 | tf_op jit(solution)/shard_map/ppermute | solution.py:634
  19.2 16.0 %pair_fields.2 = (f32[32,3584]{1,0:T(8,128)S(1)}, f32[16,4096]{1,0:T(8,128)S(1)}, f32[16,3072]{1,0:T(8,128)S(1)}) custom-call(s32[8]{0:T(128)S(1)} %stack.39.refs_0_, bf16[16,3584]{1,0:T(8,128)(2,1)S(1)} %pad_maximum_fusion.refs_1_, bf16[16,3584]{1,0:T(8,128)(2,1)S(1)} %collective-permute-done.2.refs_2_, ...), custom_call_target="tpu_custom_call" | custom-call | flops 20000000000 | bytes 50000000 | tf_op jit(solution)/shard_map/pair_fields/pallas_call | solution.py:604
  35.2 2.1 %collective-permute-start.5 = (f32[16,4096]{1,0:T(8,128)S(1)}, f32[16,4096]{1,0:T(8,128)S(1)}, u32[]{:S(2)}, u32[]{:S(2)}) collective-permute-start(f32[16,4096]{1,0:T(8,128)S(1)} %get-tuple-element.11), channel_id=1, source_target_pairs={{0,2},{1,3},{2,16},{3,17},{4,20},{5,21},{6,22},{7,23},{8,9},{9,10}... | collective-permute-start | bytes 786440 | tf_op jit(solution)/shard_map/ppermute | solution.py:634
  37.3 17.5 %pair_fields.3 = (f32[32,3584]{1,0:T(8,128)S(1)}, f32[16,3584]{1,0:T(8,128)S(1)}, f32[16,512]{1,0:T(8,128)S(1)}) custom-call(s32[8]{0:T(128)S(1)} %stack.39.refs_0_, bf16[16,3584]{1,0:T(8,128)(2,1)S(1)} %pad_maximum_fusion.refs_1_, bf16[16,3584]{1,0:T(8,128)(2,1)S(1)} %collective-permute-done.2.refs_2_, bf16[16,3584]{1,0:T(8,128)(2,1)S(1)} %collective-permute-done.3.refs_3_, ...), custom_call_target="tpu_custom_call" | custom-call | flops 20000000000 | bytes 50000000 | tf_op jit(solution)/shard_map/pair_fields/pallas_call | solution.py:604
  54.8 1.7 %collective-permute-start.8 = (f32[16,512]{1,0:T(8,128)S(1)}, f32[16,512]{1,0:T(8,128)S(1)}, u32[]{:S(2)}, u32[]{:S(2)}) collective-permute-start(f32[16,512]{1,0:T(8,128)S(1)} %get-tuple-element.13), channel_id=1, source_target_pairs={{0,10},{1,11},{2,24},{3,25},{4,28},{5,29},{6,30},{7,31},{8,1},{9,2... | collective-permute-start | bytes 98312 | tf_op jit(solution)/shard_map/ppermute | solution.py:634
  56.9 1.8 %collective-permute-start.6 = (f32[16,3584]{1,0:T(8,128)S(1)}, f32[16,3584]{1,0:T(8,128)S(1)}, u32[]{:S(2)}, u32[]{:S(2)}) collective-permute-start(f32[16,3584]{1,0:T(8,128)S(1)} %slice_add_fusion), channel_id=1, source_target_pairs={{0,8},{1,9},{2,10},{3,11},{4,12},{5,13},{6,14},{7,15},{8,0},{9,1},... | collective-permute-start | bytes 688136 | tf_op jit(solution)/shard_map/ppermute | solution.py:634
  58.6 4.2 %collective-permute-done.8 = f32[16,512]{1,0:T(8,128)S(1)} collective-permute-done((f32[16,512]{1,0:T(8,128)S(1)}, f32[16,512]{1,0:T(8,128)S(1)}, u32[]{:S(2)}, u32[]{:S(2)}) %collective-permute-start.8) | collective-permute-done | bytes 32800 | tf_op jit(solution)/shard_map/ppermute | solution.py:634
  62.8 4.0 %collective-permute-done.7 = f32[16,3584]{1,0:T(8,128)S(1)} collective-permute-done((f32[16,3584]{1,0:T(8,128)S(1)}, f32[16,3584]{1,0:T(8,128)S(1)}, u32[]{:S(2)}, u32[]{:S(2)}) %collective-permute-start.7) | collective-permute-done | bytes 229408 | tf_op jit(solution)/shard_map/ppermute | solution.py:634
  66.9 1.3 %collective-permute-done.9 = f32[8,3584]{1,0:T(8,128)S(1)} collective-permute-done((f32[8,3584]{1,0:T(8,128)S(1)}, f32[8,3584]{1,0:T(8,128)S(1)}, u32[]{:S(2)}, u32[]{:S(2)}) %collective-permute-start.9) | collective-permute-done | bytes 114720 | tf_op jit(solution)/shard_map/ppermute | solution.py:634
  68.2 0.9 %collective-permute-start.10 = (f32[8,256]{1,0:T(8,128)S(1)}, f32[8,256]{1,0:T(8,128)S(1)}, u32[]{:S(2)}, u32[]{:S(2)}) collective-permute-start(f32[8,256]{1,0:T(8,128)S(1)} %slice.44), channel_id=1, source_target_pairs={{0,16},{1,17},{2,18},{3,19},{4,20},{5,21},{6,22},{7,23},{8,24},{9,... | collective-permute-start | bytes 24584 | tf_op jit(solution)/shard_map/ppermute | solution.py:634
  69.1 0.9 %reshape.30 = f32[24,128,8]{2,1,0:T(8,128)S(1)} reshape(f32[8,3072]{1,0:T(8,128)S(1)} %slice.45) | data formatting | bytes 196608 | tf_op jit(solution)/shard_map/reshape | solution.py:706
  70.0 0.4 copy.11
  70.4 0.7 reshape.31
  71.1 0.8 %collective-permute-done.10 = f32[8,256]{1,0:T(8,128)S(1)} collective-permute-done((f32[8,256]{1,0:T(8,128)S(1)}, f32[8,256]{1,0:T(8,128)S(1)}, u32[]{:S(2)}, u32[]{:S(2)}) %collective-permute-start.10) | collective-permute-done | bytes 8224 | tf_op jit(solution)/shard_map/ppermute | solution.py:634
  72.0 0.8 %reshape.29 = f32[2,16,4,1,16]{4,3,2,1,0:T(1,128)} reshape(f32[4,8,64]{2,1,0:T(8,128)S(1)} %copy.10) | data formatting | bytes 16384 | tf_op jit(solution)/shard_map/reshape | solution.py:707
  (21 shorter events, 0.8 us)
Async XLA Ops:
  1.5 5.3 %collective-permute-start = (bf16[4,512]{1,0:T(4,128)(2,1)S(1)}, bf16[4,512]{1,0:T(4,128)(2,1)S(1)}, u32[]{:S(2)}, u32[]{:S(2)}) collective-permute-start(bf16[4,512]{1,0:T(4,128)(2,1)S(1)} %reshape.27), channel_id=1, source_target_pairs={{0,16},{1,17},{2,18},{3,19},{4,20},{5,21},{6,22},{7,23},{8,24},{9,... | collective-permute-start | bytes 12296 | tf_op jit(solution)/shard_map/ppermute | solution.py:634
  6.8 1.3 %collective-permute-start.1 = (bf16[8,3584]{1,0:T(8,128)(2,1)S(1)}, bf16[8,3584]{1,0:T(8,128)(2,1)S(1)}, u32[]{:S(2)}, u32[]{:S(2)}) collective-permute-start(bf16[8,3584]{1,0:T(8,128)(2,1)S(1)} %maximum_maximum_fusion), channel_id=1, source_target_pairs={{0,4},{1,5},{2,6},{3,7},{4,0},{5,1},{6,2},{7,3},{8,12},{9,13},{10,... | collective-permute-start | bytes 172040 | tf_op jit(solution)/shard_map/ppermute | solution.py:634
  8.1 9.2 %collective-permute-start.4 = (bf16[16,3584]{1,0:T(8,128)(2,1)S(1)}, bf16[16,3584]{1,0:T(8,128)(2,1)S(1)}, u32[]{:S(2)}, u32[]{:S(2)}) collective-permute-start(bf16[16,3584]{1,0:T(8,128)(2,1)S(1)} %pad_maximum_fusion.refs_1_), channel_id=1, source_target_pairs={{0,27},{1,8},{2,9},{3,10},{4,29},{5,30},{6,31},{7,12},{8,18},{9,19... | collective-permute-start | bytes 344072 | tf_op jit(solution)/shard_map/ppermute | solution.py:634
  13.5 5.7 %collective-permute-start.3 = (bf16[16,3584]{1,0:T(8,128)(2,1)S(1)}, bf16[16,3584]{1,0:T(8,128)(2,1)S(1)}, u32[]{:S(2)}, u32[]{:S(2)}) collective-permute-start(bf16[16,3584]{1,0:T(8,128)(2,1)S(1)} %pad_maximum_fusion.refs_1_), channel_id=1, source_target_pairs={{0,18},{1,19},{2,0},{3,1},{4,20},{5,21},{6,22},{7,23},{8,27},{9,8}... | collective-permute-start | bytes 344072 | tf_op jit(solution)/shard_map/ppermute | solution.py:634
  13.5 5.7 %collective-permute-start.2 = (bf16[16,3584]{1,0:T(8,128)(2,1)S(1)}, bf16[16,3584]{1,0:T(8,128)(2,1)S(1)}, u32[]{:S(2)}, u32[]{:S(2)}) collective-permute-start(bf16[16,3584]{1,0:T(8,128)(2,1)S(1)} %pad_maximum_fusion.refs_1_), channel_id=1, source_target_pairs={{0,8},{1,9},{2,10},{3,11},{4,12},{5,13},{6,14},{7,15},{8,0},{9,1},... | collective-permute-start | bytes 344072 | tf_op jit(solution)/shard_map/ppermute | solution.py:634
  35.2 21.6 %collective-permute-start.5 = (f32[16,4096]{1,0:T(8,128)S(1)}, f32[16,4096]{1,0:T(8,128)S(1)}, u32[]{:S(2)}, u32[]{:S(2)}) collective-permute-start(f32[16,4096]{1,0:T(8,128)S(1)} %get-tuple-element.11), channel_id=1, source_target_pairs={{0,2},{1,3},{2,16},{3,17},{4,20},{5,21},{6,22},{7,23},{8,9},{9,10}... | collective-permute-start | bytes 786440 | tf_op jit(solution)/shard_map/ppermute | solution.py:634
  54.8 8.0 %collective-permute-start.8 = (f32[16,512]{1,0:T(8,128)S(1)}, f32[16,512]{1,0:T(8,128)S(1)}, u32[]{:S(2)}, u32[]{:S(2)}) collective-permute-start(f32[16,512]{1,0:T(8,128)S(1)} %get-tuple-element.13), channel_id=1, source_target_pairs={{0,10},{1,11},{2,24},{3,25},{4,28},{5,29},{6,30},{7,31},{8,1},{9,2... | collective-permute-start | bytes 98312 | tf_op jit(solution)/shard_map/ppermute | solution.py:634
  56.5 10.3 %collective-permute-start.7 = (f32[16,3584]{1,0:T(8,128)S(1)}, f32[16,3584]{1,0:T(8,128)S(1)}, u32[]{:S(2)}, u32[]{:S(2)}) collective-permute-start(f32[16,3584]{1,0:T(8,128)S(1)} %get-tuple-element.12), channel_id=1, source_target_pairs={{0,2},{1,3},{2,16},{3,17},{4,20},{5,21},{6,22},{7,23},{8,9},{9,10}... | collective-permute-start | bytes 688136 | tf_op jit(solution)/shard_map/ppermute | solution.py:634
  56.9 9.9 %collective-permute-start.6 = (f32[16,3584]{1,0:T(8,128)S(1)}, f32[16,3584]{1,0:T(8,128)S(1)}, u32[]{:S(2)}, u32[]{:S(2)}) collective-permute-start(f32[16,3584]{1,0:T(8,128)S(1)} %slice_add_fusion), channel_id=1, source_target_pairs={{0,8},{1,9},{2,10},{3,11},{4,12},{5,13},{6,14},{7,15},{8,0},{9,1},... | collective-permute-start | bytes 688136 | tf_op jit(solution)/shard_map/ppermute | solution.py:634
  66.8 1.4 %collective-permute-start.9 = (f32[8,3584]{1,0:T(8,128)S(1)}, f32[8,3584]{1,0:T(8,128)S(1)}, u32[]{:S(2)}, u32[]{:S(2)}) collective-permute-start(f32[8,3584]{1,0:T(8,128)S(1)} %slice.42), channel_id=1, source_target_pairs={{0,4},{1,5},{2,6},{3,7},{4,0},{5,1},{6,2},{7,3},{8,12},{9,13},{10,... | collective-permute-start | bytes 344072 | tf_op jit(solution)/shard_map/ppermute | solution.py:634
  68.2 3.7 %collective-permute-start.10 = (f32[8,256]{1,0:T(8,128)S(1)}, f32[8,256]{1,0:T(8,128)S(1)}, u32[]{:S(2)}, u32[]{:S(2)}) collective-permute-start(f32[8,256]{1,0:T(8,128)S(1)} %slice.44), channel_id=1, source_target_pairs={{0,16},{1,17},{2,18},{3,19},{4,20},{5,21},{6,22},{7,23},{8,24},{9,... | collective-permute-start | bytes 24584 | tf_op jit(solution)/shard_map/ppermute | solution.py:634
